TPU v7x, 256 devices: a whole 4x4x8 slice. The times are simulated.
256 devices in a mesh: ctx: 32 (over z, y), tp: 8 (over x, core).
Axes of the slice: x: 4, y: 4, z: 8, core: 2. Of those that a mesh axis runs over, the one named last changes fastest.
Arguments:
- queries: bfloat16 [512, 128, 576], P('ctx', 'tp'), may hold values from -20 to 20
- latent_cache: bfloat16 [1024, 64, 576], P('ctx'), may hold values from -6 to 6
- output_gradient: bfloat16 [512, 128, 512], P('ctx', 'tp'), may hold values from -6 to 6
- selected: int32 [512, 32], P('ctx'), may hold values from 0 to 1023, as said below
- positions: int32 [512], P('ctx'), may hold values from 63488 to 65535, as said below
Outputs:
- attended: bfloat16 [512, 128, 512], P('ctx', 'tp')
- query_grad: bfloat16 [512, 128, 576], P('ctx', 'tp')
- cache_grad: bfloat16 [1024, 64, 576], P('ctx', 'tp')
Inputs may be any that keep to these rules, and one draw needn't show every extreme that they name: `selected`: each row names 32 different blocks; its last entry is the block that holds the row's position, one of the last 32 blocks, and the others lie in the first 992 blocks. The rows of one ctx index name exactly 64 different blocks together, and at most 3 of them lie in the blocks of any one ctx index. The queries of one ctx index hold consecutive positions, in order, inside one block.
All inputs are finite; a program needn't handle non-finite values.
Results may differ from a plain program's by a relative error of at most 0.028.
Values may be sent and summed in bfloat16 or wider, within the bound.
No kernel may reach another device: no remote copies, remote signals or barrier semaphores. Data moves between devices by JAX's collectives and lax.ppermute only.
A program may use at most 128 MiB of HBM per device.

v0:
```python
import jax
import jax.numpy as jnp
from jax import lax
from jax.sharding import PartitionSpec as P

USED = 64


score_scale = 192.0 ** (-0.5)


def slot_table(selected, block_count, owners, slot_limit):
    block_range = jnp.arange(owners * block_count, dtype=jnp.int32)
    wanted = jnp.any(selected.reshape(-1)[:, None] == block_range[None, :], axis=0)
    wanted = wanted.reshape(owners, block_count)
    rank_within = jnp.cumsum(wanted.astype(jnp.int32), axis=1) - 1
    local_ids = jnp.arange(block_count, dtype=jnp.int32)
    slot_range = jnp.arange(slot_limit, dtype=jnp.int32)
    matches = wanted[:, None, :] & (rank_within[:, None, :] == slot_range[None, :, None])
    present = jnp.any(matches, axis=2)
    found_ids = jnp.sum(jnp.where(matches, local_ids[None, None, :], 0), axis=2)
    return jnp.where(present, found_ids, -1)


def owner_sum(received, asked_ids, block_count):
    onehot = (
        asked_ids.reshape(-1)[:, None] == jnp.arange(block_count, dtype=jnp.int32)[None, :]
    ).astype(jnp.float32)
    flat_rows = received.reshape(onehot.shape[0], -1)
    summed = jnp.einsum(
        "sb,sx->bx",
        onehot,
        flat_rows,
        precision=lax.Precision.HIGHEST,
        preferred_element_type=jnp.float32,
    )
    return summed.reshape((block_count,) + received.shape[2:])


def spread_slots(block_grad, used_slot, slot_order, owners, slot_limit):
    back_ids = jnp.maximum(slot_order, 0)
    slot_grad = jnp.where(used_slot[:, None, None], block_grad[back_ids], 0.0)
    return slot_grad.reshape((owners, slot_limit) + block_grad.shape[1:])


def on_device(queries, latent_cache, output_gradient, selected, positions):
    query_count, head_count, entire_width = queries.shape
    block_count, block_size, _ = latent_cache.shape
    value_width = output_gradient.shape[2]
    owners = lax.axis_size("ctx")
    slot_limit = (USED - 2) // (owners - 1) + 1
    row_count = query_count * head_count
    requests = slot_table(selected, block_count, owners, slot_limit)
    asked_ids = lax.all_to_all(requests, "ctx", split_axis=0, concat_axis=0, tiled=True)
    blocks = latent_cache[jnp.maximum(asked_ids, 0)]
    fetched = lax.all_to_all(blocks, "ctx", split_axis=0, concat_axis=0, tiled=True)
    used_slot = (requests >= 0).reshape(-1)
    slot_order = jnp.cumsum(used_slot.astype(jnp.int32)) - 1
    slot_ids = jnp.arange(owners * slot_limit, dtype=jnp.int32)
    compact_range = jnp.arange(USED, dtype=jnp.int32)
    pick_match = used_slot[None, :] & (slot_order[None, :] == compact_range[:, None])
    picked = jnp.sum(jnp.where(pick_match, slot_ids[None, :], 0), axis=1)
    global_ids = picked // slot_limit * block_count + requests.reshape(-1)[picked]
    chosen = jnp.any(selected[:, :, None] == global_ids[None, None, :], axis=1)
    token_pos = global_ids[:, None] * block_size + jnp.arange(block_size, dtype=jnp.int32)[None, :]
    visible = chosen[:, :, None] & (token_pos[None, :, :] <= positions[:, None, None])
    visible = visible.reshape(query_count, 1, USED * block_size)
    key_matrix = fetched.reshape(owners * slot_limit, block_size, entire_width)[picked].reshape(
        USED * block_size, entire_width
    )
    value_matrix = key_matrix[:, :value_width]
    query_rows = queries.reshape(row_count, entire_width)
    grad_rows = output_gradient.reshape(row_count, value_width)
    scores = (
        jnp.einsum("rd,kd->rk", query_rows, key_matrix, preferred_element_type=jnp.float32)
        * score_scale
    )
    scores = jnp.where(visible, scores.reshape(query_count, head_count, -1), -jnp.inf)
    peak_score = jnp.max(scores, axis=2, keepdims=True)
    exponent = jnp.exp(scores - peak_score)
    weights = (exponent / jnp.sum(exponent, axis=2, keepdims=True)).reshape(row_count, -1)
    weight_half = weights.astype(jnp.bfloat16)
    attended = jnp.dot(weight_half, value_matrix, preferred_element_type=jnp.float32)
    grad_weights = jnp.einsum(
        "rl,kl->rk", grad_rows, value_matrix, preferred_element_type=jnp.float32
    )
    row_inner = jnp.sum(weights * grad_weights, axis=1, keepdims=True)
    score_half = (weights * (grad_weights - row_inner)).astype(jnp.bfloat16)
    query_grad = jnp.dot(score_half, key_matrix, preferred_element_type=jnp.float32) * score_scale
    key_grad = (
        jnp.einsum("rk,rd->kd", score_half, query_rows, preferred_element_type=jnp.float32)
        * score_scale
    )
    value_grad = jnp.einsum("rk,rl->kl", weight_half, grad_rows, preferred_element_type=jnp.float32)
    combined = key_grad + jnp.pad(value_grad, ((0, 0), (0, entire_width - value_width)))
    block_grad = combined.reshape(USED, block_size, entire_width)
    slot_grad = spread_slots(block_grad, used_slot, slot_order, owners, slot_limit)
    returned = lax.all_to_all(slot_grad, "ctx", split_axis=0, concat_axis=0, tiled=True)
    summed = owner_sum(returned, asked_ids, block_count)
    cache_grad = lax.psum_scatter(summed, "tp", scatter_dimension=1, tiled=True)
    attended = attended.astype(jnp.bfloat16).reshape(query_count, head_count, value_width)
    query_grad = query_grad.astype(jnp.bfloat16).reshape(query_count, head_count, entire_width)
    return (attended, query_grad, cache_grad.astype(jnp.bfloat16))


def solution(mesh):
    in_specs = (
        P("ctx", "tp", None),
        P("ctx", None, None),
        P("ctx", "tp", None),
        P("ctx", None),
        P("ctx"),
    )
    out_specs = (P("ctx", "tp", None), P("ctx", "tp", None), P("ctx", "tp", None))
    return jax.shard_map(
        on_device, mesh=mesh, in_specs=in_specs, out_specs=out_specs, check_vma=False
    )
```

profile of v0, /device:TPU:8, one launch (start us, length us, event | category | flops | bytes accessed | tf_op | source)
XLA Modules:
  0.0 771.0 jit_solution(16458760233656697623)
XLA Ops:
  7.2 0.9 eq.70
  8.1 0.4 fusion.9
  8.6 0.2 reduce_window_sum.18
  8.7 0.2 fusion.18
  8.9 0.1 select_reduce_fusion
  9.2 20.0 %all_to_all.16 = s32[32,1,3]{2,1,0:T(1,128)S(1)} all-to-all(s32[32,1,3]{2,1,0:T(1,128)S(1)} %copy.40), channel_id=1, replica_groups=mesh['ctx'=32,'tp'=8] {'ctx'}, dimensions={0} | all-to-all | bytes 768 | tf_op jit(solution)/shard_map/all_to_all | solution.py:54
  29.2 0.5 broadcast.255
  29.7 0.7 fusion.26
  30.4 0.1 reshape.274
  30.6 7.0 gather_fusion.1
  37.6 6.1 all-to-all-start.1
  43.7 0.1 copy.43
  43.9 0.1 select_n.83
  44.1 0.1 reduce-window.4
  44.2 0.1 maximum_reduce_fusion
  44.4 0.1 select_reduce_fusion.1
  44.5 0.8 gather_fusion
  45.3 0.2 broadcast_reduce_fusion
  45.6 0.2 compare_reduce_fusion
  45.8 0.2 and.50
  46.0 0.2 and.51
  46.3 0.1 compare_and_fusion
  46.4 0.5 broadcast_in_dim.84
  46.9 1.2 copy.41
  48.1 171.5 %all-to-all-done.1 = bf16[32,3,64,576]{3,2,1,0:T(8,128)(2,1)} async-done(((bf16[32,3,64,576]{3,2,1,0:T(8,128)(2,1)}), bf16[32,3,64,576]{3,2,1,0:T(8,128)(2,1)}, u32[]{:S(2)}, u32[]{:S(2)}) %all-to-all-start.1) | async-done | bytes 7077920 | tf_op jit(solution)/shard_map/all_to_all | solution.py:56
  219.6 6.7 gather_fusion.2
  226.3 4.6 fusion.28
  230.9 0.6 fusion.5
  231.5 0.5 copy-done.6
  232.0 1.3 multiply_reduce_fusion
  233.3 1.3 fusion.14
  234.7 1.0 multiply_convert_fusion
  235.7 5.2 pad_add_fusion
  240.9 10.8 %copy.44 = f32[4096,576]{1,0:T(8,128)} copy(f32[4096,576]{0,1:T(8,128)} %pad_add_fusion) | data formatting | bytes 18874368 | tf_op jit(solution)/shard_map/add | solution.py:95
  251.7 14.4 %gather_fusion.3 = f32[96,64,576]{2,1,0:T(8,128)} fusion(f32[64,64,576]{2,1,0:T(8,128)} %bitcast.37, s32[1024]{0:T(1024)S(1)} %pad_clamp_fusion), kind=kCustom, calls=%fused_computation.3 | custom fusion | bytes 28311936 | tf_op jit(solution)/shard_map/gather | solution.py:42
  266.1 11.4 %broadcast_select_fusion = f32[32,3,64,576]{3,2,1,0:T(8,128)} fusion(f32[32,3,64,576]{3,2,1,0:T(8,128)} %bitcast.38, pred[32,3]{1,0:T(8,128)(4,1)S(1)} %copy.43), kind=kLoop, calls=%fused_computation.7 | loop fusion | flops 3538944 | bytes 28311648 | tf_op jit(solution)/shard_map/jit(_where)/select_n | solution.py:42
  277.5 8.6 %all-to-all-start.2 = ((f32[32,3,64,576]{3,2,1,0:T(8,128)}), f32[32,3,64,576]{3,2,1,0:T(8,128)}, u32[]{:S(2)}, u32[]{:S(2)}) async-start(f32[32,3,64,576]{3,2,1,0:T(8,128)} %broadcast_select_fusion), calls=%async_computation.2 | async-start | bytes 31457280 | tf_op jit(solution)/shard_map/all_to_all | solution.py:98
  286.2 0.1 eq.82
  286.3 355.5 %all-to-all-done.2 = f32[32,3,64,576]{3,2,1,0:T(8,128)} async-done(((f32[32,3,64,576]{3,2,1,0:T(8,128)}), f32[32,3,64,576]{3,2,1,0:T(8,128)}, u32[]{:S(2)}, u32[]{:S(2)}) %all-to-all-start.2) | async-done | bytes 14155808 | tf_op jit(solution)/shard_map/all_to_all | solution.py:98
  641.8 17.5 %reshape.262 = f32[96,36864]{1,0:T(8,128)} reshape(f32[32,3,64,576]{3,2,1,0:T(8,128)} %all-to-all-done.2) | data formatting | bytes 28311552 | tf_op jit(solution)/shard_map/reshape | solution.py:29
  659.3 17.5 %dot_general.35 = f32[64,576,96]{1,0,2:T(8,128)} reshape(f32[36864,96]{0,1:T(8,128)} %bitcast.39) | data formatting | bytes 28311552 | tf_op jit(solution)/shard_map/sb,sx->bx/dot_general | solution.py:30
  676.8 20.7 %fusion = f32[32,64,576]{2,0,1:T(8,128)} fusion(f32[64,576,96]{1,0,2:T(8,128)} %dot_general.35, s32[96]{0:T(128)S(1)} %eq.82), kind=kOutput, calls=%fused_computation.4 | convolution fusion | flops 1358957568 | bytes 18874752 | tf_op jit(solution)/shard_map/sb,sx->bx/dot_general | solution.py:30
  697.5 4.6 fusion.10
  702.1 0.9 copy.42
  703.0 5.6 fusion.11
  708.6 53.6 %reduce-scatter.2.cloned.1.call-done = f32[32,8,576]{2,0,1:T(8,128)} async-done(((f32[32,64,576]{2,0,1:T(8,128)}), f32[32,8,576]{2,0,1:T(8,128)}) %reduce-scatter.2.cloned.1.call-update) | async-done | bytes 589840 | tf_op jit(solution)/shard_map/reduce_scatter | solution.py:100
  762.1 1.1 convert_element_type.45
  763.3 0.8 copy.46
  (38 shorter events, 0.8 us)
Async XLA Ops:
  7.2 23.4 %copy-start = (bf16[32,64,576]{2,1,0:T(8,128)(2,1)S(1)}, bf16[32,64,576]{2,1,0:T(8,128)(2,1)}, u32[]{:S(2)}) copy-start(bf16[32,64,576]{2,1,0:T(8,128)(2,1)} %param.6) | copy-start | bytes 7077892
  37.6 8.1 %copy-start.4 = (s32[16,32]{1,0:T(8,128)S(1)}, s32[16,32]{1,0:T(8,128)}, u32[]{:S(2)}) copy-start(s32[16,32]{1,0:T(8,128)} %param.8) | copy-start | bytes 6148
  37.6 8.7 %copy-start.5 = (s32[16]{0:T(128)S(1)}, s32[16]{0:T(128)}, u32[]{:S(2)}) copy-start(s32[16]{0:T(128)} %param.9) | copy-start | bytes 196
  37.6 182.0 %all-to-all-start.1 = ((bf16[32,3,64,576]{3,2,1,0:T(8,128)(2,1)}), bf16[32,3,64,576]{3,2,1,0:T(8,128)(2,1)}, u32[]{:S(2)}, u32[]{:S(2)}) async-start(bf16[32,3,64,576]{3,2,1,0:T(8,128)(2,1)} %bitcast.40), calls=%async_computation.1 | async-start | bytes 15728640 | tf_op jit(solution)/shard_map/all_to_all | solution.py:56
  219.6 6.7 copy-start.3
  226.3 5.2 slice-start
  226.3 5.2 slice-start.1
  230.9 3.8 copy-start.2
  230.9 1.1 copy-start.6
  277.5 364.3 %all-to-all-start.2 = ((f32[32,3,64,576]{3,2,1,0:T(8,128)}), f32[32,3,64,576]{3,2,1,0:T(8,128)}, u32[]{:S(2)}, u32[]{:S(2)}) async-start(f32[32,3,64,576]{3,2,1,0:T(8,128)} %broadcast_select_fusion), calls=%async_computation.2 | async-start | bytes 31457280 | tf_op jit(solution)/shard_map/all_to_all | solution.py:98
  286.1 476.0 %reduce-scatter.2.cloned.1.call-start = ((), (), s32[]{:S(2)}) async-start(), calls=%async_computation.4 | async-start | bytes 5898240 | tf_op jit(solution)/shard_map/reduce_scatter | solution.py:100
  703.0 61.1 %copy-start.1 = (bf16[32,64,576]{2,1,0:T(8,128)(2,1)S(1)}, bf16[32,64,576]{2,1,0:T(8,128)(2,1)}, u32[]{:S(2)}) copy-start(bf16[32,64,576]{2,1,0:T(8,128)(2,1)} %param.6) | copy-start | bytes 7077892
Sparse Core Ops, SparseCore 0:
  697.6 64.4 reduce-scatter.1
where the time goes:
time: 772 us; the launch traced here: 771 us
  waiting for transfers between devices  581 us (75%)
  local copies, waits for them, and re-layouts  81.7 us (11%)
  matrix products  43.3 us (6%)
  blocking collectives  20 us (3%)
  other arithmetic  16.5 us (2%)
  starting transfers between devices  14.7 us (2%)
  between operations  14.3 us (2%)
    all_to_all x1, waiting for transfers between devices, on_device(): lax.all_to_all(slot_grad, 'ctx', split_axis=0, concat_axis=0, tiled=True)  356 us
    all_to_all x1, waiting for transfers between devices, on_device(): lax.all_to_all(blocks, 'ctx', split_axis=0, concat_axis=0, tiled=True)  171 us
    reduce_scatter x1, waiting for transfers between devices, on_device(): cache_grad = lax.psum_scatter(summed, 'tp', scatter_dimension=1, tiled=True)  53.6 us
    dot_general x1, matrix products, owner_sum(): jnp.einsum('sb,sx->bx', onehot, flat_rows, precision=lax.Precision.HIGHES...  20.7 us
    all_to_all x1, blocking collectives, on_device(): lax.all_to_all(requests, 'ctx', split_axis=0, concat_axis=0, tiled=True)  20 us
    dot_general x1, local copies, waits for them, and re-layouts, owner_sum(): jnp.einsum('sb,sx->bx', onehot, flat_rows, precision=lax.Precision.HIGHES...  17.5 us
    reshape x1, local copies, waits for them, and re-layouts, owner_sum(): flat_rows = received.reshape(onehot.shape[0], -1)  17.5 us
  transfers between devices with their start and end apart: 3, of which 3 were waited for; matrix products, arithmetic and copies ran while one was open for 2% of the time, Pallas kernels for 0%

commit v1 on v0

v1 whole, which is shorter than its diff:
```python
import functools
import math

import jax
import jax.numpy as jnp
from jax import lax
from jax.experimental import pallas as pl
from jax.experimental.pallas import tpu as pltpu
from jax.sharding import PartitionSpec as P

USED = 64
XN = 4
CORES = 2

score_scale = 192.0 ** (-0.5)
log2e = 1.0 / math.log(2.0)
VMEM_LIMIT = 48 * 1024 * 1024
bf16 = jnp.bfloat16
f32 = jnp.float32


def x_shift(k):
    return [
        (x * CORES + c, ((x + k) % XN) * CORES + c) for x in range(XN) for c in range(CORES)
    ]


CORE_SWAP = [(t, t ^ 1) for t in range(XN * CORES)]


def send_x(value, k):
    return lax.ppermute(value, "tp", x_shift(k % XN))


def nt_dot(a, b):
    return lax.dot_general(a, b, (((1,), (1,)), ((), ())), preferred_element_type=f32)


def score_kernel(bias_ref, own_ref, other_ref, *refs):
    q_refs, g_refs = refs[:XN], refs[XN : 2 * XN]
    p_ref, gw_ref, stat_ref = refs[2 * XN :]
    half, width = own_ref.shape
    value_width = g_refs[0].shape[1]
    step = pl.program_id(0)
    for k in range(XN):

        @pl.when(step == k)
        def _(k=k):
            q, g = q_refs[k][...], g_refs[k][...]
            scores = []
            for h, key_ref in enumerate((own_ref, other_ref)):
                s = nt_dot(key_ref[...], q) * (score_scale * log2e)
                scores.append(s + bias_ref[h * half : (h + 1) * half, :].astype(f32))
            peak = jnp.maximum(
                jnp.max(scores[0], axis=0, keepdims=True), jnp.max(scores[1], axis=0, keepdims=True)
            )
            total = jnp.zeros_like(peak)
            inner = jnp.zeros_like(peak)
            for h, key_ref in enumerate((own_ref, other_ref)):
                p = jnp.exp2(scores[h] - peak)
                gw = nt_dot(key_ref[:, :value_width], g)
                total += jnp.sum(p, axis=0, keepdims=True)
                inner += jnp.sum(p * gw, axis=0, keepdims=True)
                p_ref[0, h * half : (h + 1) * half, :] = p.astype(bf16)
                gw_ref[0, h * half : (h + 1) * half, :] = gw
            stat_ref[0, 0:1, :] = peak
            stat_ref[0, 1:2, :] = total
            stat_ref[0, 2:3, :] = inner
            stat_ref[0, 3:8, :] = jnp.zeros((5, peak.shape[1]), f32)


def key_grad_kernel(p_ref, gw_ref, *refs):
    stat_refs, q_refs, g_refs = refs[:XN], refs[XN : 2 * XN], refs[2 * XN : 3 * XN]
    w_ref, ds_ref, own_ref, other_ref, acc_ref = refs[3 * XN :]
    half = own_ref.shape[0]
    value_width = g_refs[0].shape[1]
    step = pl.program_id(0)
    for k in range(XN):

        @pl.when(step == k)
        def _(k=k):
            stats = [stat_refs[j][(k - j) % XN] for j in range(XN)]
            peak = functools.reduce(jnp.maximum, [s[0:1] for s in stats])
            factors = [jnp.exp2(s[0:1] - peak) for s in stats]
            total = sum(s[1:2] * f for s, f in zip(stats, factors))
            inner = sum(s[2:3] * f for s, f in zip(stats, factors)) / total
            factor = factors[0] / total
            weights = p_ref[0].astype(f32) * factor
            ds = (weights * (gw_ref[0] - inner) * score_scale).astype(bf16)
            w = weights.astype(bf16)
            w_ref[0] = w
            ds_ref[0] = ds
            grad = jnp.dot(ds, q_refs[k][...], preferred_element_type=f32)
            value_grad = jnp.dot(w, g_refs[k][...], preferred_element_type=f32)
            if k == 0:
                acc_ref[...] = grad
            else:
                acc_ref[...] += grad
            acc_ref[:, :value_width] += value_grad

    @pl.when(step == XN - 1)
    def _():
        own_ref[...] = acc_ref[:half, :]
        other_ref[...] = acc_ref[half:, :].astype(bf16)


def query_grad_kernel(own_ref, other_ref, w_ref, ds_ref, *refs):
    out_refs, keys_t = refs[:XN], refs[XN]
    half, width = own_ref.shape
    value_width = out_refs[0].shape[0] - width
    step = pl.program_id(0)

    @pl.when(step == 0)
    def _():
        keys_t[:, :half] = own_ref[...].T
        keys_t[:, half:] = other_ref[...].T

    for k in range(XN):

        @pl.when(step == k)
        def _(k=k):
            att = jnp.dot(keys_t[:value_width, :], w_ref[0], preferred_element_type=f32)
            qg = jnp.dot(keys_t[...], ds_ref[0], preferred_element_type=f32)
            out_refs[k][:value_width, :] = att.astype(bf16)
            out_refs[k][value_width:, :] = qg.astype(bf16)


def combine_kernel(*refs):
    parts, att_ref, qg_ref = refs[:XN], refs[XN], refs[XN + 1]
    value_width = att_ref.shape[1]
    total = sum(part[...].astype(f32) for part in parts)
    att_ref[...] = total[:value_width].astype(bf16).T
    qg_ref[...] = total[value_width:].astype(bf16).T


def whole(shape):
    return pl.BlockSpec(shape, lambda i: (0,) * len(shape))


def params():
    return pltpu.CompilerParams(vmem_limit_bytes=VMEM_LIMIT)


def slot_table(selected, block_count, owners, slot_limit):
    block_range = jnp.arange(owners * block_count, dtype=jnp.int32)
    wanted = jnp.any(selected.reshape(-1)[:, None] == block_range[None, :], axis=0)
    wanted = wanted.reshape(owners, block_count)
    rank_within = jnp.cumsum(wanted.astype(jnp.int32), axis=1) - 1
    local_ids = jnp.arange(block_count, dtype=jnp.int32)
    slot_range = jnp.arange(slot_limit, dtype=jnp.int32)
    matches = wanted[:, None, :] & (rank_within[:, None, :] == slot_range[None, :, None])
    present = jnp.any(matches, axis=2)
    found_ids = jnp.sum(jnp.where(matches, local_ids[None, None, :], 0), axis=2)
    return jnp.where(present, found_ids, -1)


def row_targets(ids, tokens):
    token = jnp.arange(tokens, dtype=jnp.int32)
    rows = jnp.where(ids[:, None] >= 0, ids[:, None] * tokens + token[None, :], -1)
    return rows.reshape(-1)


def on_device(queries, latent_cache, output_gradient, selected, positions):
    query_count, head_count, width = queries.shape
    block_count, block_size, _ = latent_cache.shape
    value_width = output_gradient.shape[2]
    owners = lax.axis_size("ctx")
    tp = lax.axis_index("tp")
    tokens = block_size // (XN * CORES)
    slot_limit = (USED - 2) // (owners - 1) + 1
    slots = owners * slot_limit
    rows = query_count * head_count
    half = USED * tokens
    keys = CORES * half

    requests = slot_table(selected, block_count, owners, slot_limit)
    asked_ids = lax.all_to_all(requests, "ctx", split_axis=0, concat_axis=0, tiled=True)

    query_rows = queries.reshape(rows, width)
    grad_rows = output_gradient.reshape(rows, value_width)
    q_parts = [query_rows] + [send_x(query_rows, k) for k in range(1, XN)]
    g_parts = [grad_rows] + [send_x(grad_rows, k) for k in range(1, XN)]

    my_tokens = lax.dynamic_slice_in_dim(latent_cache, tp * tokens, tokens, axis=1)
    my_tokens = my_tokens.reshape(block_count * tokens, width)
    asked_rows = row_targets(asked_ids.reshape(-1), tokens)
    asked_hot = (
        asked_rows[:, None] == jnp.arange(block_count * tokens, dtype=jnp.int32)[None, :]
    ).astype(bf16)
    packed = jnp.dot(asked_hot, my_tokens, preferred_element_type=f32).astype(bf16)
    fetched = lax.all_to_all(
        packed.reshape(owners, slot_limit * tokens, width), "ctx", 0, 0, tiled=True
    ).reshape(slots * tokens, width)

    flat_requests = requests.reshape(-1)
    used_slot = flat_requests >= 0
    slot_order = jnp.where(used_slot, jnp.cumsum(used_slot.astype(jnp.int32)) - 1, -1)
    compact = jnp.arange(USED, dtype=jnp.int32)
    slot_match = slot_order[None, :] == compact[:, None]
    slot_owner = jnp.arange(slots, dtype=jnp.int32) // slot_limit
    slot_block = slot_owner * block_count + flat_requests
    block_ids = jnp.sum(jnp.where(slot_match, slot_block[None, :], 0), axis=1)
    slot_rows = row_targets(slot_order, tokens)
    spread_hot = (slot_rows[:, None] == jnp.arange(half, dtype=jnp.int32)[None, :]).astype(bf16)

    chosen = jnp.any(selected[None, :, :] == block_ids[:, None, None], axis=2)
    token = jnp.arange(tokens, dtype=jnp.int32)
    token_pos = jnp.stack(
        [block_ids[:, None] * block_size + t * tokens + token[None, :] for t in (tp, tp ^ 1)]
    )
    visible = chosen[None, :, None, :] & (
        token_pos[:, :, :, None] <= positions[None, None, None, :]
    )
    bias = jnp.where(visible, 0.0, -jnp.inf).astype(bf16).reshape(keys, query_count)
    bias = jnp.broadcast_to(bias[:, :, None], (keys, query_count, head_count)).reshape(keys, rows)

    own_keys = lax.dot_general(
        spread_hot, fetched, (((0,), (0,)), ((), ())), preferred_element_type=f32
    ).astype(bf16)
    other_keys = lax.ppermute(own_keys, "tp", CORE_SWAP)

    blocked = pl.BlockSpec((1, keys, rows), lambda i: (i, 0, 0))
    p, gw, stats = pl.pallas_call(
        score_kernel,
        grid=(XN,),
        in_specs=[whole((keys, rows))]
        + [whole((half, width))] * 2
        + [whole((rows, width))] * XN
        + [whole((rows, value_width))] * XN,
        out_specs=[blocked, blocked, pl.BlockSpec((1, 8, rows), lambda i: (i, 0, 0))],
        out_shape=[
            jax.ShapeDtypeStruct((XN, keys, rows), bf16),
            jax.ShapeDtypeStruct((XN, keys, rows), f32),
            jax.ShapeDtypeStruct((XN, 8, rows), f32),
        ],
        compiler_params=params(),
        name="scores",
    )(bias, own_keys, other_keys, *q_parts, *g_parts)
    all_stats = [stats] + [send_x(stats, k) for k in range(1, XN)]

    w, ds, own_grad, other_grad = pl.pallas_call(
        key_grad_kernel,
        grid=(XN,),
        in_specs=[blocked, blocked]
        + [whole((XN, 8, rows))] * XN
        + [whole((rows, width))] * XN
        + [whole((rows, value_width))] * XN,
        out_specs=[blocked, blocked, whole((half, width)), whole((half, width))],
        out_shape=[
            jax.ShapeDtypeStruct((XN, keys, rows), bf16),
            jax.ShapeDtypeStruct((XN, keys, rows), bf16),
            jax.ShapeDtypeStruct((half, width), f32),
            jax.ShapeDtypeStruct((half, width), bf16),
        ],
        scratch_shapes=[pltpu.VMEM((keys, width), f32)],
        compiler_params=params(),
        name="key_grad",
    )(p, gw, *all_stats, *q_parts, *g_parts)
    from_core = lax.ppermute(other_grad, "tp", CORE_SWAP)

    parts = pl.pallas_call(
        query_grad_kernel,
        grid=(XN,),
        in_specs=[whole((half, width))] * 2 + [blocked, blocked],
        out_specs=[whole((width + value_width, rows))] * XN,
        out_shape=[jax.ShapeDtypeStruct((width + value_width, rows), bf16)] * XN,
        scratch_shapes=[pltpu.VMEM((width, keys), bf16)],
        compiler_params=params(),
        name="query_grad",
    )(own_keys, other_keys, w, ds)
    parts = [parts[0]] + [send_x(parts[k], -k) for k in range(1, XN)]

    block_grad = (own_grad + from_core.astype(f32)).astype(bf16)
    spread = jnp.dot(spread_hot, block_grad, preferred_element_type=f32).astype(bf16)
    returned = lax.all_to_all(
        spread.reshape(owners, slot_limit * tokens, width), "ctx", 0, 0, tiled=True
    ).reshape(slots * tokens, width)
    cache_grad = lax.dot_general(
        asked_hot, returned, (((0,), (0,)), ((), ())), preferred_element_type=f32
    ).astype(bf16)

    attended, query_grad = pl.pallas_call(
        combine_kernel,
        out_shape=[
            jax.ShapeDtypeStruct((rows, value_width), bf16),
            jax.ShapeDtypeStruct((rows, width), bf16),
        ],
        compiler_params=params(),
        name="combine",
    )(*parts)
    return (
        attended.reshape(query_count, head_count, value_width),
        query_grad.reshape(query_count, head_count, width),
        cache_grad.reshape(block_count, tokens, width),
    )


def solution(mesh):
    in_specs = (
        P("ctx", "tp", None),
        P("ctx", None, None),
        P("ctx", "tp", None),
        P("ctx", None),
        P("ctx"),
    )
    out_specs = (P("ctx", "tp", None), P("ctx", "tp", None), P("ctx", "tp", None))
    return jax.shard_map(
        on_device, mesh=mesh, in_specs=in_specs, out_specs=out_specs, check_vma=False
    )
```

time: 772 us -> 168 us (0.22)
  waiting for transfers between devices: 581 us -> 66.9 us
  local copies, waits for them, and re-layouts: 81.7 us -> 26.8 us
  matrix products: 43.3 us -> 9.49 us
  starting transfers between devices: 14.7 us -> 40.1 us
  Pallas kernels: 0 us -> 20.1 us
  blocking collectives: 20 us -> 0 us
  other arithmetic: 16.5 us -> 1.8 us
  between operations: 14.3 us -> 0.91 us
    all_to_all x2 -> x3, waiting for transfers between devices: 527 us -> 26.4 us  [the longest x1 17.9 us: on_device(): lax.all_to_all(packed.reshape(owners, slot_limit * tokens, width), 'ctx',...]
    reduce_scatter x1 -> x0, waiting for transfers between devices: 53.6 us -> none  [on_device(): cache_grad = lax.psum_scatter(summed, 'tp', scatter_dimension=1, tiled=True)]
    ppermute x0 -> x14, waiting for transfers between devices: none -> 40.6 us  [the longest x12 38.2 us: send_x(): return lax.ppermute(value, 'tp', x_shift(k % XN))]
    dot_general x7 -> x4, matrix products: 43.3 us -> 9.49 us  [the longest x1 3.27 us: on_device(): jnp.dot(spread_hot, block_grad, preferred_element_type=f32).astype(bf16)]
    gather x4 -> x0, local copies, waits for them, and re-layouts: 28.9 us -> none  [the longest x1 14.4 us: spread_slots(): slot_grad = jnp.where(used_slot[:, None, None], block_grad[back_ids], 0.0)]
    pallas_call x0 -> x4, Pallas kernels: none -> 20.1 us  [the longest x1 7.96 us: on_device(): pl.pallas_call(key_grad_kernel, grid=(XN,), in_specs=[blocked, blocked] +...]
    all_to_all x1 -> x0, blocking collectives: 20 us -> none  [on_device(): lax.all_to_all(requests, 'ctx', split_axis=0, concat_axis=0, tiled=True)]
    dot_general x1 -> x0, local copies, waits for them, and re-layouts: 17.5 us -> none  [owner_sum(): jnp.einsum('sb,sx->bx', onehot, flat_rows, precision=lax.Precision.HIGHES...]
  transfers between devices with their start and end apart: 3 -> 17, of which waited for: 3 -> 10; matrix products, arithmetic and copies ran while one was open for 2% -> 7% of each run, Pallas kernels for 0% -> 3%
where the time goes in v1:
time: 168 us; the launch traced here: 166 us
  waiting for transfers between devices  66.9 us (40%)
  starting transfers between devices  40.1 us (24%)
  local copies, waits for them, and re-layouts  26.8 us (16%)
  Pallas kernels  20.1 us (12%)
  matrix products  9.49 us (6%)
  other arithmetic  1.8 us (1%)
    ppermute x12, waiting for transfers between devices, send_x(): return lax.ppermute(value, 'tp', x_shift(k % XN))  38.2 us
    all_to_all x1, waiting for transfers between devices, on_device(): lax.all_to_all(packed.reshape(owners, slot_limit * tokens, width), 'ctx',...  17.9 us
    ppermute x12, starting transfers between devices, send_x(): return lax.ppermute(value, 'tp', x_shift(k % XN))  17.1 us
    all_to_all x1, starting transfers between devices, on_device(): lax.all_to_all(requests, 'ctx', split_axis=0, concat_axis=0, tiled=True)  11.7 us
    all_to_all x1, waiting for transfers between devices, on_device(): lax.all_to_all(requests, 'ctx', split_axis=0, concat_axis=0, tiled=True)  8.44 us
    pallas_call x1, Pallas kernels, on_device(): pl.pallas_call(key_grad_kernel, grid=(XN,), in_specs=[blocked, blocked] +...  7.96 us
    unnamed x26, local copies, waits for them, and re-layouts  7.75 us
    pallas_call x1, Pallas kernels, on_device(): pl.pallas_call(score_kernel, grid=(XN,), in_specs=[whole((keys, rows))] +...  6.61 us
  transfers between devices with their start and end apart: 17, of which 10 were waited for; matrix products, arithmetic and copies ran while one was open for 7% of the time, Pallas kernels for 3%

profile of v1, /device:TPU:8, one launch (start us, length us, event | category | flops | bytes accessed | tf_op | source)
XLA Modules:
  0.0 166.1 jit_solution(18438751933318492721)
XLA Ops:
  0.6 0.9 eq.38
  2.5 0.7 copy.72
  3.2 11.7 %all-to-all-start = ((s32[32,1,3]{2,1,0:T(1,128)}), s32[32,1,3]{2,1,0:T(1,128)S(1)}, u32[]{:S(2)}, u32[]{:S(2)}) async-start(s32[32,1,3]{2,1,0:T(1,128)} %copy.72), calls=%async_computation | async-start | bytes 32768 | tf_op jit(solution)/shard_map/all_to_all | solution.py:177
  14.9 8.4 %all-to-all-done = s32[32,1,3]{2,1,0:T(1,128)S(1)} async-done(((s32[32,1,3]{2,1,0:T(1,128)}), s32[32,1,3]{2,1,0:T(1,128)S(1)}, u32[]{:S(2)}, u32[]{:S(2)}) %all-to-all-start) | async-done | bytes 416 | tf_op jit(solution)/shard_map/all_to_all | solution.py:177
  23.9 1.5 convolution_convert_fusion
  25.4 2.3 %copy.73 = bf16[768,576]{1,0:T(8,128)(2,1)} copy(bf16[768,576]{0,1:T(8,128)(2,1)} %convolution_convert_fusion) | data formatting | bytes 1769472 | tf_op jit(solution)/shard_map/convert_element_type | solution.py:190
  27.7 5.7 %all-to-all-start.1 = ((bf16[32,24,576]{2,1,0:T(8,128)(2,1)}), bf16[32,24,576]{2,1,0:T(8,128)(2,1)}, u32[]{:S(2)}, u32[]{:S(2)}) async-start(bf16[32,24,576]{2,1,0:T(8,128)(2,1)} %bitcast.22), calls=%async_computation.1 | async-start | bytes 1966080 | tf_op jit(solution)/shard_map/all_to_all | solution.py:191
  33.4 2.8 %collective-permute-start.6 = (bf16[256,512]{1,0:T(8,128)(2,1)S(1)}, bf16[256,512]{1,0:T(8,128)(2,1)S(1)}, u32[]{:S(2)}, u32[]{:S(2)}) collective-permute-start(bf16[256,512]{1,0:T(8,128)(2,1)S(1)} %bitcast.17), channel_id=1, source_target_pairs={{0,6},{1,7},{2,0},{3,1},{4,2},{5,3},{6,4},{7,5},{8,14},{9,15},{10,... | collective-permute-start | bytes 786440 | tf_op jit(solution)/shard_map/ppermute | solution.py:32
  36.2 0.8 collective-permute-start.5
  37.0 0.9 collective-permute-start.4
  37.9 2.4 %collective-permute-start.3 = (bf16[256,576]{1,0:T(8,128)(2,1)}, bf16[256,576]{1,0:T(8,128)(2,1)}, u32[]{:S(2)}, u32[]{:S(2)}) collective-permute-start(bf16[256,576]{1,0:T(8,128)(2,1)} %bitcast.6.refs_0_.refs_4_), channel_id=1, source_target_pairs={{0,6},{1,7},{2,0},{3,1},{4,2},{5,3},{6,4},{7,5},{8,14},{9,15},{10,... | collective-permute-start | bytes 884744 | tf_op jit(solution)/shard_map/ppermute | solution.py:32
  41.1 17.9 %all-to-all-done.1 = bf16[32,24,576]{2,1,0:T(8,128)(2,1)} async-done(((bf16[32,24,576]{2,1,0:T(8,128)(2,1)}), bf16[32,24,576]{2,1,0:T(8,128)(2,1)}, u32[]{:S(2)}, u32[]{:S(2)}) %all-to-all-start.1) | async-done | bytes 884768 | tf_op jit(solution)/shard_map/all_to_all | solution.py:191
  59.0 2.9 %fusion.4 = bf16[512,576]{0,1:T(8,128)(2,1)} fusion(bf16[768,576]{1,0:T(8,128)(2,1)} %bitcast.3, s32[768]{0:T(1024)S(1)} %select_n.108), kind=kOutput, calls=%fused_computation.7 | convolution fusion | flops 453672960 | bytes 1477632 | tf_op jit(solution)/shard_map/dot_general | solution.py:217
  62.2 3.1 %collective-permute-start.2 = (bf16[256,576]{1,0:T(8,128)(2,1)}, bf16[256,576]{1,0:T(8,128)(2,1)}, u32[]{:S(2)}, u32[]{:S(2)}) collective-permute-start(bf16[256,576]{1,0:T(8,128)(2,1)} %bitcast.6.refs_0_.refs_4_), channel_id=1, source_target_pairs={{0,4},{1,5},{2,6},{3,7},{4,0},{5,1},{6,2},{7,3},{8,12},{9,13},{10,... | collective-permute-start | bytes 884744 | tf_op jit(solution)/shard_map/ppermute | solution.py:32
  66.6 0.9 broadcast_in_dim.99
  67.4 2.0 %copy.77.bias_ref = bf16[1024,256]{1,0:T(8,128)(2,1)} copy(bf16[1024,256]{0,1:T(8,128)(2,1)} %bitcast.24) | data formatting | bytes 1048576 | tf_op jit(solution)/shard_map/reshape | solution.py:215
  69.5 1.4 copy.80.own_ref
  70.8 2.1 %copy.81.other_ref = bf16[512,576]{1,0:T(8,128)(2,1)} copy(bf16[512,576]{0,1:T(8,128)(2,1)} %collective-permute-done) | data formatting | bytes 1179648 | tf_op jit(solution)/shard_map/ppermute | solution.py:220
  73.0 1.7 %collective-permute-done.2.refs_2_.refs_6_ = bf16[256,576]{1,0:T(8,128)(2,1)} collective-permute-done((bf16[256,576]{1,0:T(8,128)(2,1)}, bf16[256,576]{1,0:T(8,128)(2,1)}, u32[]{:S(2)}, u32[]{:S(2)}) %collective-permute-start.2) | collective-permute-done | bytes 294944 | tf_op jit(solution)/shard_map/ppermute | solution.py:32
  74.7 6.6 %collective-permute-done.1.refs_1_.refs_5_ = bf16[256,576]{1,0:T(8,128)(2,1)} collective-permute-done((bf16[256,576]{1,0:T(8,128)(2,1)}, bf16[256,576]{1,0:T(8,128)(2,1)}, u32[]{:S(2)}, u32[]{:S(2)}) %collective-permute-start.1) | collective-permute-done | bytes 294944 | tf_op jit(solution)/shard_map/ppermute | solution.py:32
  81.3 1.1 copy-done.1
  82.4 1.0 copy-done.4
  83.4 0.9 copy-done.7
  84.4 6.6 %scores.1 = (bf16[4,1024,256]{2,1,0:T(8,128)(2,1)}, f32[4,1024,256]{2,1,0:T(8,128)}, f32[4,8,256]{2,1,0:T(8,128)S(1)}) custom-call(bf16[1024,256]{1,0:T(8,128)(2,1)S(1)} %copy-done.4, bf16[512,576]{1,0:T(8,128)(2,1)S(1)} %copy.80.own_ref, bf16[512,576]{1,0:T(8,128)(2,1)S(1)} %copy-done.1, bf16[256,576]{1,0:T(8,128)(2,1)} %bitcast.6.refs_0_.refs_4_, ...), custom_call_target="tpu_custom_call" | custom-call | tf_op jit(solution)/shard_map/scores/pallas_call | solution.py:223
  91.0 0.6 collective-permute-start.9
  91.6 3.0 %collective-permute-start.8 = (f32[4,8,256]{2,1,0:T(8,128)S(1)}, f32[4,8,256]{2,1,0:T(8,128)S(1)}, u32[]{:S(2)}, u32[]{:S(2)}) collective-permute-start(f32[4,8,256]{2,1,0:T(8,128)S(1)} %get-tuple-element.18.refs_0_), channel_id=1, source_target_pairs={{0,4},{1,5},{2,6},{3,7},{4,0},{5,1},{6,2},{7,3},{8,12},{9,13},{10,... | collective-permute-start | bytes 98312 | tf_op jit(solution)/shard_map/ppermute | solution.py:32
  94.6 0.8 collective-permute-start.7
  95.4 1.6 collective-permute-done.8.refs_2_
  97.0 2.7 %collective-permute-done.7.refs_1_ = f32[4,8,256]{2,1,0:T(8,128)S(1)} collective-permute-done((f32[4,8,256]{2,1,0:T(8,128)S(1)}, f32[4,8,256]{2,1,0:T(8,128)S(1)}, u32[]{:S(2)}, u32[]{:S(2)}) %collective-permute-start.7) | collective-permute-done | bytes 32800 | tf_op jit(solution)/shard_map/ppermute | solution.py:32
  99.7 8.0 %key_grad.1 = (bf16[4,1024,256]{2,1,0:T(8,128)(2,1)}, bf16[4,1024,256]{2,1,0:T(8,128)(2,1)}, f32[512,576]{1,0:T(8,128)S(1)}, bf16[512,576]{1,0:T(8,128)(2,1)S(1)}) custom-call(bf16[4,1024,256]{2,1,0:T(8,128)(2,1)} %get-tuple-element.16.p_ref, f32[4,1024,256]{2,1,0:T(8,128)} %get-tuple-element.17.gw_ref, f32[4,8,256]{2,1,0:T(8,128)S(1)} %get-tuple-element.18.refs_0_, ...), custom_call_target="tpu_custom_call" | custom-call | tf_op jit(solution)/shard_map/key_grad/pallas_call | solution.py:241
  107.7 0.9 copy-done.9
  108.6 1.1 copy-done.10
  109.7 2.1 %copy.82 = bf16[512,576]{0,1:T(8,128)(2,1)} copy(bf16[512,576]{1,0:T(8,128)(2,1)} %copy-done.9) | data formatting | bytes 1179648 | tf_op jit(solution)/shard_map/key_grad/pallas_call | solution.py:241
  111.8 2.3 %collective-permute-done.13 = bf16[512,576]{0,1:T(8,128)(2,1)} collective-permute-done((bf16[512,576]{0,1:T(8,128)(2,1)}, bf16[512,576]{0,1:T(8,128)(2,1)}, u32[]{:S(2)}, u32[]{:S(2)}) %collective-permute-start.13) | collective-permute-done | bytes 589856 | tf_op jit(solution)/shard_map/ppermute | solution.py:259
  114.2 2.1 %copy.83 = bf16[512,576]{1,0:T(8,128)(2,1)} copy(bf16[512,576]{0,1:T(8,128)(2,1)} %collective-permute-done.13) | data formatting | bytes 1179648 | tf_op jit(solution)/shard_map/ppermute | solution.py:259
  116.3 3.3 %fusion.3 = bf16[768,576]{0,1:T(8,128)(2,1)} fusion(s32[768]{0:T(1024)S(1)} %select_n.108, f32[512,576]{1,0:T(8,128)} %copy-done.10, bf16[512,576]{1,0:T(8,128)(2,1)} %copy.83), kind=kOutput, calls=%fused_computation.5 | convolution fusion | flops 454705152 | bytes 2657280 | tf_op jit(solution)/shard_map/dot_general | solution.py:274
  119.6 2.2 %copy.84 = bf16[768,576]{1,0:T(8,128)(2,1)} copy(bf16[768,576]{0,1:T(8,128)(2,1)} %fusion.3) | data formatting | bytes 1769472 | tf_op jit(solution)/shard_map/convert_element_type | solution.py:274
  121.8 5.6 %all-to-all-start.2 = ((bf16[32,24,576]{2,1,0:T(8,128)(2,1)}), bf16[32,24,576]{2,1,0:T(8,128)(2,1)}, u32[]{:S(2)}, u32[]{:S(2)}) async-start(bf16[32,24,576]{2,1,0:T(8,128)(2,1)} %bitcast.23), calls=%async_computation.2 | async-start | bytes 1966080 | tf_op jit(solution)/shard_map/all_to_all | solution.py:275
  127.4 1.1 copy-done.2
  128.5 1.6 copy-done.3
  130.1 4.5 %query_grad.1 = (bf16[1088,256]{1,0:T(8,128)(2,1)S(1)}, bf16[1088,256]{1,0:T(8,128)(2,1)S(1)}, bf16[1088,256]{1,0:T(8,128)(2,1)S(1)}, bf16[1088,256]{1,0:T(8,128)(2,1)S(1)}) custom-call(bf16[512,576]{1,0:T(8,128)(2,1)S(1)} %copy.80.own_ref, bf16[512,576]{1,0:T(8,128)(2,1)S(1)} %copy-done.2, bf16[4,1024,256]{2,1,0:T(8,128)(2,1)S(1)} %copy-done.3, ...), custom_call_target="tpu_custom_call" | custom-call | tf_op jit(solution)/shard_map/query_grad/pallas_call | solution.py:261
  134.9 1.4 collective-permute-start.11
  136.7 13.5 %collective-permute-done.10.refs_1_ = bf16[1088,256]{1,0:T(8,128)(2,1)S(1)} collective-permute-done((bf16[1088,256]{1,0:T(8,128)(2,1)S(1)}, bf16[1088,256]{1,0:T(8,128)(2,1)S(1)}, u32[]{:S(2)}, u32[]{:S(2)}) %collective-permute-start.10) | collective-permute-done | bytes 557088 | tf_op jit(solution)/shard_map/ppermute | solution.py:32
  150.2 1.8 %collective-permute-done.11.refs_2_ = bf16[1088,256]{1,0:T(8,128)(2,1)S(1)} collective-permute-done((bf16[1088,256]{1,0:T(8,128)(2,1)S(1)}, bf16[1088,256]{1,0:T(8,128)(2,1)S(1)}, u32[]{:S(2)}, u32[]{:S(2)}) %collective-permute-start.11) | collective-permute-done | bytes 557088 | tf_op jit(solution)/shard_map/ppermute | solution.py:32
  152.0 10.3 %collective-permute-done.12.refs_3_ = bf16[1088,256]{1,0:T(8,128)(2,1)S(1)} collective-permute-done((bf16[1088,256]{1,0:T(8,128)(2,1)S(1)}, bf16[1088,256]{1,0:T(8,128)(2,1)S(1)}, u32[]{:S(2)}, u32[]{:S(2)}) %collective-permute-start.12) | collective-permute-done | bytes 557088 | tf_op jit(solution)/shard_map/ppermute | solution.py:32
  162.3 1.1 combine.1
  163.4 1.8 %convolution_convert_fusion.1 = bf16[256,576]{0,1:T(8,128)(2,1)S(1)} fusion(bf16[768,576]{1,0:T(8,128)(2,1)} %bitcast.11, s32[768]{0:T(1024)S(1)} %select_n.111), kind=kOutput, calls=%fused_computation.9 | convolution fusion | flops 226836480 | bytes 1182720 | tf_op jit(solution)/shard_map/dot_general | solution.py:278
  165.2 0.9 copy.85
  (67 shorter events, 4.5 us)
Async XLA Ops:
  0.6 23.3 %copy-start = (bf16[32,64,576]{2,1,0:T(8,128)(2,1)S(1)}, bf16[32,64,576]{2,1,0:T(8,128)(2,1)}, u32[]{:S(2)}) copy-start(bf16[32,64,576]{2,1,0:T(8,128)(2,1)} %param.6) | copy-start | bytes 7077892
  3.2 20.2 %all-to-all-start = ((s32[32,1,3]{2,1,0:T(1,128)}), s32[32,1,3]{2,1,0:T(1,128)S(1)}, u32[]{:S(2)}, u32[]{:S(2)}) async-start(s32[32,1,3]{2,1,0:T(1,128)} %copy.72), calls=%async_computation | async-start | bytes 32768 | tf_op jit(solution)/shard_map/all_to_all | solution.py:177
  25.4 8.0 %copy-start.5 = (bf16[16,16,512]{2,1,0:T(8,128)(2,1)S(1)}, bf16[16,16,512]{2,1,0:T(8,128)(2,1)}, u32[]{:S(2)}) copy-start(bf16[16,16,512]{2,1,0:T(8,128)(2,1)} %param.7) | copy-start | bytes 786436
  27.7 31.3 %all-to-all-start.1 = ((bf16[32,24,576]{2,1,0:T(8,128)(2,1)}), bf16[32,24,576]{2,1,0:T(8,128)(2,1)}, u32[]{:S(2)}, u32[]{:S(2)}) async-start(bf16[32,24,576]{2,1,0:T(8,128)(2,1)} %bitcast.22), calls=%async_computation.1 | async-start | bytes 1966080 | tf_op jit(solution)/shard_map/all_to_all | solution.py:191
  33.4 28.7 %copy-start.11 = (s32[16,32]{1,0:T(8,128)S(1)}, s32[16,32]{1,0:T(8,128)}, u32[]{:S(2)}) copy-start(s32[16,32]{1,0:T(8,128)} %param.8) | copy-start | bytes 6148
  33.4 28.8 %collective-permute-start.6 = (bf16[256,512]{1,0:T(8,128)(2,1)S(1)}, bf16[256,512]{1,0:T(8,128)(2,1)S(1)}, u32[]{:S(2)}, u32[]{:S(2)}) collective-permute-start(bf16[256,512]{1,0:T(8,128)(2,1)S(1)} %bitcast.17), channel_id=1, source_target_pairs={{0,6},{1,7},{2,0},{3,1},{4,2},{5,3},{6,4},{7,5},{8,14},{9,15},{10,... | collective-permute-start | bytes 786440 | tf_op jit(solution)/shard_map/ppermute | solution.py:32
  36.2 36.8 %collective-permute-start.5 = (bf16[256,512]{1,0:T(8,128)(2,1)S(1)}, bf16[256,512]{1,0:T(8,128)(2,1)}, u32[]{:S(2)}, u32[]{:S(2)}) collective-permute-start(bf16[256,512]{1,0:T(8,128)(2,1)S(1)} %bitcast.18), channel_id=1, source_target_pairs={{0,4},{1,5},{2,6},{3,7},{4,0},{5,1},{6,2},{7,3},{8,12},{9,13},{10,... | collective-permute-start | bytes 786440 | tf_op jit(solution)/shard_map/ppermute | solution.py:32
  37.0 36.0 %collective-permute-start.4 = (bf16[256,512]{1,0:T(8,128)(2,1)S(1)}, bf16[256,512]{1,0:T(8,128)(2,1)}, u32[]{:S(2)}, u32[]{:S(2)}) collective-permute-start(bf16[256,512]{1,0:T(8,128)(2,1)S(1)} %bitcast.19), channel_id=1, source_target_pairs={{0,2},{1,3},{2,4},{3,5},{4,6},{5,7},{6,0},{7,1},{8,10},{9,11},{10,... | collective-permute-start | bytes 786440 | tf_op jit(solution)/shard_map/ppermute | solution.py:32
  37.9 35.1 %collective-permute-start.3 = (bf16[256,576]{1,0:T(8,128)(2,1)}, bf16[256,576]{1,0:T(8,128)(2,1)}, u32[]{:S(2)}, u32[]{:S(2)}) collective-permute-start(bf16[256,576]{1,0:T(8,128)(2,1)} %bitcast.6.refs_0_.refs_4_), channel_id=1, source_target_pairs={{0,6},{1,7},{2,0},{3,1},{4,2},{5,3},{6,4},{7,5},{8,14},{9,15},{10,... | collective-permute-start | bytes 884744 | tf_op jit(solution)/shard_map/ppermute | solution.py:32
  40.6 25.8 %copy-start.12 = (s32[16]{0:T(128)S(1)}, s32[16]{0:T(128)}, u32[]{:S(2)}) copy-start(s32[16]{0:T(128)} %param.9) | copy-start | bytes 196
  61.9 3.4 %collective-permute-start = (bf16[512,576]{0,1:T(8,128)(2,1)}, bf16[512,576]{0,1:T(8,128)(2,1)}, u32[]{:S(2)}, u32[]{:S(2)}) collective-permute-start(bf16[512,576]{0,1:T(8,128)(2,1)} %fusion.4), channel_id=1, source_target_pairs={{0,1},{1,0},{2,3},{3,2},{4,5},{5,4},{6,7},{7,6},{8,9},{9,8},{10,11... | collective-permute-start | bytes 1769480 | tf_op jit(solution)/shard_map/ppermute | solution.py:220
  62.2 5.2 %copy-start.6 = (bf16[256,512]{1,0:T(8,128)(2,1)}, bf16[256,512]{1,0:T(8,128)(2,1)S(1)}, u32[]{:S(2)}) copy-start(bf16[256,512]{1,0:T(8,128)(2,1)S(1)} %collective-permute-done.6.refs_7_.refs_11_) | copy-start | bytes 786436
  62.2 12.5 %collective-permute-start.2 = (bf16[256,576]{1,0:T(8,128)(2,1)}, bf16[256,576]{1,0:T(8,128)(2,1)}, u32[]{:S(2)}, u32[]{:S(2)}) collective-permute-start(bf16[256,576]{1,0:T(8,128)(2,1)} %bitcast.6.refs_0_.refs_4_), channel_id=1, source_target_pairs={{0,4},{1,5},{2,6},{3,7},{4,0},{5,1},{6,2},{7,3},{8,12},{9,13},{10,... | collective-permute-start | bytes 884744 | tf_op jit(solution)/shard_map/ppermute | solution.py:32
  65.4 15.9 %collective-permute-start.1 = (bf16[256,576]{1,0:T(8,128)(2,1)}, bf16[256,576]{1,0:T(8,128)(2,1)}, u32[]{:S(2)}, u32[]{:S(2)}) collective-permute-start(bf16[256,576]{1,0:T(8,128)(2,1)} %bitcast.6.refs_0_.refs_4_), channel_id=1, source_target_pairs={{0,2},{1,3},{2,4},{3,5},{4,6},{5,7},{6,0},{7,1},{8,10},{9,11},{10,... | collective-permute-start | bytes 884744 | tf_op jit(solution)/shard_map/ppermute | solution.py:32
  81.3 1.1 copy-start.1
  82.4 1.0 copy-start.4
  83.4 0.9 copy-start.7
  84.4 15.4 %copy-start.8 = (bf16[256,512]{1,0:T(8,128)(2,1)S(1)}, bf16[256,512]{1,0:T(8,128)(2,1)}, u32[]{:S(2)}) copy-start(bf16[256,512]{1,0:T(8,128)(2,1)} %copy-done.6) | copy-start | bytes 786436
  91.0 4.5 %collective-permute-start.9 = (f32[4,8,256]{2,1,0:T(8,128)S(1)}, f32[4,8,256]{2,1,0:T(8,128)S(1)}, u32[]{:S(2)}, u32[]{:S(2)}) collective-permute-start(f32[4,8,256]{2,1,0:T(8,128)S(1)} %get-tuple-element.18.refs_0_), channel_id=1, source_target_pairs={{0,6},{1,7},{2,0},{3,1},{4,2},{5,3},{6,4},{7,5},{8,14},{9,15},{10,... | collective-permute-start | bytes 98312 | tf_op jit(solution)/shard_map/ppermute | solution.py:32
  91.6 5.4 %collective-permute-start.8 = (f32[4,8,256]{2,1,0:T(8,128)S(1)}, f32[4,8,256]{2,1,0:T(8,128)S(1)}, u32[]{:S(2)}, u32[]{:S(2)}) collective-permute-start(f32[4,8,256]{2,1,0:T(8,128)S(1)} %get-tuple-element.18.refs_0_), channel_id=1, source_target_pairs={{0,4},{1,5},{2,6},{3,7},{4,0},{5,1},{6,2},{7,3},{8,12},{9,13},{10,... | collective-permute-start | bytes 98312 | tf_op jit(solution)/shard_map/ppermute | solution.py:32
  94.6 5.1 %collective-permute-start.7 = (f32[4,8,256]{2,1,0:T(8,128)S(1)}, f32[4,8,256]{2,1,0:T(8,128)S(1)}, u32[]{:S(2)}, u32[]{:S(2)}) collective-permute-start(f32[4,8,256]{2,1,0:T(8,128)S(1)} %get-tuple-element.18.refs_0_), channel_id=1, source_target_pairs={{0,2},{1,3},{2,4},{3,5},{4,6},{5,7},{6,0},{7,1},{8,10},{9,11},{10,... | collective-permute-start | bytes 98312 | tf_op jit(solution)/shard_map/ppermute | solution.py:32
  107.7 0.9 copy-start.9
  108.6 1.1 copy-start.10
  111.8 2.3 %collective-permute-start.13 = (bf16[512,576]{0,1:T(8,128)(2,1)}, bf16[512,576]{0,1:T(8,128)(2,1)}, u32[]{:S(2)}, u32[]{:S(2)}) collective-permute-start(bf16[512,576]{0,1:T(8,128)(2,1)} %copy.82), channel_id=1, source_target_pairs={{0,1},{1,0},{2,3},{3,2},{4,5},{5,4},{6,7},{7,6},{8,9},{9,8},{10,11... | collective-permute-start | bytes 1769480 | tf_op jit(solution)/shard_map/ppermute | solution.py:259
  121.8 41.6 %all-to-all-start.2 = ((bf16[32,24,576]{2,1,0:T(8,128)(2,1)}), bf16[32,24,576]{2,1,0:T(8,128)(2,1)}, u32[]{:S(2)}, u32[]{:S(2)}) async-start(bf16[32,24,576]{2,1,0:T(8,128)(2,1)} %bitcast.23), calls=%async_computation.2 | async-start | bytes 1966080 | tf_op jit(solution)/shard_map/all_to_all | solution.py:275
  127.4 1.1 copy-start.2
  128.5 1.6 copy-start.3
  134.6 15.6 %collective-permute-start.10 = (bf16[1088,256]{1,0:T(8,128)(2,1)S(1)}, bf16[1088,256]{1,0:T(8,128)(2,1)S(1)}, u32[]{:S(2)}, u32[]{:S(2)}) collective-permute-start(bf16[1088,256]{1,0:T(8,128)(2,1)S(1)} %get-tuple-element.22), channel_id=1, source_target_pairs={{0,6},{1,7},{2,0},{3,1},{4,2},{5,3},{6,4},{7,5},{8,14},{9,15},{10,... | collective-permute-start | bytes 1671176 | tf_op jit(solution)/shard_map/ppermute | solution.py:32
  134.9 17.1 %collective-permute-start.11 = (bf16[1088,256]{1,0:T(8,128)(2,1)S(1)}, bf16[1088,256]{1,0:T(8,128)(2,1)S(1)}, u32[]{:S(2)}, u32[]{:S(2)}) collective-permute-start(bf16[1088,256]{1,0:T(8,128)(2,1)S(1)} %get-tuple-element.23), channel_id=1, source_target_pairs={{0,4},{1,5},{2,6},{3,7},{4,0},{5,1},{6,2},{7,3},{8,12},{9,13},{10,... | collective-permute-start | bytes 1671176 | tf_op jit(solution)/shard_map/ppermute | solution.py:32
  136.3 26.0 %collective-permute-start.12 = (bf16[1088,256]{1,0:T(8,128)(2,1)S(1)}, bf16[1088,256]{1,0:T(8,128)(2,1)S(1)}, u32[]{:S(2)}, u32[]{:S(2)}) collective-permute-start(bf16[1088,256]{1,0:T(8,128)(2,1)S(1)} %get-tuple-element.24), channel_id=1, source_target_pairs={{0,2},{1,3},{2,4},{3,5},{4,6},{5,7},{6,0},{7,1},{8,10},{9,11},{10,... | collective-permute-start | bytes 1671176 | tf_op jit(solution)/shard_map/ppermute | solution.py:32

commit v2 on v0

v2 whole, which is shorter than its diff:
```python
import functools
import math

import jax
import jax.numpy as jnp
from jax import lax
from jax.experimental import pallas as pl
from jax.experimental.pallas import tpu as pltpu
from jax.sharding import PartitionSpec as P

USED = 64
XN = 4
CORES = 2

score_scale = 192.0 ** (-0.5)
log2e = 1.0 / math.log(2.0)
VMEM_LIMIT = 24 * 1024 * 1024
bf16 = jnp.bfloat16
f32 = jnp.float32


def x_shift(k):
    return [
        (x * CORES + c, ((x + k) % XN) * CORES + c) for x in range(XN) for c in range(CORES)
    ]


CORE_SWAP = [(t, t ^ 1) for t in range(XN * CORES)]


def send_x(value, k):
    return lax.ppermute(value, "tp", x_shift(k % XN))


def nt_dot(a, b):
    return lax.dot_general(a, b, (((1,), (1,)), ((), ())), preferred_element_type=f32)


def expand(rows, tokens):
    count, lanes = rows.shape
    wide = jnp.broadcast_to(rows[:, None, :], (count, tokens, lanes))
    return wide.reshape(count * tokens, lanes)


def iotas(shape):
    return (lax.broadcasted_iota(jnp.int32, shape, 0), lax.broadcasted_iota(jnp.int32, shape, 1))


def bit_matrix(mask):
    return jnp.where(mask, 1.0, 0.0).astype(bf16)


def dot32(a, b):
    return jnp.dot(a, b, preferred_element_type=f32)


def pack_kernel(tokens, slot_limit, place_ref, asked_ref, rows_ref, *refs):
    out_ref, hot_ref = refs[-2:]
    owners, _, block_count = asked_ref.shape
    pair = rows_ref.shape[1]
    wanted = asked_ref[:, 0, :].astype(f32)
    row, lane = iotas((block_count, block_count))
    rank = dot32(wanted.astype(bf16), bit_matrix(row < lane))
    row, lane = iotas((owners * slot_limit, owners))
    slot = jnp.zeros((owners * slot_limit, block_count), f32)
    for j in range(slot_limit):
        level = jnp.where(rank == j, wanted, 0.0).astype(bf16)
        slot += dot32(bit_matrix(row == lane * slot_limit + j), level)
    slot = slot.astype(bf16)
    for size, first, out in ((pair, place_ref[1] * tokens, None), (tokens, 0, hot_ref)):
        row, lane = iotas((block_count, block_count * size))
        start = row * size
        hot = expand(dot32(slot, bit_matrix((lane >= start) & (lane < start + size))), tokens)
        row, lane = iotas(hot.shape)
        same = (row & (tokens - 1)) + first == (lane & (size - 1))
        hot = jnp.where(same, hot, 0.0).astype(bf16)
        if out is None:
            rows = rows_ref[...].reshape(block_count * size, rows_ref.shape[2])
            out_ref[...] = dot32(hot, rows).astype(bf16)
        else:
            out[...] = hot


def owner_kernel(hot_ref, rows_ref, out_ref):
    total = lax.dot_general(
        hot_ref[...], rows_ref[...], (((0,), (0,)), ((), ())), preferred_element_type=f32
    )
    out_ref[...] = total.astype(bf16)


def slot_hot(ids_ref, tokens, lanes):
    ids = expand(jnp.broadcast_to(ids_ref[:, 0:1], (ids_ref.shape[0], lanes)), tokens)
    row, lane = iotas(ids.shape)
    return bit_matrix(ids * tokens + (row & (tokens - 1)) == lane)


def score_kernel(tokens, pick_ref, own_lim, other_lim, own_ref, other_ref, *refs):
    q_refs, g_refs = refs[:XN], refs[XN : 2 * XN]
    p_ref, gw_ref, stat_ref, key_ref, bias_ref = refs[2 * XN :]
    half = key_ref.shape[0] // CORES
    rows = bias_ref.shape[1]
    query_count = own_lim.shape[1]
    heads = rows // query_count
    value_width = g_refs[0].shape[1]
    row, lane = iotas((query_count, rows))
    start = row * heads
    repeat = bit_matrix((lane >= start) & (lane < start + heads))
    hot = slot_hot(pick_ref, tokens, own_ref.shape[0])
    for h, (lim, part_ref) in enumerate(((own_lim, own_ref), (other_lim, other_ref))):
        part = pl.ds(h * half, half)
        key_ref[part, :] = dot32(hot, part_ref[...]).astype(bf16)
        limit = expand(dot32(lim[...].astype(bf16), repeat), tokens)
        token = (iotas(limit.shape)[0] & (tokens - 1)).astype(f32)
        bias_ref[part, :] = jnp.where(token <= limit, 0.0, -jnp.inf)
    for k in range(XN):
        q, g = q_refs[k][...], g_refs[k][...]
        scores = nt_dot(key_ref[...], q) * (score_scale * log2e) + bias_ref[...]
        peak = jnp.max(scores, axis=0, keepdims=True)
        p = jnp.exp2(scores - peak)
        gw = nt_dot(key_ref[:, :value_width], g)
        p_ref[k] = p.astype(bf16)
        gw_ref[k] = gw
        stat_ref[k, 0:1, :] = peak
        stat_ref[k, 1:2, :] = jnp.sum(p, axis=0, keepdims=True)
        stat_ref[k, 2:3, :] = jnp.sum(p * gw, axis=0, keepdims=True)
        stat_ref[k, 3:8, :] = jnp.zeros((5, peak.shape[1]), f32)


def grad_kernel(tokens, order_ref, key_ref, p_ref, gw_ref, *refs):
    stat_refs, q_refs, g_refs = refs[:XN], refs[XN : 2 * XN], refs[2 * XN : 3 * XN]
    own_ref, other_ref, here_ref, right_ref, left_ref, att3_ref, qg1_ref = refs[3 * XN : -4]
    acc_ref, lhs_ref, rhs_ref, keys_t = refs[-4:]
    rows, width = q_refs[0].shape
    value_width = g_refs[0].shape[1]
    half = key_ref.shape[0] // CORES
    att_out = (
        here_ref.at[:value_width],
        left_ref.at[:value_width],
        right_ref.at[:value_width],
        att3_ref,
    )
    qg_out = (
        here_ref.at[value_width:],
        qg1_ref,
        left_ref.at[value_width:],
        right_ref.at[value_width:],
    )
    rhs_ref[rows:, value_width:] = jnp.zeros((rows, width - value_width), bf16)
    keys_t[...] = key_ref[...].T
    for k in (2, 3, 1, 0):
        stats = [stat_refs[j][(k - j) % XN] for j in range(XN)]
        peak = functools.reduce(jnp.maximum, [s[0:1] for s in stats])
        factors = [jnp.exp2(s[0:1] - peak) for s in stats]
        total = sum(s[1:2] * f for s, f in zip(stats, factors))
        inner = sum(s[2:3] * f for s, f in zip(stats, factors)) / total
        factor = factors[0] / total
        weights = p_ref[k].astype(f32) * factor
        ds = (weights * (gw_ref[k] - inner) * score_scale).astype(bf16)
        w = weights.astype(bf16)
        att_out[k][...] = dot32(keys_t[:value_width, :], w).astype(bf16)
        qg_out[k][...] = dot32(keys_t[...], ds).astype(bf16)
        lhs_ref[:, :rows] = ds
        lhs_ref[:, rows:] = w
        rhs_ref[:rows, :] = q_refs[k][...]
        rhs_ref[rows:, :value_width] = g_refs[k][...]
        grad = dot32(lhs_ref[...], rhs_ref[...])
        if k == 2:
            acc_ref[...] = grad
        else:
            acc_ref[...] += grad
    hot = slot_hot(order_ref, tokens, half)
    own_ref[...] = dot32(hot, acc_ref[:half, :].astype(bf16)).astype(bf16)
    other_ref[...] = dot32(hot, acc_ref[half:, :].astype(bf16)).astype(bf16)


def combine_kernel(here, right, left, att, qg, att_ref, qg_ref):
    value_width = att_ref.shape[1]
    total = here[:value_width].astype(f32) + left[:value_width].astype(f32) + att[...].astype(f32)
    att_ref[...] = total.astype(bf16).T
    total = here[value_width:].astype(f32) + right[value_width:].astype(f32) + qg[...].astype(f32)
    qg_ref[...] = total.astype(bf16).T


def shaped(shape, dtype=bf16):
    return jax.ShapeDtypeStruct(shape, dtype)


def call(kernel, out_shape, operands, name, unused=(), scratch=()):
    return pl.pallas_call(
        kernel,
        out_shape=out_shape,
        in_specs=[pl.BlockSpec(memory_space=pltpu.VMEM)] * len(operands)
        + [pl.BlockSpec(memory_space=pl.ANY)] * len(unused),
        scratch_shapes=list(scratch),
        compiler_params=pltpu.CompilerParams(vmem_limit_bytes=VMEM_LIMIT),
        name=name,
    )(*operands, *unused)


def slot_table(wanted, slot_limit):
    rank_within = jnp.cumsum(wanted.astype(jnp.int32), axis=1) - 1
    local_ids = jnp.arange(wanted.shape[1], dtype=jnp.int32)
    slot_range = jnp.arange(slot_limit, dtype=jnp.int32)
    matches = wanted[:, None, :] & (rank_within[:, None, :] == slot_range[None, :, None])
    present = jnp.any(matches, axis=2)
    found_ids = jnp.sum(jnp.where(matches, local_ids[None, None, :], 0), axis=2)
    return jnp.where(present, found_ids, -1).reshape(-1)


def on_device(queries, latent_cache, output_gradient, selected, positions):
    query_count, head_count, width = queries.shape
    block_count, block_size, _ = latent_cache.shape
    value_width = output_gradient.shape[2]
    owners = lax.axis_size("ctx")
    tp = lax.axis_index("tp")
    tokens = block_size // (XN * CORES)
    slot_limit = (USED - 2) // (owners - 1) + 1
    slots = owners * slot_limit
    rows = query_count * head_count
    half = USED * tokens
    keys = CORES * half
    held = block_count * tokens
    parcels = (owners, slot_limit * tokens, width)

    block_range = jnp.arange(owners * block_count, dtype=jnp.int32)
    wanted = jnp.any(selected.reshape(-1)[:, None] == block_range[None, :], axis=0)
    wanted = wanted.reshape(owners, block_count)
    asked = lax.all_to_all(
        wanted.astype(jnp.int32)[:, None, :], "ctx", split_axis=0, concat_axis=0, tiled=True
    )

    query_rows = queries.reshape(rows, width)
    grad_rows = output_gradient.reshape(rows, value_width)
    q1, q3 = send_x(query_rows, 1), send_x(query_rows, -1)
    g1, g3 = send_x(grad_rows, 1), send_x(grad_rows, -1)
    q2, g2 = send_x(q1, 1), send_x(g3, -1)
    q_parts, g_parts = [query_rows, q1, q2, q3], [grad_rows, g1, g2, g3]

    requests = slot_table(wanted, slot_limit)
    used_slot = requests >= 0
    slot_order = jnp.where(used_slot, jnp.cumsum(used_slot.astype(jnp.int32)) - 1, -1)
    compact = jnp.arange(USED, dtype=jnp.int32)
    slot_match = slot_order[None, :] == compact[:, None]
    slot_ids = jnp.arange(slots, dtype=jnp.int32)
    slot_block = slot_ids // slot_limit * block_count + requests
    picked = jnp.sum(jnp.where(slot_match, slot_ids[None, :], 0), axis=1)
    block_ids = jnp.sum(jnp.where(slot_match, slot_block[None, :], 0), axis=1)
    chosen = jnp.any(selected[None, :, :] == block_ids[:, None, None], axis=2)
    limit = jnp.where(chosen, positions[None, :] - block_ids[:, None] * block_size, -1)
    limit = jnp.clip(limit, -1, block_size - 1)
    own_limit = (limit - tp * tokens).astype(f32)
    other_limit = (limit - (tp ^ 1) * tokens).astype(f32)
    pick = jnp.broadcast_to(picked[:, None], (USED, 128))
    order = jnp.broadcast_to(slot_order[:, None], (slots, 128))

    early = (q1, q2, q3, g1, g2, g3, own_limit, other_limit, pick, order)
    place = jnp.stack([tp // CORES, tp % CORES]).astype(jnp.int32)
    packed, asked_hot = pl.pallas_call(
        functools.partial(pack_kernel, tokens, slot_limit),
        grid_spec=pltpu.PrefetchScalarGridSpec(
            num_scalar_prefetch=1,
            grid=(1,),
            in_specs=[
                pl.BlockSpec((owners, 1, block_count), lambda i, place: (0, 0, 0)),
                pl.BlockSpec(
                    (block_count, CORES * tokens, width), lambda i, place: (0, place[0], 0)
                ),
            ]
            + [pl.BlockSpec(memory_space=pl.ANY)] * len(early),
            out_specs=[
                pl.BlockSpec((slots * tokens, width), lambda i, place: (0, 0)),
                pl.BlockSpec((slots * tokens, held), lambda i, place: (0, 0)),
            ],
        ),
        out_shape=[shaped((slots * tokens, width)), shaped((slots * tokens, held))],
        compiler_params=pltpu.CompilerParams(vmem_limit_bytes=VMEM_LIMIT),
        name="pack",
    )(place, asked, latent_cache, *early)
    fetched = lax.all_to_all(packed.reshape(parcels), "ctx", 0, 0, tiled=True)
    fetched_other = lax.ppermute(fetched, "tp", CORE_SWAP)

    p, gw, stats, key_rows = call(
        functools.partial(score_kernel, tokens),
        [
            shaped((XN, keys, rows)),
            shaped((XN, keys, rows), f32),
            shaped((XN, 8, rows), f32),
            shaped((keys, width)),
        ],
        [
            pick,
            own_limit,
            other_limit,
            fetched.reshape(slots * tokens, width),
            fetched_other.reshape(slots * tokens, width),
            *q_parts,
            *g_parts,
        ],
        "scores",
        scratch=[pltpu.VMEM((keys, rows), f32)],
    )
    all_stats = [stats] + [send_x(stats, k) for k in range(1, XN)]

    both = width + value_width
    own_grad, other_grad, here, right, left, att3, qg1 = call(
        functools.partial(grad_kernel, tokens),
        [shaped((slots * tokens, width))] * 2
        + [shaped((n, rows)) for n in (both, both, both, value_width, width)],
        [order, key_rows, p, gw, *all_stats, *q_parts, *g_parts],
        "grads",
        scratch=[
            pltpu.VMEM((keys, width), f32),
            pltpu.VMEM((keys, 2 * rows), bf16),
            pltpu.VMEM((2 * rows, width), bf16),
            pltpu.VMEM((width, keys), bf16),
        ],
    )
    from_core = lax.ppermute(other_grad.reshape(parcels), "tp", CORE_SWAP)
    returning = (own_grad.reshape(parcels).astype(f32) + from_core.astype(f32)).astype(bf16)
    returned = lax.all_to_all(returning, "ctx", 0, 0, tiled=True)

    right, left = send_x(right, 1), send_x(left, -1)
    att = (att3.astype(f32) + right[:value_width].astype(f32)).astype(bf16)
    qg = (qg1.astype(f32) + left[value_width:].astype(f32)).astype(bf16)
    attended, query_grad = call(
        combine_kernel,
        [shaped((rows, value_width)), shaped((rows, width))],
        [here, right, left, send_x(att, 1), send_x(qg, -1)],
        "combine",
    )
    cache_grad = call(
        owner_kernel,
        shaped((held, width)),
        [asked_hot, returned.reshape(slots * tokens, width)],
        "owner_sum",
    )
    return (
        attended.reshape(query_count, head_count, value_width),
        query_grad.reshape(query_count, head_count, width),
        cache_grad.reshape(block_count, tokens, width),
    )


def solution(mesh):
    in_specs = (
        P("ctx", "tp", None),
        P("ctx", None, None),
        P("ctx", "tp", None),
        P("ctx", None),
        P("ctx"),
    )
    out_specs = (P("ctx", "tp", None), P("ctx", "tp", None), P("ctx", "tp", None))
    return jax.shard_map(
        on_device, mesh=mesh, in_specs=in_specs, out_specs=out_specs, check_vma=False
    )
```

time: 772 us -> 132 us (0.17)
  waiting for transfers between devices: 581 us -> 37.9 us
  local copies, waits for them, and re-layouts: 81.7 us -> 4.72 us
  matrix products: 43.3 us -> 0 us
  starting transfers between devices: 14.7 us -> 34.3 us
  Pallas kernels: 0 us -> 16 us
  blocking collectives: 20 us -> 33.5 us
  between operations: 14.3 us -> 0.83 us
  other arithmetic: 16.5 us -> 4.27 us
    all_to_all x2, waiting for transfers between devices: 527 us -> 2.37 us  [the longest x1 1.95 us: on_device(): lax.all_to_all(wanted.astype(jnp.int32)[:, None, :], 'ctx', split_axis=0,...]
    reduce_scatter x1 -> x0, waiting for transfers between devices: 53.6 us -> none  [on_device(): cache_grad = lax.psum_scatter(summed, 'tp', scatter_dimension=1, tiled=True)]
    dot_general x7 -> x0, matrix products: 43.3 us -> none  [the longest x1 20.7 us: owner_sum(): jnp.einsum('sb,sx->bx', onehot, flat_rows, precision=lax.Precision.HIGHES...]
    ppermute x0 -> x15, waiting for transfers between devices: none -> 35.5 us  [the longest x13 30.4 us: send_x(): return lax.ppermute(value, 'tp', x_shift(k % XN))]
    gather x4 -> x0, local copies, waits for them, and re-layouts: 28.9 us -> none  [the longest x1 14.4 us: spread_slots(): slot_grad = jnp.where(used_slot[:, None, None], block_grad[back_ids], 0.0)]
    dot_general x1 -> x0, local copies, waits for them, and re-layouts: 17.5 us -> none  [owner_sum(): jnp.einsum('sb,sx->bx', onehot, flat_rows, precision=lax.Precision.HIGHES...]
    reshape x1 -> x0, local copies, waits for them, and re-layouts: 17.5 us -> none  [owner_sum(): flat_rows = received.reshape(onehot.shape[0], -1)]
    ppermute x0 -> x15, starting transfers between devices: none -> 17 us  [the longest x13 17 us: send_x(): return lax.ppermute(value, 'tp', x_shift(k % XN))]
  transfers between devices with their start and end apart: 3 -> 17, of which waited for: 3 -> 11; matrix products, arithmetic and copies ran while one was open for 2% -> 4% of each run, Pallas kernels for 0% -> 1%
where the time goes in v2:
time: 132 us; the launch traced here: 131 us
  waiting for transfers between devices  37.9 us (29%)
  starting transfers between devices  34.3 us (26%)
  blocking collectives  33.5 us (25%)
  Pallas kernels  16 us (12%)
  local copies, waits for them, and re-layouts  4.72 us (4%)
  other arithmetic  4.27 us (3%)
    all_to_all x1, blocking collectives, on_device(): fetched = lax.all_to_all(packed.reshape(parcels), 'ctx', 0, 0, tiled=True)  33.5 us
    ppermute x13, waiting for transfers between devices, send_x(): return lax.ppermute(value, 'tp', x_shift(k % XN))  30.4 us
    ppermute x13, starting transfers between devices, send_x(): return lax.ppermute(value, 'tp', x_shift(k % XN))  17 us
    pallas_call x4, Pallas kernels, call(): pl.pallas_call(kernel, out_shape=out_shape, in_specs=[pl.BlockSpec(memory...  14.2 us
    all_to_all x1, starting transfers between devices, on_device(): lax.all_to_all(wanted.astype(jnp.int32)[:, None, :], 'ctx', split_axis=0,...  11.7 us
    all_to_all x1, starting transfers between devices, on_device(): returned = lax.all_to_all(returning, 'ctx', 0, 0, tiled=True)  5.57 us
  transfers between devices with their start and end apart: 17, of which 11 were waited for; matrix products, arithmetic and copies ran while one was open for 4% of the time, Pallas kernels for 1%

profile of v2, /device:TPU:8, one launch (start us, length us, event | category | flops | bytes accessed | tf_op | source)
XLA Modules:
  0.0 131.4 jit_solution(16323773540746840681)
XLA Ops:
  0.6 2.8 %collective-permute-start.4 = (bf16[256,512]{1,0:T(8,128)(2,1)}, bf16[256,512]{1,0:T(8,128)(2,1)S(1)}, u32[]{:S(2)}, u32[]{:S(2)}) collective-permute-start(bf16[256,512]{1,0:T(8,128)(2,1)} %bitcast.20), channel_id=1, source_target_pairs={{0,6},{1,7},{2,0},{3,1},{4,2},{5,3},{6,4},{7,5},{8,14},{9,15},{10,... | collective-permute-start | bytes 786440 | tf_op jit(solution)/shard_map/ppermute | solution.py:32
  3.5 3.2 %collective-permute-start.2 = (bf16[256,576]{1,0:T(8,128)(2,1)}, bf16[256,576]{1,0:T(8,128)(2,1)S(1)}, u32[]{:S(2)}, u32[]{:S(2)}) collective-permute-start(bf16[256,576]{1,0:T(8,128)(2,1)} %bitcast.16), channel_id=1, source_target_pairs={{0,6},{1,7},{2,0},{3,1},{4,2},{5,3},{6,4},{7,5},{8,14},{9,15},{10,... | collective-permute-start | bytes 884744 | tf_op jit(solution)/shard_map/ppermute | solution.py:32
  6.7 0.8 eq.27
  7.5 0.4 fusion
  7.8 0.7 reshape.174
  8.5 11.7 %all-to-all-start = ((s32[32,1,32]{2,1,0:T(1,128)}), s32[32,1,32]{2,1,0:T(1,128)S(1)}, u32[]{:S(2)}, u32[]{:S(2)}) async-start(s32[32,1,32]{2,1,0:T(1,128)} %reshape.174), calls=%async_computation | async-start | bytes 32768 | tf_op jit(solution)/shard_map/all_to_all | solution.py:228
  20.2 0.1 and.29
  20.3 0.2 reduce_window_sum.18
  20.5 0.2 fusion.3
  20.7 0.1 select_reduce_fusion
  20.9 0.1 copy.11
  20.9 0.1 copy.10
  21.0 0.1 select_n.75
  21.1 0.1 reshape.176
  21.2 0.1 reduce-window.7
  21.4 0.1 add_reduce_fusion
  21.5 0.1 select_reduce_fusion.1
  21.6 0.9 compare_reduce_fusion
  22.5 0.1 copy.13
  22.6 3.3 %collective-permute-start.5 = (bf16[256,512]{1,0:T(8,128)(2,1)S(1)}, bf16[256,512]{1,0:T(8,128)(2,1)S(1)}, u32[]{:S(2)}, u32[]{:S(2)}) collective-permute-start(bf16[256,512]{1,0:T(8,128)(2,1)S(1)} %collective-permute-done.4.refs_5_.refs_7_.refs_11_), channel_id=1, source_target_pairs={{0,6},{1,7},{2,0},{3,1},{4,2},{5,3},{6,4},{7,5},{8,14},{9,15},{10,... | collective-permute-start | bytes 786440 | tf_op jit(solution)/shard_map/ppermute | solution.py:32
  25.9 0.7 subtract_convert_fusion
  26.8 2.0 %all-to-all-done.asked_ref = s32[32,1,32]{2,1,0:T(1,128)S(1)} async-done(((s32[32,1,32]{2,1,0:T(1,128)}), s32[32,1,32]{2,1,0:T(1,128)S(1)}, u32[]{:S(2)}, u32[]{:S(2)}) %all-to-all-start) | async-done | bytes 4128 | tf_op jit(solution)/shard_map/all_to_all | solution.py:228
  28.7 1.1 collective-permute-done.5.refs_4_.refs_6_.refs_10_
  29.8 4.8 %collective-permute-done.1.refs_1_.refs_2_.refs_6_ = bf16[256,576]{1,0:T(8,128)(2,1)S(1)} collective-permute-done((bf16[256,576]{1,0:T(8,128)(2,1)S(1)}, bf16[256,576]{1,0:T(8,128)(2,1)S(1)}, u32[]{:S(2)}, u32[]{:S(2)}) %collective-permute-start.1) | collective-permute-done | bytes 294944 | tf_op jit(solution)/shard_map/ppermute | solution.py:32
  34.8 1.8 %copy-done = bf16[32,64,576]{2,1,0:T(8,128)(2,1)S(1)} copy-done((bf16[32,64,576]{2,1,0:T(8,128)(2,1)S(1)}, bf16[32,64,576]{2,1,0:T(8,128)(2,1)}, u32[]{:S(2)}) %copy-start) | copy-done | bytes 2359320
  36.5 1.9 %pack.1 = (bf16[768,576]{1,0:T(8,128)(2,1)S(1)}, bf16[768,256]{1,0:T(8,128)(2,1)S(1)}) custom-call(s32[2]{0:T(128)S(1)} %pad_add_fusion.place_ref, s32[32,1,32]{2,1,0:T(1,128)S(1)} %all-to-all-done.asked_ref, bf16[32,64,576]{2,1,0:T(8,128)(2,1)S(1)} %copy-done, bf16[256,576]{1,0:T(8,128)(2,1)S(1)} %collective-permute-done.refs_0_.refs_1_.refs_5_, ...), custom_call_target="tpu_custom_call" | custom-call | tf_op jit(solution)/shard_map/pack/pallas_call | solution.py:258
  38.4 33.5 %all_to_all.15 = bf16[32,24,576]{2,1,0:T(8,128)(2,1)S(1)} all-to-all(bf16[32,24,576]{2,1,0:T(8,128)(2,1)S(1)} %bitcast.26), channel_id=1, replica_groups=mesh['ctx'=32,'tp'=8] {'ctx'}, dimensions={0} | all-to-all | bytes 1769472 | tf_op jit(solution)/shard_map/all_to_all | solution.py:279
  71.9 2.6 %collective-permute-done.6 = bf16[32,24,576]{2,1,0:T(8,128)(2,1)S(1)} collective-permute-done((bf16[32,24,576]{2,1,0:T(8,128)(2,1)S(1)}, bf16[32,24,576]{2,1,0:T(8,128)(2,1)S(1)}, u32[]{:S(2)}, u32[]{:S(2)}) %collective-permute-start.6) | collective-permute-done | bytes 884768 | tf_op jit(solution)/shard_map/ppermute | solution.py:280
  74.5 4.9 %scores.1 = (bf16[4,1024,256]{2,1,0:T(8,128)(2,1)S(1)}, f32[4,1024,256]{2,1,0:T(8,128)S(1)}, f32[4,8,256]{2,1,0:T(8,128)S(1)}, bf16[1024,576]{1,0:T(8,128)(2,1)S(1)}) custom-call(s32[64,128]{1,0:T(8,128)S(1)} %broadcast_in_dim.75.refs_8_.pick_ref, f32[64,16]{1,0:T(8,128)S(1)} %get-tuple-element.38.refs_6_.own_lim, ...), custom_call_target="tpu_custom_call" | custom-call | tf_op jit(solution)/shard_map/scores/pallas_call | solution.py:189
  79.3 0.1 collective-permute-start.9
  79.4 1.4 %collective-permute-start.8 = (f32[4,8,256]{2,1,0:T(8,128)S(1)}, f32[4,8,256]{2,1,0:T(8,128)S(1)}, u32[]{:S(2)}, u32[]{:S(2)}) collective-permute-start(f32[4,8,256]{2,1,0:T(8,128)S(1)} %get-tuple-element.22.refs_0_), channel_id=1, source_target_pairs={{0,4},{1,5},{2,6},{3,7},{4,0},{5,1},{6,2},{7,3},{8,12},{9,13},{10,... | collective-permute-start | bytes 98312 | tf_op jit(solution)/shard_map/ppermute | solution.py:32
  80.8 0.6 collective-permute-start.7
  81.4 1.9 %collective-permute-done.9.refs_3_ = f32[4,8,256]{2,1,0:T(8,128)S(1)} collective-permute-done((f32[4,8,256]{2,1,0:T(8,128)S(1)}, f32[4,8,256]{2,1,0:T(8,128)S(1)}, u32[]{:S(2)}, u32[]{:S(2)}) %collective-permute-start.9) | collective-permute-done | bytes 32800 | tf_op jit(solution)/shard_map/ppermute | solution.py:32
  83.3 1.7 %collective-permute-done.8.refs_2_ = f32[4,8,256]{2,1,0:T(8,128)S(1)} collective-permute-done((f32[4,8,256]{2,1,0:T(8,128)S(1)}, f32[4,8,256]{2,1,0:T(8,128)S(1)}, u32[]{:S(2)}, u32[]{:S(2)}) %collective-permute-start.8) | collective-permute-done | bytes 32800 | tf_op jit(solution)/shard_map/ppermute | solution.py:32
  85.0 1.0 collective-permute-done.7.refs_1_
  86.0 7.1 %grads.1 = (bf16[768,576]{1,0:T(8,128)(2,1)S(1)}, bf16[768,576]{1,0:T(8,128)(2,1)S(1)}, bf16[1088,256]{1,0:T(8,128)(2,1)S(1)}, bf16[1088,256]{1,0:T(8,128)(2,1)}...) custom-call(s32[96,128]{1,0:T(8,128)S(1)} %broadcast_in_dim.72.refs_9_.order_ref, ...), custom_call_target="tpu_custom_call" | custom-call | tf_op jit(solution)/shard_map/grads/pallas_call | solution.py:189
  93.1 0.8 copy-done.3
  93.9 2.6 %collective-permute-done.14 = bf16[32,24,576]{2,1,0:T(8,128)(2,1)S(1)} collective-permute-done((bf16[32,24,576]{2,1,0:T(8,128)(2,1)S(1)}, bf16[32,24,576]{2,1,0:T(8,128)(2,1)S(1)}, u32[]{:S(2)}, u32[]{:S(2)}) %collective-permute-start.14) | collective-permute-done | bytes 884768 | tf_op jit(solution)/shard_map/ppermute | solution.py:318
  96.4 1.2 fusion.1
  97.7 5.6 %all-to-all-start.2 = ((bf16[32,24,576]{2,1,0:T(8,128)(2,1)}), bf16[32,24,576]{2,1,0:T(8,128)(2,1)S(1)}, u32[]{:S(2)}, u32[]{:S(2)}) async-start(bf16[32,24,576]{2,1,0:T(8,128)(2,1)} %fusion.1), calls=%async_computation.2 | async-start | bytes 1966080 | tf_op jit(solution)/shard_map/all_to_all | solution.py:320
  103.2 2.1 %collective-permute-start.11 = (bf16[1088,256]{1,0:T(8,128)(2,1)S(1)}, bf16[1088,256]{1,0:T(8,128)(2,1)S(1)}, u32[]{:S(2)}, u32[]{:S(2)}) collective-permute-start(bf16[1088,256]{1,0:T(8,128)(2,1)S(1)} %copy-done.4), channel_id=1, source_target_pairs={{0,6},{1,7},{2,0},{3,1},{4,2},{5,3},{6,4},{7,5},{8,14},{9,15},{10,... | collective-permute-start | bytes 1671176 | tf_op jit(solution)/shard_map/ppermute | solution.py:32
  105.3 12.1 %collective-permute-done.11.left = bf16[1088,256]{1,0:T(8,128)(2,1)S(1)} collective-permute-done((bf16[1088,256]{1,0:T(8,128)(2,1)S(1)}, bf16[1088,256]{1,0:T(8,128)(2,1)S(1)}, u32[]{:S(2)}, u32[]{:S(2)}) %collective-permute-start.11) | collective-permute-done | bytes 557088 | tf_op jit(solution)/shard_map/ppermute | solution.py:32
  117.5 3.3 %collective-permute-start.13 = (bf16[576,256]{1,0:T(8,128)(2,1)S(1)}, bf16[576,256]{1,0:T(8,128)(2,1)S(1)}, u32[]{:S(2)}, u32[]{:S(2)}) collective-permute-start(bf16[576,256]{1,0:T(8,128)(2,1)S(1)} %add_convert_fusion), channel_id=1, source_target_pairs={{0,6},{1,7},{2,0},{3,1},{4,2},{5,3},{6,4},{7,5},{8,14},{9,15},{10,... | collective-permute-start | bytes 884744 | tf_op jit(solution)/shard_map/ppermute | solution.py:32
  120.9 0.1 collective-permute-start.12
  121.0 7.8 %collective-permute-done.12.att = bf16[512,256]{1,0:T(8,128)(2,1)S(1)} collective-permute-done((bf16[512,256]{1,0:T(8,128)(2,1)S(1)}, bf16[512,256]{1,0:T(8,128)(2,1)S(1)}, u32[]{:S(2)}, u32[]{:S(2)}) %collective-permute-start.12) | collective-permute-done | bytes 262176 | tf_op jit(solution)/shard_map/ppermute | solution.py:32
  128.8 1.0 combine.1
  129.8 0.4 all-to-all-done.2
  130.2 1.2 owner_sum.1
  (31 shorter events, 0.5 us)
Async XLA Ops:
  0.6 22.0 %collective-permute-start.4 = (bf16[256,512]{1,0:T(8,128)(2,1)}, bf16[256,512]{1,0:T(8,128)(2,1)S(1)}, u32[]{:S(2)}, u32[]{:S(2)}) collective-permute-start(bf16[256,512]{1,0:T(8,128)(2,1)} %bitcast.20), channel_id=1, source_target_pairs={{0,6},{1,7},{2,0},{3,1},{4,2},{5,3},{6,4},{7,5},{8,14},{9,15},{10,... | collective-permute-start | bytes 786440 | tf_op jit(solution)/shard_map/ppermute | solution.py:32
  3.5 25.3 %collective-permute-start.3 = (bf16[256,512]{1,0:T(8,128)(2,1)}, bf16[256,512]{1,0:T(8,128)(2,1)S(1)}, u32[]{:S(2)}, u32[]{:S(2)}) collective-permute-start(bf16[256,512]{1,0:T(8,128)(2,1)} %bitcast.21), channel_id=1, source_target_pairs={{0,2},{1,3},{2,4},{3,5},{4,6},{5,7},{6,0},{7,1},{8,10},{9,11},{10,... | collective-permute-start | bytes 786440 | tf_op jit(solution)/shard_map/ppermute | solution.py:32
  3.5 25.3 %collective-permute-start.2 = (bf16[256,576]{1,0:T(8,128)(2,1)}, bf16[256,576]{1,0:T(8,128)(2,1)S(1)}, u32[]{:S(2)}, u32[]{:S(2)}) collective-permute-start(bf16[256,576]{1,0:T(8,128)(2,1)} %bitcast.16), channel_id=1, source_target_pairs={{0,6},{1,7},{2,0},{3,1},{4,2},{5,3},{6,4},{7,5},{8,14},{9,15},{10,... | collective-permute-start | bytes 884744 | tf_op jit(solution)/shard_map/ppermute | solution.py:32
  6.7 19.2 %collective-permute-start = (bf16[256,576]{1,0:T(8,128)(2,1)}, bf16[256,576]{1,0:T(8,128)(2,1)S(1)}, u32[]{:S(2)}, u32[]{:S(2)}) collective-permute-start(bf16[256,576]{1,0:T(8,128)(2,1)} %bitcast.17), channel_id=1, source_target_pairs={{0,2},{1,3},{2,4},{3,5},{4,6},{5,7},{6,0},{7,1},{8,10},{9,11},{10,... | collective-permute-start | bytes 884744 | tf_op jit(solution)/shard_map/ppermute | solution.py:32
  8.5 20.2 %all-to-all-start = ((s32[32,1,32]{2,1,0:T(1,128)}), s32[32,1,32]{2,1,0:T(1,128)S(1)}, u32[]{:S(2)}, u32[]{:S(2)}) async-start(s32[32,1,32]{2,1,0:T(1,128)} %reshape.174), calls=%async_computation | async-start | bytes 32768 | tf_op jit(solution)/shard_map/all_to_all | solution.py:228
  22.6 7.2 %collective-permute-start.5 = (bf16[256,512]{1,0:T(8,128)(2,1)S(1)}, bf16[256,512]{1,0:T(8,128)(2,1)S(1)}, u32[]{:S(2)}, u32[]{:S(2)}) collective-permute-start(bf16[256,512]{1,0:T(8,128)(2,1)S(1)} %collective-permute-done.4.refs_5_.refs_7_.refs_11_), channel_id=1, source_target_pairs={{0,6},{1,7},{2,0},{3,1},{4,2},{5,3},{6,4},{7,5},{8,14},{9,15},{10,... | collective-permute-start | bytes 786440 | tf_op jit(solution)/shard_map/ppermute | solution.py:32
  25.9 8.7 %collective-permute-start.1 = (bf16[256,576]{1,0:T(8,128)(2,1)S(1)}, bf16[256,576]{1,0:T(8,128)(2,1)S(1)}, u32[]{:S(2)}, u32[]{:S(2)}) collective-permute-start(bf16[256,576]{1,0:T(8,128)(2,1)S(1)} %collective-permute-done.refs_0_.refs_1_.refs_5_), channel_id=1, source_target_pairs={{0,2},{1,3},{2,4},{3,5},{4,6},{5,7},{6,0},{7,1},{8,10},{9,11},{10,... | collective-permute-start | bytes 884744 | tf_op jit(solution)/shard_map/ppermute | solution.py:32
  34.8 1.8 %copy-start = (bf16[32,64,576]{2,1,0:T(8,128)(2,1)S(1)}, bf16[32,64,576]{2,1,0:T(8,128)(2,1)}, u32[]{:S(2)}) copy-start(bf16[32,64,576]{2,1,0:T(8,128)(2,1)} %rows_ref.1) | copy-start | bytes 7077892
  38.4 36.1 %copy-start.1 = (bf16[16,16,576]{2,1,0:T(8,128)(2,1)S(1)}, bf16[16,16,576]{2,1,0:T(8,128)(2,1)}, u32[]{:S(2)}) copy-start(bf16[16,16,576]{2,1,0:T(8,128)(2,1)} %param.5) | copy-start | bytes 884740
  38.4 36.1 %copy-start.2 = (bf16[16,16,512]{2,1,0:T(8,128)(2,1)S(1)}, bf16[16,16,512]{2,1,0:T(8,128)(2,1)}, u32[]{:S(2)}) copy-start(bf16[16,16,512]{2,1,0:T(8,128)(2,1)} %param.7) | copy-start | bytes 786436
  71.9 2.6 %collective-permute-start.6 = (bf16[32,24,576]{2,1,0:T(8,128)(2,1)S(1)}, bf16[32,24,576]{2,1,0:T(8,128)(2,1)S(1)}, u32[]{:S(2)}, u32[]{:S(2)}) collective-permute-start(bf16[32,24,576]{2,1,0:T(8,128)(2,1)S(1)} %all_to_all.15), channel_id=1, source_target_pairs={{0,1},{1,0},{2,3},{3,2},{4,5},{5,4},{6,7},{7,6},{8,9},{9,8},{10,11... | collective-permute-start | bytes 2654216 | tf_op jit(solution)/shard_map/ppermute | solution.py:280
  79.3 4.0 %collective-permute-start.9 = (f32[4,8,256]{2,1,0:T(8,128)S(1)}, f32[4,8,256]{2,1,0:T(8,128)S(1)}, u32[]{:S(2)}, u32[]{:S(2)}) collective-permute-start(f32[4,8,256]{2,1,0:T(8,128)S(1)} %get-tuple-element.22.refs_0_), channel_id=1, source_target_pairs={{0,6},{1,7},{2,0},{3,1},{4,2},{5,3},{6,4},{7,5},{8,14},{9,15},{10,... | collective-permute-start | bytes 98312 | tf_op jit(solution)/shard_map/ppermute | solution.py:32
  79.4 5.6 %collective-permute-start.8 = (f32[4,8,256]{2,1,0:T(8,128)S(1)}, f32[4,8,256]{2,1,0:T(8,128)S(1)}, u32[]{:S(2)}, u32[]{:S(2)}) collective-permute-start(f32[4,8,256]{2,1,0:T(8,128)S(1)} %get-tuple-element.22.refs_0_), channel_id=1, source_target_pairs={{0,4},{1,5},{2,6},{3,7},{4,0},{5,1},{6,2},{7,3},{8,12},{9,13},{10,... | collective-permute-start | bytes 98312 | tf_op jit(solution)/shard_map/ppermute | solution.py:32
  80.8 5.2 %collective-permute-start.7 = (f32[4,8,256]{2,1,0:T(8,128)S(1)}, f32[4,8,256]{2,1,0:T(8,128)S(1)}, u32[]{:S(2)}, u32[]{:S(2)}) collective-permute-start(f32[4,8,256]{2,1,0:T(8,128)S(1)} %get-tuple-element.22.refs_0_), channel_id=1, source_target_pairs={{0,2},{1,3},{2,4},{3,5},{4,6},{5,7},{6,0},{7,1},{8,10},{9,11},{10,... | collective-permute-start | bytes 98312 | tf_op jit(solution)/shard_map/ppermute | solution.py:32
  93.1 0.8 copy-start.3
  93.9 2.6 %collective-permute-start.14 = (bf16[32,24,576]{2,1,0:T(8,128)(2,1)S(1)}, bf16[32,24,576]{2,1,0:T(8,128)(2,1)S(1)}, u32[]{:S(2)}, u32[]{:S(2)}) collective-permute-start(bf16[32,24,576]{2,1,0:T(8,128)(2,1)S(1)} %bitcast.27), channel_id=1, source_target_pairs={{0,1},{1,0},{2,3},{3,2},{4,5},{5,4},{6,7},{7,6},{8,9},{9,8},{10,11... | collective-permute-start | bytes 2654216 | tf_op jit(solution)/shard_map/ppermute | solution.py:318
  96.4 6.8 %copy-start.4 = (bf16[1088,256]{1,0:T(8,128)(2,1)S(1)}, bf16[1088,256]{1,0:T(8,128)(2,1)}, u32[]{:S(2)}) copy-start(bf16[1088,256]{1,0:T(8,128)(2,1)} %copy-done.3) | copy-start | bytes 1671172
  97.7 32.5 %all-to-all-start.2 = ((bf16[32,24,576]{2,1,0:T(8,128)(2,1)}), bf16[32,24,576]{2,1,0:T(8,128)(2,1)S(1)}, u32[]{:S(2)}, u32[]{:S(2)}) async-start(bf16[32,24,576]{2,1,0:T(8,128)(2,1)} %fusion.1), calls=%async_computation.2 | async-start | bytes 1966080 | tf_op jit(solution)/shard_map/all_to_all | solution.py:320
  103.2 14.2 %collective-permute-start.11 = (bf16[1088,256]{1,0:T(8,128)(2,1)S(1)}, bf16[1088,256]{1,0:T(8,128)(2,1)S(1)}, u32[]{:S(2)}, u32[]{:S(2)}) collective-permute-start(bf16[1088,256]{1,0:T(8,128)(2,1)S(1)} %copy-done.4), channel_id=1, source_target_pairs={{0,6},{1,7},{2,0},{3,1},{4,2},{5,3},{6,4},{7,5},{8,14},{9,15},{10,... | collective-permute-start | bytes 1671176 | tf_op jit(solution)/shard_map/ppermute | solution.py:32
  105.3 15.5 %collective-permute-start.10 = (bf16[1088,256]{1,0:T(8,128)(2,1)}, bf16[1088,256]{1,0:T(8,128)(2,1)S(1)}, u32[]{:S(2)}, u32[]{:S(2)}) collective-permute-start(bf16[1088,256]{1,0:T(8,128)(2,1)} %get-tuple-element.24), channel_id=1, source_target_pairs={{0,2},{1,3},{2,4},{3,5},{4,6},{5,7},{6,0},{7,1},{8,10},{9,11},{10,... | collective-permute-start | bytes 1671176 | tf_op jit(solution)/shard_map/ppermute | solution.py:32
  117.5 11.3 %collective-permute-start.13 = (bf16[576,256]{1,0:T(8,128)(2,1)S(1)}, bf16[576,256]{1,0:T(8,128)(2,1)S(1)}, u32[]{:S(2)}, u32[]{:S(2)}) collective-permute-start(bf16[576,256]{1,0:T(8,128)(2,1)S(1)} %add_convert_fusion), channel_id=1, source_target_pairs={{0,6},{1,7},{2,0},{3,1},{4,2},{5,3},{6,4},{7,5},{8,14},{9,15},{10,... | collective-permute-start | bytes 884744 | tf_op jit(solution)/shard_map/ppermute | solution.py:32
  120.9 7.9 %collective-permute-start.12 = (bf16[512,256]{1,0:T(8,128)(2,1)S(1)}, bf16[512,256]{1,0:T(8,128)(2,1)S(1)}, u32[]{:S(2)}, u32[]{:S(2)}) collective-permute-start(bf16[512,256]{1,0:T(8,128)(2,1)S(1)} %add_convert_fusion.1), channel_id=1, source_target_pairs={{0,2},{1,3},{2,4},{3,5},{4,6},{5,7},{6,0},{7,1},{8,10},{9,11},{10,... | collective-permute-start | bytes 786440 | tf_op jit(solution)/shard_map/ppermute | solution.py:32

commit v3 on v2

v3 whole, which is shorter than its diff:
```python
import functools
import math

import jax
import jax.numpy as jnp
from jax import lax
from jax.experimental import pallas as pl
from jax.experimental.pallas import tpu as pltpu
from jax.sharding import PartitionSpec as P

USED = 64
XN = 4
CORES = 2

score_scale = 192.0 ** (-0.5)
log2e = 1.0 / math.log(2.0)
VMEM_LIMIT = 24 * 1024 * 1024
bf16 = jnp.bfloat16
f32 = jnp.float32


def x_shift(k):
    return [
        (x * CORES + c, ((x + k) % XN) * CORES + c) for x in range(XN) for c in range(CORES)
    ]


CORE_SWAP = [(t, t ^ 1) for t in range(XN * CORES)]


def send_x(value, k):
    return lax.ppermute(value, "tp", x_shift(k % XN))


def nt_dot(a, b):
    return lax.dot_general(a, b, (((1,), (1,)), ((), ())), preferred_element_type=f32)


def expand(rows, tokens):
    count, lanes = rows.shape
    wide = jnp.broadcast_to(rows[:, None, :], (count, tokens, lanes))
    return wide.reshape(count * tokens, lanes)


def iotas(shape):
    return (lax.broadcasted_iota(jnp.int32, shape, 0), lax.broadcasted_iota(jnp.int32, shape, 1))


def bit_matrix(mask):
    return jnp.where(mask, 1.0, 0.0).astype(bf16)


def dot32(a, b):
    return jnp.dot(a, b, preferred_element_type=f32)


def pack_kernel(tokens, slot_limit, asked_ref, cache_ref, q_ref, g_ref, *refs):
    out_ref, hot_out, q_out, g_out, rows_ref, hot_ref, sems = refs[-7:]
    owners, _, block_count = asked_ref.shape
    pair = CORES * tokens
    tp = lax.axis_index("tp")
    first = pl.multiple_of(tp // CORES * pair, pair)
    copies = [
        pltpu.make_async_copy(cache_ref.at[:, pl.ds(first, pair), :], rows_ref, sems.at[0]),
        pltpu.make_async_copy(q_ref, q_out, sems.at[1]),
        pltpu.make_async_copy(g_ref, g_out, sems.at[2]),
    ]
    for copy in copies:
        copy.start()
    wanted = asked_ref[:, 0, :].astype(f32)
    row, lane = iotas((block_count, block_count))
    rank = dot32(wanted.astype(bf16), bit_matrix(row < lane))
    row, lane = iotas((owners * slot_limit, owners))
    slot = jnp.zeros((owners * slot_limit, block_count), f32)
    for j in range(slot_limit):
        level = jnp.where(rank == j, wanted, 0.0).astype(bf16)
        slot += dot32(bit_matrix(row == lane * slot_limit + j), level)
    slot = slot.astype(bf16)

    def hot_matrix(size, offset):
        row, lane = iotas((block_count, block_count * size))
        start = row * size
        hot = expand(dot32(slot, bit_matrix((lane >= start) & (lane < start + size))), tokens)
        row, lane = iotas(hot.shape)
        same = (row & (tokens - 1)) + offset == (lane & (size - 1))
        return jnp.where(same, hot, 0.0).astype(bf16)

    hot_ref[...] = hot_matrix(tokens, 0)
    copies.append(pltpu.make_async_copy(hot_ref, hot_out, sems.at[3]))
    copies[3].start()
    hot = hot_matrix(pair, tp % CORES * tokens)
    copies[0].wait()
    rows = rows_ref[...].reshape(block_count * pair, rows_ref.shape[2])
    out_ref[...] = dot32(hot, rows).astype(bf16)
    for copy in copies[1:]:
        copy.wait()


def owner_kernel(hot_ref, rows_ref, out_ref):
    total = lax.dot_general(
        hot_ref[...], rows_ref[...], (((0,), (0,)), ((), ())), preferred_element_type=f32
    )
    out_ref[...] = total.astype(bf16)


def slot_hot(ids_ref, tokens, lanes):
    ids = expand(jnp.broadcast_to(ids_ref[:, 0:1], (ids_ref.shape[0], lanes)), tokens)
    row, lane = iotas(ids.shape)
    return bit_matrix(ids * tokens + (row & (tokens - 1)) == lane)


def unpack_kernel(tokens, pick_ref, rows_ref, *refs):
    hot = slot_hot(pick_ref, tokens, rows_ref.shape[0])
    refs[-1][...] = dot32(hot, rows_ref[...]).astype(bf16)


def score_half(tokens, lim_ref, key_ref, q_refs, g_refs, p_ref, gw_ref):
    rows = p_ref.shape[2]
    query_count = lim_ref.shape[1]
    heads = rows // query_count
    value_width = g_refs[0].shape[1]
    row, lane = iotas((query_count, rows))
    start = row * heads
    repeat = bit_matrix((lane >= start) & (lane < start + heads))
    limit = expand(dot32(lim_ref[...].astype(bf16), repeat), tokens)
    token = (iotas(limit.shape)[0] & (tokens - 1)).astype(f32)
    bias = jnp.where(token <= limit, 0.0, -jnp.inf)
    for k in range(XN):
        scores = nt_dot(key_ref[...], q_refs[k][...]) * (score_scale * log2e) + bias
        peak = jnp.max(scores, axis=0, keepdims=True)
        p = jnp.exp2(scores - peak)
        gw = nt_dot(key_ref[:, :value_width], g_refs[k][...])
        p_ref[k] = p.astype(bf16)
        gw_ref[k] = gw
        total = jnp.sum(p, axis=0, keepdims=True)
        yield k, peak, total, jnp.sum(p * gw, axis=0, keepdims=True)


def own_score_kernel(tokens, lim_ref, key_ref, *refs):
    q_refs, g_refs = refs[:XN], refs[XN : 2 * XN]
    p_ref, gw_ref, stat_ref = refs[2 * XN :]
    for k, peak, total, inner in score_half(
        tokens, lim_ref, key_ref, q_refs, g_refs, p_ref, gw_ref
    ):
        pad = jnp.zeros((5, peak.shape[1]), f32)
        stat_ref[k] = jnp.concatenate([peak, total, inner, pad])


def other_score_kernel(tokens, lim_ref, key_ref, *refs):
    q_refs, g_refs, own_ref = refs[:XN], refs[XN : 2 * XN], refs[2 * XN]
    p_ref, gw_ref, stat_ref = refs[2 * XN + 1 :]
    for k, peak, total, inner in score_half(
        tokens, lim_ref, key_ref, q_refs, g_refs, p_ref, gw_ref
    ):
        own = own_ref[k]
        top = jnp.maximum(peak, own[0:1])
        f_own, f_other = jnp.exp2(own[0:1] - top), jnp.exp2(peak - top)
        total = own[1:2] * f_own + total * f_other
        inner = own[2:3] * f_own + inner * f_other
        pad = jnp.zeros((3, peak.shape[1]), f32)
        stat_ref[k] = jnp.concatenate([top, total, inner, f_own, f_other, pad])


def local_kernel(*refs):
    key_refs, p_refs, gw_refs = refs[:CORES], refs[CORES : 2 * CORES], refs[2 * CORES : 3 * CORES]
    stat_ref, value_ref, grad_ref = refs[3 * CORES :]
    keys_t = [key_ref[...].T for key_ref in key_refs]
    for k in range(XN):
        stats = stat_ref[k]
        inner = stats[2:3] / stats[1:2]
        value, grad = [], []
        for h in range(CORES):
            p = p_refs[h][k].astype(f32) * stats[3 + h : 4 + h]
            value.append(dot32(keys_t[h], p.astype(bf16)))
            grad.append(dot32(keys_t[h], (p * (gw_refs[h][k] - inner)).astype(bf16)))
        value_ref[k] = value[0] + value[1]
        grad_ref[k] = grad[0] + grad[1]


def row_stats(stat_refs, k):
    stats = [stat_refs[j][(k - j) % XN] for j in range(XN)]
    peak = functools.reduce(jnp.maximum, [s[0:1] for s in stats])
    factors = [jnp.exp2(s[0:1] - peak) for s in stats]
    total = sum(s[1:2] * f for s, f in zip(stats, factors))
    inner = sum(s[2:3] * f for s, f in zip(stats, factors)) / total
    return stats[0], inner, factors[0] / total


def key_grad_kernel(tokens, half, order_ref, p_ref, gw_ref, *refs):
    stat_refs, q_refs, g_refs = refs[:XN], refs[XN : 2 * XN], refs[2 * XN : 3 * XN]
    out_ref, sum_ref = refs[-2:]
    value_width = g_refs[0].shape[1]
    key_grad, value_grad = [], []
    for k in range(XN):
        mine, inner, factor = row_stats(stat_refs, k)
        weights = p_ref[k].astype(f32) * (factor * mine[3 + half : 4 + half])
        ds = (weights * (gw_ref[k] - inner) * score_scale).astype(bf16)
        key_grad.append(dot32(ds, q_refs[k][...]))
        value_grad.append(dot32(weights.astype(bf16), g_refs[k][...]))
    key_grad, value_grad = sum(key_grad), sum(value_grad)
    sum_ref[:, :value_width] = (key_grad[:, :value_width] + value_grad).astype(bf16)
    sum_ref[:, value_width:] = key_grad[:, value_width:].astype(bf16)
    hot = slot_hot(order_ref, tokens, sum_ref.shape[0])
    out_ref[...] = dot32(hot, sum_ref[...]).astype(bf16)


def own_grad_kernel(tokens, *refs):
    value_ref, grad_ref = refs[:2]
    stat_refs = refs[5 : 5 + XN]
    outs, sum_ref, sems = refs[-12:-7], refs[-7], refs[-1]
    here_ref, right_ref, left_ref, att3_ref, qg1_ref = refs[-6:-1]
    value_width = att3_ref.shape[0]
    att_out = (
        here_ref.at[:value_width],
        left_ref.at[:value_width],
        right_ref.at[:value_width],
        att3_ref,
    )
    qg_out = (
        here_ref.at[value_width:],
        qg1_ref,
        left_ref.at[value_width:],
        right_ref.at[value_width:],
    )
    for k in range(XN):
        mine, inner, factor = row_stats(stat_refs, k)
        shift = mine[2:3] / mine[1:2] - inner
        att_out[k][...] = (value_ref[k, :value_width] * factor).astype(bf16)
        qg = (grad_ref[k] + value_ref[k] * shift) * (factor * score_scale)
        qg_out[k][...] = qg.astype(bf16)
    copies = [
        pltpu.make_async_copy(src, dst, sems.at[i])
        for i, (src, dst) in enumerate(zip(refs[-6:-1], outs))
    ]
    for copy in copies:
        copy.start()
    key_grad_kernel(tokens, 0, *refs[2:-12], sum_ref)
    for copy in copies:
        copy.wait()


def combine_kernel(here, right, left, att, qg, att_ref, qg_ref):
    value_width = att_ref.shape[1]
    total = here[:value_width].astype(f32) + left[:value_width].astype(f32) + att[...].astype(f32)
    att_ref[...] = total.astype(bf16).T
    total = here[value_width:].astype(f32) + right[value_width:].astype(f32) + qg[...].astype(f32)
    qg_ref[...] = total.astype(bf16).T


def shaped(shape, dtype=bf16):
    return jax.ShapeDtypeStruct(shape, dtype)


def call(kernel, out_shape, operands, name, unused=(), scratch=(), far_in=0, far_out=()):
    vmem, hbm = (pl.BlockSpec(memory_space=m) for m in (pltpu.VMEM, pltpu.HBM))
    near = len(operands) - far_in
    operands = operands[:near] + [
        pltpu.with_memory_space_constraint(x, pltpu.HBM) for x in operands[near:]
    ]
    return pl.pallas_call(
        kernel,
        out_shape=[
            pltpu.HBM(x.shape, x.dtype) if i in far_out else x for i, x in enumerate(out_shape)
        ],
        in_specs=[vmem] * near
        + [hbm] * far_in
        + [pl.BlockSpec(memory_space=pl.ANY)] * len(unused),
        out_specs=[hbm if i in far_out else vmem for i in range(len(out_shape))],
        scratch_shapes=list(scratch),
        compiler_params=pltpu.CompilerParams(vmem_limit_bytes=VMEM_LIMIT),
        name=name,
    )(*operands, *unused)


def slot_table(wanted, slot_limit):
    rank_within = jnp.cumsum(wanted.astype(jnp.int32), axis=1) - 1
    local_ids = jnp.arange(wanted.shape[1], dtype=jnp.int32)
    slot_range = jnp.arange(slot_limit, dtype=jnp.int32)
    matches = wanted[:, None, :] & (rank_within[:, None, :] == slot_range[None, :, None])
    present = jnp.any(matches, axis=2)
    found_ids = jnp.sum(jnp.where(matches, local_ids[None, None, :], 0), axis=2)
    return jnp.where(present, found_ids, -1).reshape(-1)


def on_device(queries, latent_cache, output_gradient, selected, positions):
    query_count, head_count, width = queries.shape
    block_count, block_size, _ = latent_cache.shape
    value_width = output_gradient.shape[2]
    owners = lax.axis_size("ctx")
    tp = lax.axis_index("tp")
    tokens = block_size // (XN * CORES)
    slot_limit = (USED - 2) // (owners - 1) + 1
    slots = owners * slot_limit
    rows = query_count * head_count
    half = USED * tokens
    keys = CORES * half
    held = block_count * tokens
    parcels = (owners, slot_limit * tokens, width)

    block_range = jnp.arange(owners * block_count, dtype=jnp.int32)
    wanted = jnp.any(selected.reshape(-1)[:, None] == block_range[None, :], axis=0)
    wanted = wanted.reshape(owners, block_count)
    asked = lax.all_to_all(
        wanted.astype(jnp.int32)[:, None, :], "ctx", split_axis=0, concat_axis=0, tiled=True
    )

    query_rows = queries.reshape(rows, width)
    grad_rows = output_gradient.reshape(rows, value_width)
    requests = slot_table(wanted, slot_limit)
    used_slot = requests >= 0
    slot_order = jnp.where(used_slot, jnp.cumsum(used_slot.astype(jnp.int32)) - 1, -1)
    compact = jnp.arange(USED, dtype=jnp.int32)
    slot_match = slot_order[None, :] == compact[:, None]
    slot_ids = jnp.arange(slots, dtype=jnp.int32)
    slot_block = slot_ids // slot_limit * block_count + requests
    picked = jnp.sum(jnp.where(slot_match, slot_ids[None, :], 0), axis=1)
    block_ids = jnp.sum(jnp.where(slot_match, slot_block[None, :], 0), axis=1)
    chosen = jnp.any(selected[None, :, :] == block_ids[:, None, None], axis=2)
    limit = jnp.where(chosen, positions[None, :] - block_ids[:, None] * block_size, -1)
    limit = jnp.clip(limit, -1, block_size - 1)
    own_limit = (limit - tp * tokens).astype(f32)
    other_limit = (limit - (tp ^ 1) * tokens).astype(f32)
    pick = jnp.broadcast_to(picked[:, None], (USED, 128))
    order = jnp.broadcast_to(slot_order[:, None], (slots, 128))

    early = (own_limit, other_limit, pick, order)
    packed, asked_hot, q0, g0 = call(
        functools.partial(pack_kernel, tokens, slot_limit),
        [
            shaped((slots * tokens, width)),
            shaped((slots * tokens, held)),
            shaped((rows, width)),
            shaped((rows, value_width)),
        ],
        [asked, latent_cache, query_rows, grad_rows],
        "pack",
        unused=early,
        scratch=[
            pltpu.VMEM((block_count, CORES * tokens, width), bf16),
            pltpu.VMEM((slots * tokens, held), bf16),
            pltpu.SemaphoreType.DMA((4,)),
        ],
        far_in=3,
        far_out=(1,),
    )
    fetched = lax.all_to_all(packed.reshape(parcels), "ctx", 0, 0, tiled=True)

    q1, q3 = send_x(q0, 1), send_x(q0, -1)
    g1, g3 = send_x(g0, 1), send_x(g0, -1)
    q2, g2 = send_x(q1, 1), send_x(g3, -1)
    gathered = [q0, q1, q2, q3, g0, g1, g2, g3]

    (own_keys,) = call(
        functools.partial(unpack_kernel, tokens),
        [shaped((half, width))],
        [pick, fetched.reshape(slots * tokens, width)],
        "unpack",
        unused=(q1, q2, q3, g1, g2, g3),
    )
    other_keys = lax.ppermute(own_keys.reshape(USED, tokens, width), "tp", CORE_SWAP)
    other_keys = other_keys.reshape(half, width)
    score_shapes = [
        shaped((XN, half, rows)),
        shaped((XN, half, rows), f32),
        shaped((XN, 8, rows), f32),
    ]
    own_p, own_gw, own_stats = call(
        functools.partial(own_score_kernel, tokens),
        score_shapes,
        [own_limit, own_keys, *gathered],
        "own_scores",
    )
    other_p, other_gw, stats = call(
        functools.partial(other_score_kernel, tokens),
        score_shapes,
        [other_limit, other_keys, *gathered, own_stats],
        "other_scores",
    )
    all_stats = [stats] + [send_x(stats, k) for k in range(1, XN)]
    value_part, grad_part = call(
        local_kernel,
        [shaped((XN, width, rows), f32)] * 2,
        [own_keys, other_keys, own_p, other_p, own_gw, other_gw, stats],
        "local",
    )

    both = width + value_width
    sum_scratch = [pltpu.VMEM((half, width), bf16)]
    (other_grad,) = call(
        functools.partial(key_grad_kernel, tokens, 1),
        [shaped((slots * tokens, width))],
        [order, other_p, other_gw, *all_stats, *gathered],
        "other_grads",
        unused=(value_part,),
        scratch=sum_scratch,
    )
    from_core = lax.ppermute(other_grad.reshape(parcels), "tp", CORE_SWAP)
    own_grad, here, right, left, att3, qg1 = call(
        functools.partial(own_grad_kernel, tokens),
        [shaped((slots * tokens, width))]
        + [shaped((n, rows)) for n in (both, both, both, value_width, width)],
        [value_part, grad_part, order, own_p, own_gw, *all_stats, *gathered],
        "own_grads",
        scratch=sum_scratch
        + [pltpu.VMEM((n, rows), bf16) for n in (both, both, both, value_width, width)]
        + [pltpu.SemaphoreType.DMA((5,))],
        far_out=(1, 2, 3, 4, 5),
    )
    returning = (own_grad.reshape(parcels).astype(f32) + from_core.astype(f32)).astype(bf16)
    returned = lax.all_to_all(returning, "ctx", 0, 0, tiled=True)

    right, left = send_x(right, 1), send_x(left, -1)
    att = (att3.astype(f32) + right[:value_width].astype(f32)).astype(bf16)
    qg = (qg1.astype(f32) + left[value_width:].astype(f32)).astype(bf16)
    attended, query_grad = call(
        combine_kernel,
        [shaped((rows, value_width)), shaped((rows, width))],
        [here, right, left, send_x(att, 1), send_x(qg, -1)],
        "combine",
    )
    (cache_grad,) = call(
        owner_kernel,
        [shaped((held, width))],
        [asked_hot, returned.reshape(slots * tokens, width)],
        "owner_sum",
    )
    return (
        attended.reshape(query_count, head_count, value_width),
        query_grad.reshape(query_count, head_count, width),
        cache_grad.reshape(block_count, tokens, width),
    )


def solution(mesh):
    in_specs = (
        P("ctx", "tp", None),
        P("ctx", None, None),
        P("ctx", "tp", None),
        P("ctx", None),
        P("ctx"),
    )
    out_specs = (P("ctx", "tp", None), P("ctx", "tp", None), P("ctx", "tp", None))
    return jax.shard_map(
        on_device, mesh=mesh, in_specs=in_specs, out_specs=out_specs, check_vma=False
    )
```

time: 132 us -> 114 us (0.86)
  blocking collectives: 33.5 us -> 0 us
  starting transfers between devices: 34.3 us -> 44.6 us
  waiting for transfers between devices: 37.9 us -> 42.1 us
  Pallas kernels: 16 us -> 19.3 us
  local copies, waits for them, and re-layouts: 4.72 us -> 2.19 us
    all_to_all x1 -> x0, blocking collectives: 33.5 us -> none  [on_device(): fetched = lax.all_to_all(packed.reshape(parcels), 'ctx', 0, 0, tiled=True)]
    all_to_all x0 -> x1, starting transfers between devices: none -> 5.04 us  [on_device(): fetched = lax.all_to_all(packed.reshape(parcels), 'ctx', 0, 0, tiled=True)]
    ppermute x13, starting transfers between devices: 17 us -> 21.6 us  [send_x(): return lax.ppermute(value, 'tp', x_shift(k % XN))]
    all_to_all x1, waiting for transfers between devices: 1.95 us -> 5.36 us  [on_device(): lax.all_to_all(wanted.astype(jnp.int32)[:, None, :], 'ctx', split_axis=0,...]
    pallas_call x5 -> x9, Pallas kernels: 16 us -> 19.3 us  [call(): pl.pallas_call(kernel, out_shape=[pltpu.HBM(x.shape, x.dtype) if i in far...]
    ppermute x13, waiting for transfers between devices: 30.4 us -> 33.6 us  [send_x(): return lax.ppermute(value, 'tp', x_shift(k % XN))]
    all_to_all x0 -> x1, waiting for transfers between devices: none -> 2.9 us  [on_device(): fetched = lax.all_to_all(packed.reshape(parcels), 'ctx', 0, 0, tiled=True)]
    ppermute x1, waiting for transfers between devices: 2.56 us -> 0.01 us  [on_device(): from_core = lax.ppermute(other_grad.reshape(parcels), 'tp', CORE_SWAP)]
  transfers between devices with their start and end apart: 17 -> 18, of which waited for: 11 -> 7; matrix products, arithmetic and copies ran while one was open for 4% -> 3% of each run, Pallas kernels for 1% -> 9%
where the time goes in v3:
time: 114 us; the launch traced here: 113 us
  starting transfers between devices  44.6 us (39%)
  waiting for transfers between devices  42.1 us (37%)
  Pallas kernels  19.3 us (17%)
  other arithmetic  4.17 us (4%)
  local copies, waits for them, and re-layouts  2.19 us (2%)
    ppermute x13, waiting for transfers between devices, send_x(): return lax.ppermute(value, 'tp', x_shift(k % XN))  33.6 us
    ppermute x13, starting transfers between devices, send_x(): return lax.ppermute(value, 'tp', x_shift(k % XN))  21.6 us
    pallas_call x9, Pallas kernels, call(): pl.pallas_call(kernel, out_shape=[pltpu.HBM(x.shape, x.dtype) if i in far...  19.3 us
    all_to_all x1, starting transfers between devices, on_device(): lax.all_to_all(wanted.astype(jnp.int32)[:, None, :], 'ctx', split_axis=0,...  11.7 us
    all_to_all x1, starting transfers between devices, on_device(): returned = lax.all_to_all(returning, 'ctx', 0, 0, tiled=True)  5.71 us
    all_to_all x1, waiting for transfers between devices, on_device(): lax.all_to_all(wanted.astype(jnp.int32)[:, None, :], 'ctx', split_axis=0,...  5.36 us
    all_to_all x1, starting transfers between devices, on_device(): fetched = lax.all_to_all(packed.reshape(parcels), 'ctx', 0, 0, tiled=True)  5.04 us
    all_to_all x1, waiting for transfers between devices, on_device(): fetched = lax.all_to_all(packed.reshape(parcels), 'ctx', 0, 0, tiled=True)  2.9 us
  transfers between devices with their start and end apart: 18, of which 7 were waited for; matrix products, arithmetic and copies ran while one was open for 3% of the time, Pallas kernels for 9%

profile of v3, /device:TPU:8, one launch (start us, length us, event | category | flops | bytes accessed | tf_op | source)
XLA Modules:
  0.0 113.2 jit_solution(1171910899774276449)
XLA Ops:
  0.6 0.8 eq.26
  1.4 0.4 fusion
  1.8 0.7 reshape.178
  2.5 11.7 %all-to-all-start = ((s32[32,1,32]{2,1,0:T(1,128)}), s32[32,1,32]{2,1,0:T(1,128)S(1)}, u32[]{:S(2)}, u32[]{:S(2)}) async-start(s32[32,1,32]{2,1,0:T(1,128)} %reshape.178), calls=%async_computation | async-start | bytes 32768 | tf_op jit(solution)/shard_map/all_to_all | solution.py:303
  14.3 0.2 reduce_window_sum.18
  14.5 0.2 select_reduce_fusion
  14.6 0.2 fusion.3
  14.8 0.1 copy.11
  15.0 0.1 reduce-window.7
  15.1 0.1 add_reduce_fusion
  15.2 0.1 copy.10
  15.3 0.1 select_n.64
  15.4 0.1 select_reduce_fusion.1
  15.5 0.9 compare_reduce_fusion
  16.4 0.1 copy.13
  16.5 0.7 subtract_convert_fusion
  17.3 5.4 %all-to-all-done.asked_ref = s32[32,1,32]{2,1,0:T(1,128)S(1)} async-done(((s32[32,1,32]{2,1,0:T(1,128)}), s32[32,1,32]{2,1,0:T(1,128)S(1)}, u32[]{:S(2)}, u32[]{:S(2)}) %all-to-all-start) | async-done | bytes 4128 | tf_op jit(solution)/shard_map/all_to_all | solution.py:303
  22.8 2.9 %pack.1 = (bf16[768,576]{1,0:T(8,128)(2,1)}, bf16[768,256]{1,0:T(8,128)(2,1)}, bf16[256,576]{1,0:T(8,128)(2,1)S(1)}, bf16[256,512]{1,0:T(8,128)(2,1)S(1)}) custom-call(s32[32,1,32]{2,1,0:T(1,128)S(1)} %all-to-all-done.asked_ref, bf16[32,64,576]{2,1,0:T(8,128)(2,1)} %cache_ref.1, bf16[256,576]{1,0:T(8,128)(2,1)} %bitcast.20, bf16[256,512]{1,0:T(8,128)(2,1)} %bitcast.22, ...), custom_call_target="tpu_custom_call" | custom-call | tf_op jit(solution)/shard_map/pack/pallas_call | solution.py:260
  25.7 5.0 %all-to-all-start.1 = ((bf16[32,24,576]{2,1,0:T(8,128)(2,1)}), bf16[32,24,576]{2,1,0:T(8,128)(2,1)S(1)}, u32[]{:S(2)}, u32[]{:S(2)}) async-start(bf16[32,24,576]{2,1,0:T(8,128)(2,1)} %bitcast.2), calls=%async_computation.1 | async-start | bytes 1966080 | tf_op jit(solution)/shard_map/all_to_all | solution.py:346
  30.7 1.6 %collective-permute-start = (bf16[256,576]{1,0:T(8,128)(2,1)S(1)}, bf16[256,576]{1,0:T(8,128)(2,1)S(1)}, u32[]{:S(2)}, u32[]{:S(2)}) collective-permute-start(bf16[256,576]{1,0:T(8,128)(2,1)S(1)} %get-tuple-element.24.refs_0_.refs_9_.refs_4_), channel_id=1, source_target_pairs={{0,2},{1,3},{2,4},{3,5},{4,6},{5,7},{6,0},{7,1},{8,10},{9,11},{10,... | collective-permute-start | bytes 884744 | tf_op jit(solution)/shard_map/ppermute | solution.py:32
  32.3 1.7 %collective-permute-start.4 = (bf16[256,512]{1,0:T(8,128)(2,1)S(1)}, bf16[256,512]{1,0:T(8,128)(2,1)S(1)}, u32[]{:S(2)}, u32[]{:S(2)}) collective-permute-start(bf16[256,512]{1,0:T(8,128)(2,1)S(1)} %get-tuple-element.25.refs_4_.refs_13_.refs_8_), channel_id=1, source_target_pairs={{0,6},{1,7},{2,0},{3,1},{4,2},{5,3},{6,4},{7,5},{8,14},{9,15},{10,... | collective-permute-start | bytes 786440 | tf_op jit(solution)/shard_map/ppermute | solution.py:32
  34.0 1.6 %collective-permute-start.2 = (bf16[256,576]{1,0:T(8,128)(2,1)S(1)}, bf16[256,576]{1,0:T(8,128)(2,1)S(1)}, u32[]{:S(2)}, u32[]{:S(2)}) collective-permute-start(bf16[256,576]{1,0:T(8,128)(2,1)S(1)} %get-tuple-element.24.refs_0_.refs_9_.refs_4_), channel_id=1, source_target_pairs={{0,6},{1,7},{2,0},{3,1},{4,2},{5,3},{6,4},{7,5},{8,14},{9,15},{10,... | collective-permute-start | bytes 884744 | tf_op jit(solution)/shard_map/ppermute | solution.py:32
  35.6 4.2 %collective-permute-done.refs_0_.refs_1_.refs_10_.refs_5_ = bf16[256,576]{1,0:T(8,128)(2,1)S(1)} collective-permute-done((bf16[256,576]{1,0:T(8,128)(2,1)S(1)}, bf16[256,576]{1,0:T(8,128)(2,1)S(1)}, u32[]{:S(2)}, u32[]{:S(2)}) %collective-permute-start) | collective-permute-done | bytes 294944 | tf_op jit(solution)/shard_map/ppermute | solution.py:32
  39.8 0.4 collective-permute-start.1
  40.2 1.5 %collective-permute-start.3 = (bf16[256,512]{1,0:T(8,128)(2,1)S(1)}, bf16[256,512]{1,0:T(8,128)(2,1)S(1)}, u32[]{:S(2)}, u32[]{:S(2)}) collective-permute-start(bf16[256,512]{1,0:T(8,128)(2,1)S(1)} %get-tuple-element.25.refs_4_.refs_13_.refs_8_), channel_id=1, source_target_pairs={{0,2},{1,3},{2,4},{3,5},{4,6},{5,7},{6,0},{7,1},{8,10},{9,11},{10,... | collective-permute-start | bytes 786440 | tf_op jit(solution)/shard_map/ppermute | solution.py:32
  41.7 2.8 %collective-permute-start.5 = (bf16[256,512]{1,0:T(8,128)(2,1)S(1)}, bf16[256,512]{1,0:T(8,128)(2,1)S(1)}, u32[]{:S(2)}, u32[]{:S(2)}) collective-permute-start(bf16[256,512]{1,0:T(8,128)(2,1)S(1)} %collective-permute-done.4.refs_5_.refs_7_.refs_16_.refs_11_), channel_id=1, source_target_pairs={{0,6},{1,7},{2,0},{3,1},{4,2},{5,3},{6,4},{7,5},{8,14},{9,15},{10,... | collective-permute-start | bytes 786440 | tf_op jit(solution)/shard_map/ppermute | solution.py:32
  44.5 8.9 %collective-permute-done.3.refs_3_.refs_5_.refs_14_.refs_9_ = bf16[256,512]{1,0:T(8,128)(2,1)S(1)} collective-permute-done((bf16[256,512]{1,0:T(8,128)(2,1)S(1)}, bf16[256,512]{1,0:T(8,128)(2,1)S(1)}, u32[]{:S(2)}, u32[]{:S(2)}) %collective-permute-start.3) | collective-permute-done | bytes 262176 | tf_op jit(solution)/shard_map/ppermute | solution.py:32
  53.4 2.9 %all-to-all-done.1 = bf16[32,24,576]{2,1,0:T(8,128)(2,1)S(1)} async-done(((bf16[32,24,576]{2,1,0:T(8,128)(2,1)}), bf16[32,24,576]{2,1,0:T(8,128)(2,1)S(1)}, u32[]{:S(2)}, u32[]{:S(2)}) %all-to-all-start.1) | async-done | bytes 884768 | tf_op jit(solution)/shard_map/all_to_all | solution.py:346
  56.3 0.9 unpack.1.key_ref.refs_0_
  57.2 0.3 collective-permute-start.6
  57.5 1.9 %own_scores.1 = (bf16[4,512,256]{2,1,0:T(8,128)(2,1)S(1)}, f32[4,512,256]{2,1,0:T(8,128)S(1)}, f32[4,8,256]{2,1,0:T(8,128)S(1)}) custom-call(f32[64,16]{1,0:T(8,128)S(1)} %get-tuple-element.48.refs_0_.lim_ref, bf16[512,576]{1,0:T(8,128)(2,1)S(1)} %unpack.1.key_ref.refs_0_, bf16[256,576]{1,0:T(8,128)(2,1)S(1)} %get-tuple-element.24.refs_0_.refs_9_.refs_4_, ...), custom_call_target="tpu_custom_call" | custom-call | tf_op jit(solution)/shard_map/own_scores/pallas_call | solution.py:260
  59.4 0.2 collective-permute-done.6
  59.6 1.9 %other_scores.1 = (bf16[4,512,256]{2,1,0:T(8,128)(2,1)S(1)}, f32[4,512,256]{2,1,0:T(8,128)S(1)}, f32[4,8,256]{2,1,0:T(8,128)S(1)}) custom-call(f32[64,16]{1,0:T(8,128)S(1)} %get-tuple-element.47.refs_1_.lim_ref, bf16[512,576]{1,0:T(8,128)(2,1)S(1)} %bitcast.16, bf16[256,576]{1,0:T(8,128)(2,1)S(1)} %get-tuple-element.24.refs_0_.refs_9_.refs_4_, ...), custom_call_target="tpu_custom_call" | custom-call | tf_op jit(solution)/shard_map/other_scores/pallas_call | solution.py:260
  61.5 1.6 %collective-permute-start.7 = (f32[4,8,256]{2,1,0:T(8,128)S(1)}, f32[4,8,256]{2,1,0:T(8,128)S(1)}, u32[]{:S(2)}, u32[]{:S(2)}) collective-permute-start(f32[4,8,256]{2,1,0:T(8,128)S(1)} %get-tuple-element.31.refs_6_.refs_5_.refs_0_), channel_id=1, source_target_pairs={{0,2},{1,3},{2,4},{3,5},{4,6},{5,7},{6,0},{7,1},{8,10},{9,11},{10,... | collective-permute-start | bytes 98312 | tf_op jit(solution)/shard_map/ppermute | solution.py:32
  63.1 2.7 %collective-permute-start.8 = (f32[4,8,256]{2,1,0:T(8,128)S(1)}, f32[4,8,256]{2,1,0:T(8,128)S(1)}, u32[]{:S(2)}, u32[]{:S(2)}) collective-permute-start(f32[4,8,256]{2,1,0:T(8,128)S(1)} %get-tuple-element.31.refs_6_.refs_5_.refs_0_), channel_id=1, source_target_pairs={{0,4},{1,5},{2,6},{3,7},{4,0},{5,1},{6,2},{7,3},{8,12},{9,13},{10,... | collective-permute-start | bytes 98312 | tf_op jit(solution)/shard_map/ppermute | solution.py:32
  65.8 1.4 %collective-permute-start.9 = (f32[4,8,256]{2,1,0:T(8,128)S(1)}, f32[4,8,256]{2,1,0:T(8,128)S(1)}, u32[]{:S(2)}, u32[]{:S(2)}) collective-permute-start(f32[4,8,256]{2,1,0:T(8,128)S(1)} %get-tuple-element.31.refs_6_.refs_5_.refs_0_), channel_id=1, source_target_pairs={{0,6},{1,7},{2,0},{3,1},{4,2},{5,3},{6,4},{7,5},{8,14},{9,15},{10,... | collective-permute-start | bytes 98312 | tf_op jit(solution)/shard_map/ppermute | solution.py:32
  67.2 2.6 %local.1 = (f32[4,576,256]{2,1,0:T(8,128)S(1)}, f32[4,576,256]{2,1,0:T(8,128)S(1)}) custom-call(bf16[512,576]{1,0:T(8,128)(2,1)S(1)} %unpack.1.key_ref.refs_0_, bf16[512,576]{1,0:T(8,128)(2,1)S(1)} %bitcast.17, bf16[4,512,256]{2,1,0:T(8,128)(2,1)S(1)} %get-tuple-element.26.refs_2_.refs_3_, bf16[4,512,256]{2,1,0:T(8,128)(2,1)S(1)} %get-tuple-element.28.refs_3_.p_ref, ...), custom_call_target="tpu_custom_call" | custom-call | tf_op jit(solution)/shard_map/local/pallas_call | solution.py:260
  69.9 2.6 %other_grads.1 = bf16[768,576]{1,0:T(8,128)(2,1)S(1)} custom-call(s32[96,128]{1,0:T(8,128)S(1)} %broadcast_in_dim.76.refs_3_.refs_2_.order_ref, bf16[4,512,256]{2,1,0:T(8,128)(2,1)S(1)} %get-tuple-element.28.refs_3_.p_ref, f32[4,512,256]{2,1,0:T(8,128)S(1)} %get-tuple-element.30.refs_5_.gw_ref, f32[4,8,256]{2,1,0:T(8,128)S(1)} %get-tuple-element.31.refs_6_.refs_5_.refs_0_, ...), custom_call_target="tpu_custom_call" | custom-call | tf_op jit(solution)/shard_map/other_grads/pallas_call | solution.py:260
  72.5 0.3 collective-permute-start.14
  72.9 4.2 %own_grads.1 = (bf16[768,576]{1,0:T(8,128)(2,1)S(1)}, bf16[1088,256]{1,0:T(8,128)(2,1)}, bf16[1088,256]{1,0:T(8,128)(2,1)}, bf16[1088,256]{1,0:T(8,128)(2,1)}, b...) custom-call(f32[4,576,256]{2,1,0:T(8,128)S(1)} %get-tuple-element.32.refs_0_.refs_12_, ...), custom_call_target="tpu_custom_call" | custom-call | tf_op jit(solution)/shard_map/own_grads/pallas_call | solution.py:260
  77.1 1.2 %fusion.1 = bf16[32,24,576]{2,1,0:T(8,128)(2,1)} fusion(bf16[32,24,576]{2,1,0:T(8,128)(2,1)S(1)} %bitcast.19, bf16[32,24,576]{2,1,0:T(8,128)(2,1)S(1)} %collective-permute-done.14), kind=kLoop, calls=%fused_computation.3 | loop fusion | flops 1769472 | bytes 2654208 | tf_op jit(solution)/shard_map/convert_element_type | solution.py:409
  78.3 5.7 %all-to-all-start.2 = ((bf16[32,24,576]{2,1,0:T(8,128)(2,1)}), bf16[32,24,576]{2,1,0:T(8,128)(2,1)S(1)}, u32[]{:S(2)}, u32[]{:S(2)}) async-start(bf16[32,24,576]{2,1,0:T(8,128)(2,1)} %fusion.1), calls=%async_computation.2 | async-start | bytes 1966080 | tf_op jit(solution)/shard_map/all_to_all | solution.py:410
  84.0 2.5 %collective-permute-start.11 = (bf16[1088,256]{1,0:T(8,128)(2,1)}, bf16[1088,256]{1,0:T(8,128)(2,1)S(1)}, u32[]{:S(2)}, u32[]{:S(2)}) collective-permute-start(bf16[1088,256]{1,0:T(8,128)(2,1)} %get-tuple-element.36), channel_id=1, source_target_pairs={{0,6},{1,7},{2,0},{3,1},{4,2},{5,3},{6,4},{7,5},{8,14},{9,15},{10,... | collective-permute-start | bytes 1671176 | tf_op jit(solution)/shard_map/ppermute | solution.py:32
  86.5 12.3 %collective-permute-done.11.left = bf16[1088,256]{1,0:T(8,128)(2,1)S(1)} collective-permute-done((bf16[1088,256]{1,0:T(8,128)(2,1)}, bf16[1088,256]{1,0:T(8,128)(2,1)S(1)}, u32[]{:S(2)}, u32[]{:S(2)}) %collective-permute-start.11) | collective-permute-done | bytes 557088 | tf_op jit(solution)/shard_map/ppermute | solution.py:32
  98.9 3.7 %collective-permute-start.13 = (bf16[576,256]{1,0:T(8,128)(2,1)S(1)}, bf16[576,256]{1,0:T(8,128)(2,1)S(1)}, u32[]{:S(2)}, u32[]{:S(2)}) collective-permute-start(bf16[576,256]{1,0:T(8,128)(2,1)S(1)} %add_convert_fusion), channel_id=1, source_target_pairs={{0,6},{1,7},{2,0},{3,1},{4,2},{5,3},{6,4},{7,5},{8,14},{9,15},{10,... | collective-permute-start | bytes 884744 | tf_op jit(solution)/shard_map/ppermute | solution.py:32
  102.7 8.2 %collective-permute-done.12.att = bf16[512,256]{1,0:T(8,128)(2,1)S(1)} collective-permute-done((bf16[512,256]{1,0:T(8,128)(2,1)S(1)}, bf16[512,256]{1,0:T(8,128)(2,1)S(1)}, u32[]{:S(2)}, u32[]{:S(2)}) %collective-permute-start.12) | collective-permute-done | bytes 262176 | tf_op jit(solution)/shard_map/ppermute | solution.py:32
  110.9 1.0 combine.1
  111.9 1.2 %owner_sum.1 = bf16[256,576]{1,0:T(8,128)(2,1)} custom-call(bf16[768,256]{1,0:T(8,128)(2,1)S(1)} %copy-done.1, bf16[768,576]{1,0:T(8,128)(2,1)S(1)} %bitcast.14), custom_call_target="tpu_custom_call" | custom-call | tf_op jit(solution)/shard_map/owner_sum/pallas_call | solution.py:260
  (35 shorter events, 0.6 us)
Async XLA Ops:
  2.5 20.2 %all-to-all-start = ((s32[32,1,32]{2,1,0:T(1,128)}), s32[32,1,32]{2,1,0:T(1,128)S(1)}, u32[]{:S(2)}, u32[]{:S(2)}) async-start(s32[32,1,32]{2,1,0:T(1,128)} %reshape.178), calls=%async_computation | async-start | bytes 32768 | tf_op jit(solution)/shard_map/all_to_all | solution.py:303
  25.7 30.6 %all-to-all-start.1 = ((bf16[32,24,576]{2,1,0:T(8,128)(2,1)}), bf16[32,24,576]{2,1,0:T(8,128)(2,1)S(1)}, u32[]{:S(2)}, u32[]{:S(2)}) async-start(bf16[32,24,576]{2,1,0:T(8,128)(2,1)} %bitcast.2), calls=%async_computation.1 | async-start | bytes 1966080 | tf_op jit(solution)/shard_map/all_to_all | solution.py:346
  30.7 9.0 %collective-permute-start = (bf16[256,576]{1,0:T(8,128)(2,1)S(1)}, bf16[256,576]{1,0:T(8,128)(2,1)S(1)}, u32[]{:S(2)}, u32[]{:S(2)}) collective-permute-start(bf16[256,576]{1,0:T(8,128)(2,1)S(1)} %get-tuple-element.24.refs_0_.refs_9_.refs_4_), channel_id=1, source_target_pairs={{0,2},{1,3},{2,4},{3,5},{4,6},{5,7},{6,0},{7,1},{8,10},{9,11},{10,... | collective-permute-start | bytes 884744 | tf_op jit(solution)/shard_map/ppermute | solution.py:32
  32.3 9.4 %collective-permute-start.4 = (bf16[256,512]{1,0:T(8,128)(2,1)S(1)}, bf16[256,512]{1,0:T(8,128)(2,1)S(1)}, u32[]{:S(2)}, u32[]{:S(2)}) collective-permute-start(bf16[256,512]{1,0:T(8,128)(2,1)S(1)} %get-tuple-element.25.refs_4_.refs_13_.refs_8_), channel_id=1, source_target_pairs={{0,6},{1,7},{2,0},{3,1},{4,2},{5,3},{6,4},{7,5},{8,14},{9,15},{10,... | collective-permute-start | bytes 786440 | tf_op jit(solution)/shard_map/ppermute | solution.py:32
  34.0 19.4 %collective-permute-start.2 = (bf16[256,576]{1,0:T(8,128)(2,1)S(1)}, bf16[256,576]{1,0:T(8,128)(2,1)S(1)}, u32[]{:S(2)}, u32[]{:S(2)}) collective-permute-start(bf16[256,576]{1,0:T(8,128)(2,1)S(1)} %get-tuple-element.24.refs_0_.refs_9_.refs_4_), channel_id=1, source_target_pairs={{0,6},{1,7},{2,0},{3,1},{4,2},{5,3},{6,4},{7,5},{8,14},{9,15},{10,... | collective-permute-start | bytes 884744 | tf_op jit(solution)/shard_map/ppermute | solution.py:32
  39.8 13.7 %collective-permute-start.1 = (bf16[256,576]{1,0:T(8,128)(2,1)S(1)}, bf16[256,576]{1,0:T(8,128)(2,1)S(1)}, u32[]{:S(2)}, u32[]{:S(2)}) collective-permute-start(bf16[256,576]{1,0:T(8,128)(2,1)S(1)} %collective-permute-done.refs_0_.refs_1_.refs_10_.refs_5_), channel_id=1, source_target_pairs={{0,2},{1,3},{2,4},{3,5},{4,6},{5,7},{6,0},{7,1},{8,10},{9,11},{10,... | collective-permute-start | bytes 884744 | tf_op jit(solution)/shard_map/ppermute | solution.py:32
  40.2 13.2 %collective-permute-start.3 = (bf16[256,512]{1,0:T(8,128)(2,1)S(1)}, bf16[256,512]{1,0:T(8,128)(2,1)S(1)}, u32[]{:S(2)}, u32[]{:S(2)}) collective-permute-start(bf16[256,512]{1,0:T(8,128)(2,1)S(1)} %get-tuple-element.25.refs_4_.refs_13_.refs_8_), channel_id=1, source_target_pairs={{0,2},{1,3},{2,4},{3,5},{4,6},{5,7},{6,0},{7,1},{8,10},{9,11},{10,... | collective-permute-start | bytes 786440 | tf_op jit(solution)/shard_map/ppermute | solution.py:32
  41.7 11.7 %collective-permute-start.5 = (bf16[256,512]{1,0:T(8,128)(2,1)S(1)}, bf16[256,512]{1,0:T(8,128)(2,1)S(1)}, u32[]{:S(2)}, u32[]{:S(2)}) collective-permute-start(bf16[256,512]{1,0:T(8,128)(2,1)S(1)} %collective-permute-done.4.refs_5_.refs_7_.refs_16_.refs_11_), channel_id=1, source_target_pairs={{0,6},{1,7},{2,0},{3,1},{4,2},{5,3},{6,4},{7,5},{8,14},{9,15},{10,... | collective-permute-start | bytes 786440 | tf_op jit(solution)/shard_map/ppermute | solution.py:32
  57.2 2.4 %collective-permute-start.6 = (bf16[64,8,576]{2,1,0:T(8,128)(2,1)S(1)}, bf16[64,8,576]{2,1,0:T(8,128)(2,1)S(1)}, u32[]{:S(2)}, u32[]{:S(2)}) collective-permute-start(bf16[64,8,576]{2,1,0:T(8,128)(2,1)S(1)} %bitcast.13), channel_id=1, source_target_pairs={{0,1},{1,0},{2,3},{3,2},{4,5},{5,4},{6,7},{7,6},{8,9},{9,8},{10,11... | collective-permute-start | bytes 1769480 | tf_op jit(solution)/shard_map/ppermute | solution.py:360
  61.5 8.4 %collective-permute-start.7 = (f32[4,8,256]{2,1,0:T(8,128)S(1)}, f32[4,8,256]{2,1,0:T(8,128)S(1)}, u32[]{:S(2)}, u32[]{:S(2)}) collective-permute-start(f32[4,8,256]{2,1,0:T(8,128)S(1)} %get-tuple-element.31.refs_6_.refs_5_.refs_0_), channel_id=1, source_target_pairs={{0,2},{1,3},{2,4},{3,5},{4,6},{5,7},{6,0},{7,1},{8,10},{9,11},{10,... | collective-permute-start | bytes 98312 | tf_op jit(solution)/shard_map/ppermute | solution.py:32
  63.1 6.8 %collective-permute-start.8 = (f32[4,8,256]{2,1,0:T(8,128)S(1)}, f32[4,8,256]{2,1,0:T(8,128)S(1)}, u32[]{:S(2)}, u32[]{:S(2)}) collective-permute-start(f32[4,8,256]{2,1,0:T(8,128)S(1)} %get-tuple-element.31.refs_6_.refs_5_.refs_0_), channel_id=1, source_target_pairs={{0,4},{1,5},{2,6},{3,7},{4,0},{5,1},{6,2},{7,3},{8,12},{9,13},{10,... | collective-permute-start | bytes 98312 | tf_op jit(solution)/shard_map/ppermute | solution.py:32
  65.8 4.1 %collective-permute-start.9 = (f32[4,8,256]{2,1,0:T(8,128)S(1)}, f32[4,8,256]{2,1,0:T(8,128)S(1)}, u32[]{:S(2)}, u32[]{:S(2)}) collective-permute-start(f32[4,8,256]{2,1,0:T(8,128)S(1)} %get-tuple-element.31.refs_6_.refs_5_.refs_0_), channel_id=1, source_target_pairs={{0,6},{1,7},{2,0},{3,1},{4,2},{5,3},{6,4},{7,5},{8,14},{9,15},{10,... | collective-permute-start | bytes 98312 | tf_op jit(solution)/shard_map/ppermute | solution.py:32
  72.5 4.5 %collective-permute-start.14 = (bf16[32,24,576]{2,1,0:T(8,128)(2,1)S(1)}, bf16[32,24,576]{2,1,0:T(8,128)(2,1)S(1)}, u32[]{:S(2)}, u32[]{:S(2)}) collective-permute-start(bf16[32,24,576]{2,1,0:T(8,128)(2,1)S(1)} %bitcast.18), channel_id=1, source_target_pairs={{0,1},{1,0},{2,3},{3,2},{4,5},{5,4},{6,7},{7,6},{8,9},{9,8},{10,11... | collective-permute-start | bytes 2654216 | tf_op jit(solution)/shard_map/ppermute | solution.py:397
  77.1 9.5 %copy-start.4 = (bf16[1088,256]{1,0:T(8,128)(2,1)S(1)}, bf16[1088,256]{1,0:T(8,128)(2,1)}, u32[]{:S(2)}) copy-start(bf16[1088,256]{1,0:T(8,128)(2,1)} %get-tuple-element.35) | copy-start | bytes 1671172
  77.1 21.7 %copy-start.2 = (bf16[576,256]{1,0:T(8,128)(2,1)S(1)}, bf16[576,256]{1,0:T(8,128)(2,1)}, u32[]{:S(2)}) copy-start(bf16[576,256]{1,0:T(8,128)(2,1)} %get-tuple-element.38) | copy-start | bytes 884740
  78.3 24.3 %copy-start.3 = (bf16[512,256]{1,0:T(8,128)(2,1)S(1)}, bf16[512,256]{1,0:T(8,128)(2,1)}, u32[]{:S(2)}) copy-start(bf16[512,256]{1,0:T(8,128)(2,1)} %get-tuple-element.37) | copy-start | bytes 786436
  78.3 32.6 %copy-start = (bf16[1088,256]{1,0:T(8,128)(2,1)S(1)}, bf16[1088,256]{1,0:T(8,128)(2,1)}, u32[]{:S(2)}) copy-start(bf16[1088,256]{1,0:T(8,128)(2,1)} %get-tuple-element.34.here) | copy-start | bytes 1671172
  78.3 33.7 %all-to-all-start.2 = ((bf16[32,24,576]{2,1,0:T(8,128)(2,1)}), bf16[32,24,576]{2,1,0:T(8,128)(2,1)S(1)}, u32[]{:S(2)}, u32[]{:S(2)}) async-start(bf16[32,24,576]{2,1,0:T(8,128)(2,1)} %fusion.1), calls=%async_computation.2 | async-start | bytes 1966080 | tf_op jit(solution)/shard_map/all_to_all | solution.py:410
  84.0 27.9 %copy-start.1 = (bf16[768,256]{1,0:T(8,128)(2,1)S(1)}, bf16[768,256]{1,0:T(8,128)(2,1)}, u32[]{:S(2)}) copy-start(bf16[768,256]{1,0:T(8,128)(2,1)} %get-tuple-element.41.hot_ref) | copy-start | bytes 1179652
  84.0 14.8 %collective-permute-start.11 = (bf16[1088,256]{1,0:T(8,128)(2,1)}, bf16[1088,256]{1,0:T(8,128)(2,1)S(1)}, u32[]{:S(2)}, u32[]{:S(2)}) collective-permute-start(bf16[1088,256]{1,0:T(8,128)(2,1)} %get-tuple-element.36), channel_id=1, source_target_pairs={{0,6},{1,7},{2,0},{3,1},{4,2},{5,3},{6,4},{7,5},{8,14},{9,15},{10,... | collective-permute-start | bytes 1671176 | tf_op jit(solution)/shard_map/ppermute | solution.py:32
  86.5 16.0 %collective-permute-start.10 = (bf16[1088,256]{1,0:T(8,128)(2,1)S(1)}, bf16[1088,256]{1,0:T(8,128)(2,1)S(1)}, u32[]{:S(2)}, u32[]{:S(2)}) collective-permute-start(bf16[1088,256]{1,0:T(8,128)(2,1)S(1)} %copy-done.4), channel_id=1, source_target_pairs={{0,2},{1,3},{2,4},{3,5},{4,6},{5,7},{6,0},{7,1},{8,10},{9,11},{10,... | collective-permute-start | bytes 1671176 | tf_op jit(solution)/shard_map/ppermute | solution.py:32
  98.9 12.0 %collective-permute-start.13 = (bf16[576,256]{1,0:T(8,128)(2,1)S(1)}, bf16[576,256]{1,0:T(8,128)(2,1)S(1)}, u32[]{:S(2)}, u32[]{:S(2)}) collective-permute-start(bf16[576,256]{1,0:T(8,128)(2,1)S(1)} %add_convert_fusion), channel_id=1, source_target_pairs={{0,6},{1,7},{2,0},{3,1},{4,2},{5,3},{6,4},{7,5},{8,14},{9,15},{10,... | collective-permute-start | bytes 884744 | tf_op jit(solution)/shard_map/ppermute | solution.py:32
  102.6 8.3 %collective-permute-start.12 = (bf16[512,256]{1,0:T(8,128)(2,1)S(1)}, bf16[512,256]{1,0:T(8,128)(2,1)S(1)}, u32[]{:S(2)}, u32[]{:S(2)}) collective-permute-start(bf16[512,256]{1,0:T(8,128)(2,1)S(1)} %add_convert_fusion.1), channel_id=1, source_target_pairs={{0,2},{1,3},{2,4},{3,5},{4,6},{5,7},{6,0},{7,1},{8,10},{9,11},{10,... | collective-permute-start | bytes 786440 | tf_op jit(solution)/shard_map/ppermute | solution.py:32

commit v4 on v3

--- a/solution.py
+++ b/solution.py
@@ -9,6 +9,7 @@
 from jax.sharding import PartitionSpec as P
 
 USED = 64
+QUERIES = 16
 XN = 4
 CORES = 2
 
@@ -103,26 +104,25 @@
     out_ref[...] = total.astype(bf16)
 
 
-def slot_hot(ids_ref, tokens, lanes):
-    ids = expand(jnp.broadcast_to(ids_ref[:, 0:1], (ids_ref.shape[0], lanes)), tokens)
+def slot_hot(ids, tokens, lanes):
+    ids = expand(jnp.broadcast_to(ids, (ids.shape[0], lanes)), tokens)
     row, lane = iotas(ids.shape)
     return bit_matrix(ids * tokens + (row & (tokens - 1)) == lane)
 
 
-def unpack_kernel(tokens, pick_ref, rows_ref, *refs):
-    hot = slot_hot(pick_ref, tokens, rows_ref.shape[0])
+def unpack_kernel(tokens, plan_ref, rows_ref, *refs):
+    hot = slot_hot(plan_ref[:USED, 1:2], tokens, rows_ref.shape[0])
     refs[-1][...] = dot32(hot, rows_ref[...]).astype(bf16)
 
 
-def score_half(tokens, lim_ref, key_ref, q_refs, g_refs, p_ref, gw_ref):
+def score_half(tokens, half, plan_ref, key_ref, q_refs, g_refs, p_ref, gw_ref):
     rows = p_ref.shape[2]
-    query_count = lim_ref.shape[1]
-    heads = rows // query_count
+    heads = rows // QUERIES
     value_width = g_refs[0].shape[1]
-    row, lane = iotas((query_count, rows))
-    start = row * heads
+    row, lane = iotas((plan_ref.shape[1], rows))
+    start = (row - 2 - half * QUERIES) * heads
     repeat = bit_matrix((lane >= start) & (lane < start + heads))
-    limit = expand(dot32(lim_ref[...].astype(bf16), repeat), tokens)
+    limit = expand(dot32(plan_ref[:USED, :].astype(f32).astype(bf16), repeat), tokens)
     token = (iotas(limit.shape)[0] & (tokens - 1)).astype(f32)
     bias = jnp.where(token <= limit, 0.0, -jnp.inf)
     for k in range(XN):
@@ -136,21 +136,21 @@
         yield k, peak, total, jnp.sum(p * gw, axis=0, keepdims=True)
 
 
-def own_score_kernel(tokens, lim_ref, key_ref, *refs):
+def own_score_kernel(tokens, plan_ref, key_ref, *refs):
     q_refs, g_refs = refs[:XN], refs[XN : 2 * XN]
     p_ref, gw_ref, stat_ref = refs[2 * XN :]
     for k, peak, total, inner in score_half(
-        tokens, lim_ref, key_ref, q_refs, g_refs, p_ref, gw_ref
+        tokens, 0, plan_ref, key_ref, q_refs, g_refs, p_ref, gw_ref
     ):
         pad = jnp.zeros((5, peak.shape[1]), f32)
         stat_ref[k] = jnp.concatenate([peak, total, inner, pad])
 
 
-def other_score_kernel(tokens, lim_ref, key_ref, *refs):
+def other_score_kernel(tokens, plan_ref, key_ref, *refs):
     q_refs, g_refs, own_ref = refs[:XN], refs[XN : 2 * XN], refs[2 * XN]
     p_ref, gw_ref, stat_ref = refs[2 * XN + 1 :]
     for k, peak, total, inner in score_half(
-        tokens, lim_ref, key_ref, q_refs, g_refs, p_ref, gw_ref
+        tokens, 1, plan_ref, key_ref, q_refs, g_refs, p_ref, gw_ref
     ):
         own = own_ref[k]
         top = jnp.maximum(peak, own[0:1])
@@ -163,7 +163,10 @@
 
 def local_kernel(*refs):
     key_refs, p_refs, gw_refs = refs[:CORES], refs[CORES : 2 * CORES], refs[2 * CORES : 3 * CORES]
-    stat_ref, value_ref, grad_ref = refs[3 * CORES :]
+    stat_ref, value_ref, grad_out, grad_ref, sems = refs[3 * CORES :]
+    copies = [
+        pltpu.make_async_copy(grad_ref.at[k], grad_out.at[k], sems.at[k]) for k in range(XN)
+    ]
     keys_t = [key_ref[...].T for key_ref in key_refs]
     for k in range(XN):
         stats = stat_ref[k]
@@ -173,8 +176,11 @@
             p = p_refs[h][k].astype(f32) * stats[3 + h : 4 + h]
             value.append(dot32(keys_t[h], p.astype(bf16)))
             grad.append(dot32(keys_t[h], (p * (gw_refs[h][k] - inner)).astype(bf16)))
-        value_ref[k] = value[0] + value[1]
-        grad_ref[k] = grad[0] + grad[1]
+        value_ref[k] = (value[0] + value[1]).astype(bf16)
+        grad_ref[k] = (grad[0] + grad[1]).astype(bf16)
+        copies[k].start()
+    for copy in copies:
+        copy.wait()
 
 
 def row_stats(stat_refs, k):
@@ -186,72 +192,60 @@
     return stats[0], inner, factors[0] / total
 
 
-def key_grad_kernel(tokens, half, order_ref, p_ref, gw_ref, *refs):
-    stat_refs, q_refs, g_refs = refs[:XN], refs[XN : 2 * XN], refs[2 * XN : 3 * XN]
-    out_ref, sum_ref = refs[-2:]
+def key_grad_kernel(tokens, half, *refs):
+    p_ref, gw_ref = refs[:2]
+    stat_refs, q_refs, g_refs = (refs[2 + i * XN : 2 + (i + 1) * XN] for i in range(3))
+    last_ref, sum_ref = refs[2 + 3 * XN], refs[-1]
     value_width = g_refs[0].shape[1]
     key_grad, value_grad = [], []
     for k in range(XN):
         mine, inner, factor = row_stats(stat_refs, k)
-        weights = p_ref[k].astype(f32) * (factor * mine[3 + half : 4 + half])
-        ds = (weights * (gw_ref[k] - inner) * score_scale).astype(bf16)
+        factor = factor * mine[3 + half : 4 + half]
+        p = p_ref[k].astype(f32)
+        ds = (p * (factor * score_scale) * (gw_ref[k] - inner)).astype(bf16)
         key_grad.append(dot32(ds, q_refs[k][...]))
-        value_grad.append(dot32(weights.astype(bf16), g_refs[k][...]))
+        value_grad.append(dot32((p * factor).astype(bf16), g_refs[k][...]))
     key_grad, value_grad = sum(key_grad), sum(value_grad)
     sum_ref[:, :value_width] = (key_grad[:, :value_width] + value_grad).astype(bf16)
     sum_ref[:, value_width:] = key_grad[:, value_width:].astype(bf16)
-    hot = slot_hot(order_ref, tokens, sum_ref.shape[0])
-    out_ref[...] = dot32(hot, sum_ref[...]).astype(bf16)
-
-
-def own_grad_kernel(tokens, *refs):
-    value_ref, grad_ref = refs[:2]
-    stat_refs = refs[5 : 5 + XN]
-    outs, sum_ref, sems = refs[-12:-7], refs[-7], refs[-1]
-    here_ref, right_ref, left_ref, att3_ref, qg1_ref = refs[-6:-1]
-    value_width = att3_ref.shape[0]
-    att_out = (
-        here_ref.at[:value_width],
-        left_ref.at[:value_width],
-        right_ref.at[:value_width],
-        att3_ref,
-    )
-    qg_out = (
-        here_ref.at[value_width:],
-        qg1_ref,
-        left_ref.at[value_width:],
-        right_ref.at[value_width:],
-    )
+    if half == 0:
+        hot_ref, out_ref = last_ref, refs[-2]
+    else:
+        out_ref, hot_ref = refs[-3:-1]
+        hot_ref[...] = slot_hot(last_ref[:, 0:1], tokens, sum_ref.shape[0])
+    out_ref[...] = dot32(hot_ref[...], sum_ref[...]).astype(bf16)
+
+
+def scale_kernel(*refs):
+    stat_refs, (value_ref, grad_in), outs = refs[:XN], refs[XN : XN + 2], refs[XN + 2 : -2]
+    grad_ref, sems = refs[-2:]
+    att_refs, qg_refs = outs[:XN], outs[XN:]
+    copies = [pltpu.make_async_copy(grad_in.at[k], grad_ref.at[k], sems.at[k]) for k in range(XN)]
+    for copy in copies:
+        copy.start()
     for k in range(XN):
+        copies[k].wait()
         mine, inner, factor = row_stats(stat_refs, k)
         shift = mine[2:3] / mine[1:2] - inner
-        att_out[k][...] = (value_ref[k, :value_width] * factor).astype(bf16)
-        qg = (grad_ref[k] + value_ref[k] * shift) * (factor * score_scale)
-        qg_out[k][...] = qg.astype(bf16)
-    copies = [
-        pltpu.make_async_copy(src, dst, sems.at[i])
-        for i, (src, dst) in enumerate(zip(refs[-6:-1], outs))
-    ]
-    for copy in copies:
-        copy.start()
-    key_grad_kernel(tokens, 0, *refs[2:-12], sum_ref)
-    for copy in copies:
-        copy.wait()
-
-
-def combine_kernel(here, right, left, att, qg, att_ref, qg_ref):
-    value_width = att_ref.shape[1]
-    total = here[:value_width].astype(f32) + left[:value_width].astype(f32) + att[...].astype(f32)
-    att_ref[...] = total.astype(bf16).T
-    total = here[value_width:].astype(f32) + right[value_width:].astype(f32) + qg[...].astype(f32)
-    qg_ref[...] = total.astype(bf16).T
+        value = value_ref[k].astype(f32)
+        att_refs[k][...] = (value[: att_refs[k].shape[0]] * factor).astype(bf16)
+        qg = (grad_ref[k].astype(f32) + value * shift) * (factor * score_scale)
+        qg_refs[k][...] = qg.astype(bf16)
+
+
+def combine_kernel(*refs):
+    for parts, out_ref in ((refs[:3], refs[6]), (refs[3:6], refs[7])):
+        total = sum(part[...].astype(f32) for part in parts)
+        out_ref[...] = total.astype(bf16).T
 
 
 def shaped(shape, dtype=bf16):
     return jax.ShapeDtypeStruct(shape, dtype)
 
 
-def call(kernel, out_shape, operands, name, unused=(), scratch=(), far_in=0, far_out=()):
+def call(
+    kernel, out_shape, operands, name, unused=(), unused_far=(), scratch=(), far_in=0, far_out=()
+):
     vmem, hbm = (pl.BlockSpec(memory_space=m) for m in (pltpu.VMEM, pltpu.HBM))
     near = len(operands) - far_in
     operands = operands[:near] + [
@@ -264,12 +258,17 @@
         ],
         in_specs=[vmem] * near
         + [hbm] * far_in
-        + [pl.BlockSpec(memory_space=pl.ANY)] * len(unused),
+        + [pl.BlockSpec(memory_space=pl.ANY)] * len(unused)
+        + [hbm] * len(unused_far),
         out_specs=[hbm if i in far_out else vmem for i in range(len(out_shape))],
         scratch_shapes=list(scratch),
         compiler_params=pltpu.CompilerParams(vmem_limit_bytes=VMEM_LIMIT),
         name=name,
-    )(*operands, *unused)
+    )(
+        *operands,
+        *unused,
+        *(pltpu.with_memory_space_constraint(x, pltpu.HBM) for x in unused_far),
+    )
 
 
 def slot_table(wanted, slot_limit):
@@ -318,12 +317,11 @@
     chosen = jnp.any(selected[None, :, :] == block_ids[:, None, None], axis=2)
     limit = jnp.where(chosen, positions[None, :] - block_ids[:, None] * block_size, -1)
     limit = jnp.clip(limit, -1, block_size - 1)
-    own_limit = (limit - tp * tokens).astype(f32)
-    other_limit = (limit - (tp ^ 1) * tokens).astype(f32)
-    pick = jnp.broadcast_to(picked[:, None], (USED, 128))
-    order = jnp.broadcast_to(slot_order[:, None], (slots, 128))
-
-    early = (own_limit, other_limit, pick, order)
+    columns = [picked[:, None], limit - tp * tokens, limit - (tp ^ 1) * tokens]
+    plan = jnp.pad(jnp.concatenate(columns, axis=1), ((0, slots - USED), (0, 0)))
+    plan = jnp.concatenate([slot_order[:, None], plan], axis=1)
+    plan = jnp.pad(plan, ((0, 0), (0, 128 - plan.shape[1])))
+
     packed, asked_hot, q0, g0 = call(
         functools.partial(pack_kernel, tokens, slot_limit),
         [
@@ -334,7 +332,7 @@
         ],
         [asked, latent_cache, query_rows, grad_rows],
         "pack",
-        unused=early,
+        unused=(plan,),
         scratch=[
             pltpu.VMEM((block_count, CORES * tokens, width), bf16),
             pltpu.VMEM((slots * tokens, held), bf16),
@@ -353,7 +351,7 @@
     (own_keys,) = call(
         functools.partial(unpack_kernel, tokens),
         [shaped((half, width))],
-        [pick, fetched.reshape(slots * tokens, width)],
+        [plan, fetched.reshape(slots * tokens, width)],
         "unpack",
         unused=(q1, q2, q3, g1, g2, g3),
     )
@@ -367,55 +365,66 @@
     own_p, own_gw, own_stats = call(
         functools.partial(own_score_kernel, tokens),
         score_shapes,
-        [own_limit, own_keys, *gathered],
+        [plan, own_keys, *gathered],
         "own_scores",
     )
     other_p, other_gw, stats = call(
         functools.partial(other_score_kernel, tokens),
         score_shapes,
-        [other_limit, other_keys, *gathered, own_stats],
+        [plan, other_keys, *gathered, own_stats],
         "other_scores",
     )
     all_stats = [stats] + [send_x(stats, k) for k in range(1, XN)]
+    part_shape = (XN, width, rows)
+    part_scratch = [pltpu.VMEM(part_shape, bf16), pltpu.SemaphoreType.DMA((XN,))]
     value_part, grad_part = call(
         local_kernel,
-        [shaped((XN, width, rows), f32)] * 2,
+        [shaped(part_shape)] * 2,
         [own_keys, other_keys, own_p, other_p, own_gw, other_gw, stats],
         "local",
-    )
-
-    both = width + value_width
+        far_out=(1,),
+        scratch=part_scratch,
+    )
+
+    grad_shape = shaped((slots * tokens, width))
     sum_scratch = [pltpu.VMEM((half, width), bf16)]
-    (other_grad,) = call(
+    other_grad, spread_hot = call(
         functools.partial(key_grad_kernel, tokens, 1),
-        [shaped((slots * tokens, width))],
-        [order, other_p, other_gw, *all_stats, *gathered],
+        [grad_shape, shaped((slots * tokens, half))],
+        [other_p, other_gw, *all_stats, *gathered, plan],
         "other_grads",
         unused=(value_part,),
         scratch=sum_scratch,
     )
     from_core = lax.ppermute(other_grad.reshape(parcels), "tp", CORE_SWAP)
-    own_grad, here, right, left, att3, qg1 = call(
-        functools.partial(own_grad_kernel, tokens),
-        [shaped((slots * tokens, width))]
-        + [shaped((n, rows)) for n in (both, both, both, value_width, width)],
-        [value_part, grad_part, order, own_p, own_gw, *all_stats, *gathered],
+    (own_grad,) = call(
+        functools.partial(key_grad_kernel, tokens, 0),
+        [grad_shape],
+        [own_p, own_gw, *all_stats, *gathered, spread_hot],
         "own_grads",
-        scratch=sum_scratch
-        + [pltpu.VMEM((n, rows), bf16) for n in (both, both, both, value_width, width)]
-        + [pltpu.SemaphoreType.DMA((5,))],
-        far_out=(1, 2, 3, 4, 5),
+        scratch=sum_scratch,
     )
     returning = (own_grad.reshape(parcels).astype(f32) + from_core.astype(f32)).astype(bf16)
     returned = lax.all_to_all(returning, "ctx", 0, 0, tiled=True)
 
-    right, left = send_x(right, 1), send_x(left, -1)
-    att = (att3.astype(f32) + right[:value_width].astype(f32)).astype(bf16)
-    qg = (qg1.astype(f32) + left[value_width:].astype(f32)).astype(bf16)
+    out_shapes = [(value_width, rows)] * XN + [(width, rows)] * XN
+    outs = call(
+        scale_kernel,
+        [shaped(x) for x in out_shapes],
+        [*all_stats, value_part, grad_part],
+        "scale",
+        far_in=1,
+        scratch=part_scratch,
+    )
+    att, qg = outs[:XN], outs[XN:]
+    att_far, qg_far = send_x(att[2], 1), send_x(qg[2], -1)
+    qg_left, att_right = send_x(qg[3], 1), send_x(att[1], -1)
+    att_left = (att[3].astype(f32) + att_far.astype(f32)).astype(bf16)
+    qg_right = (qg[1].astype(f32) + qg_far.astype(f32)).astype(bf16)
     attended, query_grad = call(
         combine_kernel,
         [shaped((rows, value_width)), shaped((rows, width))],
-        [here, right, left, send_x(att, 1), send_x(qg, -1)],
+        [att[0], send_x(att_left, 1), att_right, qg[0], qg_left, send_x(qg_right, -1)],
         "combine",
     )
     (cache_grad,) = call(

time: 114 us -> 112 us (0.982)
  waiting for transfers between devices: 42.1 us -> 38.9 us
    ppermute x13 -> x15, waiting for transfers between devices: 33.6 us -> 30 us  [send_x(): return lax.ppermute(value, 'tp', x_shift(k % XN))]
    all_to_all x1, waiting for transfers between devices: 0.01 us -> 1.66 us  [on_device(): returned = lax.all_to_all(returning, 'ctx', 0, 0, tiled=True)]
    pallas_call x9 -> x10, Pallas kernels: 19.3 us -> 20.4 us  [call(): pl.pallas_call(kernel, out_shape=[pltpu.HBM(x.shape, x.dtype) if i in far...]
    ppermute x13 -> x15, starting transfers between devices: 21.6 us -> 21.8 us  [send_x(): return lax.ppermute(value, 'tp', x_shift(k % XN))]
  transfers between devices with their start and end apart: 18 -> 20, of which waited for: 7 -> 12; matrix products, arithmetic and copies ran while one was open for 3% -> 3% of each run, Pallas kernels for 9% -> 10%
where the time goes in v4:
time: 112 us
  starting transfers between devices  44.7 us (40%)
  waiting for transfers between devices  38.9 us (35%)
  Pallas kernels  20.4 us (18%)
  other arithmetic  4.33 us (4%)
  local copies, waits for them, and re-layouts  2.46 us (2%)
    ppermute x15, waiting for transfers between devices, send_x(): return lax.ppermute(value, 'tp', x_shift(k % XN))  30 us
    ppermute x15, starting transfers between devices, send_x(): return lax.ppermute(value, 'tp', x_shift(k % XN))  21.8 us
    pallas_call x10, Pallas kernels, call(): pl.pallas_call(kernel, out_shape=[pltpu.HBM(x.shape, x.dtype) if i in far...  20.4 us
    all_to_all x1, starting transfers between devices, on_device(): lax.all_to_all(wanted.astype(jnp.int32)[:, None, :], 'ctx', split_axis=0,...  11.7 us
    all_to_all x1, starting transfers between devices, on_device(): returned = lax.all_to_all(returning, 'ctx', 0, 0, tiled=True)  5.57 us
    all_to_all x1, starting transfers between devices, on_device(): fetched = lax.all_to_all(packed.reshape(parcels), 'ctx', 0, 0, tiled=True)  5.03 us
    all_to_all x1, waiting for transfers between devices, on_device(): lax.all_to_all(wanted.astype(jnp.int32)[:, None, :], 'ctx', split_axis=0,...  4.79 us
    all_to_all x1, waiting for transfers between devices, on_device(): fetched = lax.all_to_all(packed.reshape(parcels), 'ctx', 0, 0, tiled=True)  2.25 us
  transfers between devices with their start and end apart: 20, of which 12 were waited for; matrix products, arithmetic and copies ran while one was open for 3% of the time, Pallas kernels for 10%

profile of v4, /device:TPU:8, one launch (start us, length us, event | category | flops | bytes accessed | tf_op | source)
XLA Modules:
  0.0 111.8 jit_solution(14418330742341428881)
XLA Ops:
  0.6 0.8 eq.26
  1.4 0.4 fusion
  1.8 0.7 reshape.173
  2.5 11.7 %all-to-all-start = ((s32[32,1,32]{2,1,0:T(1,128)}), s32[32,1,32]{2,1,0:T(1,128)S(1)}, u32[]{:S(2)}, u32[]{:S(2)}) async-start(s32[32,1,32]{2,1,0:T(1,128)} %reshape.173), calls=%async_computation | async-start | bytes 32768 | tf_op jit(solution)/shard_map/all_to_all | solution.py:302
  14.3 0.2 reduce_window_sum.18
  14.5 0.2 fusion.3
  15.8 0.9 compare_reduce_fusion
  16.9 0.7 fusion.5
  17.8 4.8 %all-to-all-done.asked_ref = s32[32,1,32]{2,1,0:T(1,128)S(1)} async-done(((s32[32,1,32]{2,1,0:T(1,128)}), s32[32,1,32]{2,1,0:T(1,128)S(1)}, u32[]{:S(2)}, u32[]{:S(2)}) %all-to-all-start) | async-done | bytes 4128 | tf_op jit(solution)/shard_map/all_to_all | solution.py:302
  22.6 2.9 %pack.1 = (bf16[768,576]{1,0:T(8,128)(2,1)}, bf16[768,256]{1,0:T(8,128)(2,1)}, bf16[256,576]{1,0:T(8,128)(2,1)S(1)}, bf16[256,512]{1,0:T(8,128)(2,1)S(1)}) custom-call(s32[32,1,32]{2,1,0:T(1,128)S(1)} %all-to-all-done.asked_ref, bf16[32,64,576]{2,1,0:T(8,128)(2,1)} %cache_ref.1, bf16[256,576]{1,0:T(8,128)(2,1)} %bitcast.21, bf16[256,512]{1,0:T(8,128)(2,1)} %bitcast.23, ...), custom_call_target="tpu_custom_call" | custom-call | tf_op jit(solution)/shard_map/pack/pallas_call | solution.py:254
  25.5 5.0 %all-to-all-start.1 = ((bf16[32,24,576]{2,1,0:T(8,128)(2,1)}), bf16[32,24,576]{2,1,0:T(8,128)(2,1)S(1)}, u32[]{:S(2)}, u32[]{:S(2)}) async-start(bf16[32,24,576]{2,1,0:T(8,128)(2,1)} %bitcast.3), calls=%async_computation.1 | async-start | bytes 1966080 | tf_op jit(solution)/shard_map/all_to_all | solution.py:344
  30.6 1.6 %collective-permute-start = (bf16[256,576]{1,0:T(8,128)(2,1)S(1)}, bf16[256,576]{1,0:T(8,128)(2,1)S(1)}, u32[]{:S(2)}, u32[]{:S(2)}) collective-permute-start(bf16[256,576]{1,0:T(8,128)(2,1)S(1)} %get-tuple-element.28.refs_0_.refs_6_), channel_id=1, source_target_pairs={{0,2},{1,3},{2,4},{3,5},{4,6},{5,7},{6,0},{7,1},{8,10},{9,11},{10,... | collective-permute-start | bytes 884744 | tf_op jit(solution)/shard_map/ppermute | solution.py:33
  32.1 1.7 %collective-permute-start.4 = (bf16[256,512]{1,0:T(8,128)(2,1)S(1)}, bf16[256,512]{1,0:T(8,128)(2,1)S(1)}, u32[]{:S(2)}, u32[]{:S(2)}) collective-permute-start(bf16[256,512]{1,0:T(8,128)(2,1)S(1)} %get-tuple-element.29.refs_4_.refs_10_), channel_id=1, source_target_pairs={{0,6},{1,7},{2,0},{3,1},{4,2},{5,3},{6,4},{7,5},{8,14},{9,15},{10,... | collective-permute-start | bytes 786440 | tf_op jit(solution)/shard_map/ppermute | solution.py:33
  33.9 1.6 %collective-permute-start.2 = (bf16[256,576]{1,0:T(8,128)(2,1)S(1)}, bf16[256,576]{1,0:T(8,128)(2,1)S(1)}, u32[]{:S(2)}, u32[]{:S(2)}) collective-permute-start(bf16[256,576]{1,0:T(8,128)(2,1)S(1)} %get-tuple-element.28.refs_0_.refs_6_), channel_id=1, source_target_pairs={{0,6},{1,7},{2,0},{3,1},{4,2},{5,3},{6,4},{7,5},{8,14},{9,15},{10,... | collective-permute-start | bytes 884744 | tf_op jit(solution)/shard_map/ppermute | solution.py:33
  35.4 4.7 %collective-permute-done.refs_0_.refs_1_.refs_7_ = bf16[256,576]{1,0:T(8,128)(2,1)S(1)} collective-permute-done((bf16[256,576]{1,0:T(8,128)(2,1)S(1)}, bf16[256,576]{1,0:T(8,128)(2,1)S(1)}, u32[]{:S(2)}, u32[]{:S(2)}) %collective-permute-start) | collective-permute-done | bytes 294944 | tf_op jit(solution)/shard_map/ppermute | solution.py:33
  40.2 0.3 collective-permute-start.1
  40.5 1.5 %collective-permute-start.3 = (bf16[256,512]{1,0:T(8,128)(2,1)S(1)}, bf16[256,512]{1,0:T(8,128)(2,1)S(1)}, u32[]{:S(2)}, u32[]{:S(2)}) collective-permute-start(bf16[256,512]{1,0:T(8,128)(2,1)S(1)} %get-tuple-element.29.refs_4_.refs_10_), channel_id=1, source_target_pairs={{0,2},{1,3},{2,4},{3,5},{4,6},{5,7},{6,0},{7,1},{8,10},{9,11},{10,... | collective-permute-start | bytes 786440 | tf_op jit(solution)/shard_map/ppermute | solution.py:33
  42.0 2.4 %collective-permute-start.5 = (bf16[256,512]{1,0:T(8,128)(2,1)S(1)}, bf16[256,512]{1,0:T(8,128)(2,1)S(1)}, u32[]{:S(2)}, u32[]{:S(2)}) collective-permute-start(bf16[256,512]{1,0:T(8,128)(2,1)S(1)} %collective-permute-done.4.refs_5_.refs_7_.refs_13_), channel_id=1, source_target_pairs={{0,6},{1,7},{2,0},{3,1},{4,2},{5,3},{6,4},{7,5},{8,14},{9,15},{10,... | collective-permute-start | bytes 786440 | tf_op jit(solution)/shard_map/ppermute | solution.py:33
  44.3 10.0 %collective-permute-done.3.refs_3_.refs_5_.refs_11_ = bf16[256,512]{1,0:T(8,128)(2,1)S(1)} collective-permute-done((bf16[256,512]{1,0:T(8,128)(2,1)S(1)}, bf16[256,512]{1,0:T(8,128)(2,1)S(1)}, u32[]{:S(2)}, u32[]{:S(2)}) %collective-permute-start.3) | collective-permute-done | bytes 262176 | tf_op jit(solution)/shard_map/ppermute | solution.py:33
  54.4 2.3 %all-to-all-done.1 = bf16[32,24,576]{2,1,0:T(8,128)(2,1)S(1)} async-done(((bf16[32,24,576]{2,1,0:T(8,128)(2,1)}), bf16[32,24,576]{2,1,0:T(8,128)(2,1)S(1)}, u32[]{:S(2)}, u32[]{:S(2)}) %all-to-all-start.1) | async-done | bytes 884768 | tf_op jit(solution)/shard_map/all_to_all | solution.py:344
  56.7 0.9 unpack.1.key_ref.refs_0_
  57.6 0.3 collective-permute-start.6
  57.9 1.9 %own_scores.1 = (bf16[4,512,256]{2,1,0:T(8,128)(2,1)S(1)}, f32[4,512,256]{2,1,0:T(8,128)S(1)}, f32[4,8,256]{2,1,0:T(8,128)S(1)}) custom-call(s32[96,128]{1,0:T(8,128)S(1)} %pad.9.refs_0_.plan_ref.refs_14_, bf16[512,576]{1,0:T(8,128)(2,1)S(1)} %unpack.1.key_ref.refs_0_, bf16[256,576]{1,0:T(8,128)(2,1)S(1)} %get-tuple-element.28.refs_0_.refs_6_, ...), custom_call_target="tpu_custom_call" | custom-call | tf_op jit(solution)/shard_map/own_scores/pallas_call | solution.py:254
  59.8 0.2 collective-permute-done.6
  60.0 1.9 %other_scores.1 = (bf16[4,512,256]{2,1,0:T(8,128)(2,1)S(1)}, f32[4,512,256]{2,1,0:T(8,128)S(1)}, f32[4,8,256]{2,1,0:T(8,128)S(1)}) custom-call(s32[96,128]{1,0:T(8,128)S(1)} %pad.9.refs_0_.plan_ref.refs_14_, bf16[512,576]{1,0:T(8,128)(2,1)S(1)} %bitcast.18, bf16[256,576]{1,0:T(8,128)(2,1)S(1)} %get-tuple-element.28.refs_0_.refs_6_, ...), custom_call_target="tpu_custom_call" | custom-call | tf_op jit(solution)/shard_map/other_scores/pallas_call | solution.py:254
  61.9 2.8 %collective-permute-start.9 = (f32[4,8,256]{2,1,0:T(8,128)S(1)}, f32[4,8,256]{2,1,0:T(8,128)S(1)}, u32[]{:S(2)}, u32[]{:S(2)}) collective-permute-start(f32[4,8,256]{2,1,0:T(8,128)S(1)} %get-tuple-element.31.refs_6_.refs_0_.refs_2_), channel_id=1, source_target_pairs={{0,6},{1,7},{2,0},{3,1},{4,2},{5,3},{6,4},{7,5},{8,14},{9,15},{10,... | collective-permute-start | bytes 98312 | tf_op jit(solution)/shard_map/ppermute | solution.py:33
  64.7 0.8 collective-permute-start.8
  65.5 0.9 collective-permute-start.7
  66.4 3.4 %local.1 = (bf16[4,576,256]{2,1,0:T(8,128)(2,1)S(1)}, bf16[4,576,256]{2,1,0:T(8,128)(2,1)}) custom-call(bf16[512,576]{1,0:T(8,128)(2,1)S(1)} %unpack.1.key_ref.refs_0_, bf16[512,576]{1,0:T(8,128)(2,1)S(1)} %bitcast.19, bf16[4,512,256]{2,1,0:T(8,128)(2,1)S(1)} %get-tuple-element.32.refs_2_.refs_0_, ...), custom_call_target="tpu_custom_call" | custom-call | tf_op jit(solution)/shard_map/local/pallas_call | solution.py:254
  69.9 0.3 collective-permute-done.8.refs_2_.refs_4_
  70.2 0.5 collective-permute-done.7.refs_1_.refs_3_
  70.7 2.7 %other_grads.1 = (bf16[768,576]{1,0:T(8,128)(2,1)S(1)}, bf16[768,512]{1,0:T(8,128)(2,1)S(1)}) custom-call(bf16[4,512,256]{2,1,0:T(8,128)(2,1)S(1)} %get-tuple-element.33.refs_3_.refs_0_, f32[4,512,256]{2,1,0:T(8,128)S(1)} %get-tuple-element.35.refs_5_.refs_1_, f32[4,8,256]{2,1,0:T(8,128)S(1)} %get-tuple-element.31.refs_6_.refs_0_.refs_2_, ...), custom_call_target="tpu_custom_call" | custom-call | tf_op jit(solution)/shard_map/other_grads/pallas_call | solution.py:254
  73.4 0.3 collective-permute-start.16
  73.8 2.6 %own_grads.1 = bf16[768,576]{1,0:T(8,128)(2,1)S(1)} custom-call(bf16[4,512,256]{2,1,0:T(8,128)(2,1)S(1)} %get-tuple-element.32.refs_2_.refs_0_, f32[4,512,256]{2,1,0:T(8,128)S(1)} %get-tuple-element.34.refs_4_.refs_1_, f32[4,8,256]{2,1,0:T(8,128)S(1)} %get-tuple-element.31.refs_6_.refs_0_.refs_2_, f32[4,8,256]{2,1,0:T(8,128)S(1)} %collective-permute-done.7.refs_1_.refs_3_, ...), custom_call_target="tpu_custom_call" | custom-call | tf_op jit(solution)/shard_map/own_grads/pallas_call | solution.py:254
  76.5 1.2 %fusion.1 = bf16[32,24,576]{2,1,0:T(8,128)(2,1)} fusion(bf16[32,24,576]{2,1,0:T(8,128)(2,1)S(1)} %bitcast.15, bf16[32,24,576]{2,1,0:T(8,128)(2,1)S(1)} %collective-permute-done.16), kind=kLoop, calls=%fused_computation.3 | loop fusion | flops 1769472 | bytes 2654208 | tf_op jit(solution)/shard_map/convert_element_type | solution.py:407
  77.7 5.6 %all-to-all-start.2 = ((bf16[32,24,576]{2,1,0:T(8,128)(2,1)}), bf16[32,24,576]{2,1,0:T(8,128)(2,1)S(1)}, u32[]{:S(2)}, u32[]{:S(2)}) async-start(bf16[32,24,576]{2,1,0:T(8,128)(2,1)} %fusion.1), calls=%async_computation.2 | async-start | bytes 1966080 | tf_op jit(solution)/shard_map/all_to_all | solution.py:408
  83.3 1.7 %scale.1 = (bf16[512,256]{1,0:T(8,128)(2,1)S(1)}, bf16[512,256]{1,0:T(8,128)(2,1)S(1)}, bf16[512,256]{1,0:T(8,128)(2,1)S(1)}, bf16[512,256]{1,0:T(8,128)(2,1)S(1...) custom-call(f32[4,8,256]{2,1,0:T(8,128)S(1)} %copy-done.3, ...), custom_call_target="tpu_custom_call" | custom-call | tf_op jit(solution)/shard_map/scale/pallas_call | solution.py:254
  85.0 1.9 %collective-permute-start.14 = (bf16[576,256]{1,0:T(8,128)(2,1)S(1)}, bf16[576,256]{1,0:T(8,128)(2,1)S(1)}, u32[]{:S(2)}, u32[]{:S(2)}) collective-permute-start(bf16[576,256]{1,0:T(8,128)(2,1)S(1)} %get-tuple-element.45), channel_id=1, source_target_pairs={{0,6},{1,7},{2,0},{3,1},{4,2},{5,3},{6,4},{7,5},{8,14},{9,15},{10,... | collective-permute-start | bytes 884744 | tf_op jit(solution)/shard_map/ppermute | solution.py:33
  86.9 0.2 collective-permute-start.10
  87.1 3.0 %collective-permute-start.12 = (bf16[512,256]{1,0:T(8,128)(2,1)S(1)}, bf16[512,256]{1,0:T(8,128)(2,1)S(1)}, u32[]{:S(2)}, u32[]{:S(2)}) collective-permute-start(bf16[512,256]{1,0:T(8,128)(2,1)S(1)} %get-tuple-element.41), channel_id=1, source_target_pairs={{0,6},{1,7},{2,0},{3,1},{4,2},{5,3},{6,4},{7,5},{8,14},{9,15},{10,... | collective-permute-start | bytes 786440 | tf_op jit(solution)/shard_map/ppermute | solution.py:33
  90.1 4.9 %collective-permute-done.14 = bf16[576,256]{1,0:T(8,128)(2,1)S(1)} collective-permute-done((bf16[576,256]{1,0:T(8,128)(2,1)S(1)}, bf16[576,256]{1,0:T(8,128)(2,1)S(1)}, u32[]{:S(2)}, u32[]{:S(2)}) %collective-permute-start.14) | collective-permute-done | bytes 294944 | tf_op jit(solution)/shard_map/ppermute | solution.py:33
  95.0 3.1 %collective-permute-start.15 = (bf16[576,256]{1,0:T(8,128)(2,1)S(1)}, bf16[576,256]{1,0:T(8,128)(2,1)S(1)}, u32[]{:S(2)}, u32[]{:S(2)}) collective-permute-start(bf16[576,256]{1,0:T(8,128)(2,1)S(1)} %add_convert_fusion), channel_id=1, source_target_pairs={{0,6},{1,7},{2,0},{3,1},{4,2},{5,3},{6,4},{7,5},{8,14},{9,15},{10,... | collective-permute-start | bytes 884744 | tf_op jit(solution)/shard_map/ppermute | solution.py:33
  98.3 2.3 %collective-permute-done.12.refs_2_ = bf16[512,256]{1,0:T(8,128)(2,1)S(1)} collective-permute-done((bf16[512,256]{1,0:T(8,128)(2,1)S(1)}, bf16[512,256]{1,0:T(8,128)(2,1)S(1)}, u32[]{:S(2)}, u32[]{:S(2)}) %collective-permute-start.12) | collective-permute-done | bytes 262176 | tf_op jit(solution)/shard_map/ppermute | solution.py:33
  100.6 3.0 %collective-permute-done.13.refs_4_ = bf16[576,256]{1,0:T(8,128)(2,1)S(1)} collective-permute-done((bf16[576,256]{1,0:T(8,128)(2,1)S(1)}, bf16[576,256]{1,0:T(8,128)(2,1)S(1)}, u32[]{:S(2)}, u32[]{:S(2)}) %collective-permute-start.13) | collective-permute-done | bytes 294944 | tf_op jit(solution)/shard_map/ppermute | solution.py:33
  103.6 4.2 %collective-permute-done.11.refs_1_ = bf16[512,256]{1,0:T(8,128)(2,1)S(1)} collective-permute-done((bf16[512,256]{1,0:T(8,128)(2,1)S(1)}, bf16[512,256]{1,0:T(8,128)(2,1)S(1)}, u32[]{:S(2)}, u32[]{:S(2)}) %collective-permute-start.11) | collective-permute-done | bytes 262176 | tf_op jit(solution)/shard_map/ppermute | solution.py:33
  107.9 1.0 combine.1
  108.9 1.7 %all-to-all-done.2 = bf16[32,24,576]{2,1,0:T(8,128)(2,1)S(1)} async-done(((bf16[32,24,576]{2,1,0:T(8,128)(2,1)}), bf16[32,24,576]{2,1,0:T(8,128)(2,1)S(1)}, u32[]{:S(2)}, u32[]{:S(2)}) %all-to-all-start.2) | async-done | bytes 884768 | tf_op jit(solution)/shard_map/all_to_all | solution.py:408
  110.5 1.2 %owner_sum.1 = bf16[256,576]{1,0:T(8,128)(2,1)} custom-call(bf16[768,256]{1,0:T(8,128)(2,1)S(1)} %copy-done.4, bf16[768,576]{1,0:T(8,128)(2,1)S(1)} %bitcast.16), custom_call_target="tpu_custom_call" | custom-call | tf_op jit(solution)/shard_map/owner_sum/pallas_call | solution.py:254
  (57 shorter events, 1.9 us)
Async XLA Ops:
  2.5 20.2 %all-to-all-start = ((s32[32,1,32]{2,1,0:T(1,128)}), s32[32,1,32]{2,1,0:T(1,128)S(1)}, u32[]{:S(2)}, u32[]{:S(2)}) async-start(s32[32,1,32]{2,1,0:T(1,128)} %reshape.173), calls=%async_computation | async-start | bytes 32768 | tf_op jit(solution)/shard_map/all_to_all | solution.py:302
  17.8 42.1 %copy-start = (s32[96,128]{1,0:T(8,128)}, s32[96,128]{1,0:T(8,128)S(1)}, u32[]{:S(2)}) copy-start(s32[96,128]{1,0:T(8,128)S(1)} %pad.9.refs_0_.plan_ref.refs_14_) | copy-start | bytes 147460
  25.5 31.1 %all-to-all-start.1 = ((bf16[32,24,576]{2,1,0:T(8,128)(2,1)}), bf16[32,24,576]{2,1,0:T(8,128)(2,1)S(1)}, u32[]{:S(2)}, u32[]{:S(2)}) async-start(bf16[32,24,576]{2,1,0:T(8,128)(2,1)} %bitcast.3), calls=%async_computation.1 | async-start | bytes 1966080 | tf_op jit(solution)/shard_map/all_to_all | solution.py:344
  30.6 9.6 %collective-permute-start = (bf16[256,576]{1,0:T(8,128)(2,1)S(1)}, bf16[256,576]{1,0:T(8,128)(2,1)S(1)}, u32[]{:S(2)}, u32[]{:S(2)}) collective-permute-start(bf16[256,576]{1,0:T(8,128)(2,1)S(1)} %get-tuple-element.28.refs_0_.refs_6_), channel_id=1, source_target_pairs={{0,2},{1,3},{2,4},{3,5},{4,6},{5,7},{6,0},{7,1},{8,10},{9,11},{10,... | collective-permute-start | bytes 884744 | tf_op jit(solution)/shard_map/ppermute | solution.py:33
  32.1 9.8 %collective-permute-start.4 = (bf16[256,512]{1,0:T(8,128)(2,1)S(1)}, bf16[256,512]{1,0:T(8,128)(2,1)S(1)}, u32[]{:S(2)}, u32[]{:S(2)}) collective-permute-start(bf16[256,512]{1,0:T(8,128)(2,1)S(1)} %get-tuple-element.29.refs_4_.refs_10_), channel_id=1, source_target_pairs={{0,6},{1,7},{2,0},{3,1},{4,2},{5,3},{6,4},{7,5},{8,14},{9,15},{10,... | collective-permute-start | bytes 786440 | tf_op jit(solution)/shard_map/ppermute | solution.py:33
  33.9 20.5 %collective-permute-start.2 = (bf16[256,576]{1,0:T(8,128)(2,1)S(1)}, bf16[256,576]{1,0:T(8,128)(2,1)S(1)}, u32[]{:S(2)}, u32[]{:S(2)}) collective-permute-start(bf16[256,576]{1,0:T(8,128)(2,1)S(1)} %get-tuple-element.28.refs_0_.refs_6_), channel_id=1, source_target_pairs={{0,6},{1,7},{2,0},{3,1},{4,2},{5,3},{6,4},{7,5},{8,14},{9,15},{10,... | collective-permute-start | bytes 884744 | tf_op jit(solution)/shard_map/ppermute | solution.py:33
  40.2 14.2 %collective-permute-start.1 = (bf16[256,576]{1,0:T(8,128)(2,1)S(1)}, bf16[256,576]{1,0:T(8,128)(2,1)S(1)}, u32[]{:S(2)}, u32[]{:S(2)}) collective-permute-start(bf16[256,576]{1,0:T(8,128)(2,1)S(1)} %collective-permute-done.refs_0_.refs_1_.refs_7_), channel_id=1, source_target_pairs={{0,2},{1,3},{2,4},{3,5},{4,6},{5,7},{6,0},{7,1},{8,10},{9,11},{10,... | collective-permute-start | bytes 884744 | tf_op jit(solution)/shard_map/ppermute | solution.py:33
  40.5 13.9 %collective-permute-start.3 = (bf16[256,512]{1,0:T(8,128)(2,1)S(1)}, bf16[256,512]{1,0:T(8,128)(2,1)S(1)}, u32[]{:S(2)}, u32[]{:S(2)}) collective-permute-start(bf16[256,512]{1,0:T(8,128)(2,1)S(1)} %get-tuple-element.29.refs_4_.refs_10_), channel_id=1, source_target_pairs={{0,2},{1,3},{2,4},{3,5},{4,6},{5,7},{6,0},{7,1},{8,10},{9,11},{10,... | collective-permute-start | bytes 786440 | tf_op jit(solution)/shard_map/ppermute | solution.py:33
  42.0 12.4 %collective-permute-start.5 = (bf16[256,512]{1,0:T(8,128)(2,1)S(1)}, bf16[256,512]{1,0:T(8,128)(2,1)S(1)}, u32[]{:S(2)}, u32[]{:S(2)}) collective-permute-start(bf16[256,512]{1,0:T(8,128)(2,1)S(1)} %collective-permute-done.4.refs_5_.refs_7_.refs_13_), channel_id=1, source_target_pairs={{0,6},{1,7},{2,0},{3,1},{4,2},{5,3},{6,4},{7,5},{8,14},{9,15},{10,... | collective-permute-start | bytes 786440 | tf_op jit(solution)/shard_map/ppermute | solution.py:33
  57.6 2.4 %collective-permute-start.6 = (bf16[64,8,576]{2,1,0:T(8,128)(2,1)S(1)}, bf16[64,8,576]{2,1,0:T(8,128)(2,1)S(1)}, u32[]{:S(2)}, u32[]{:S(2)}) collective-permute-start(bf16[64,8,576]{2,1,0:T(8,128)(2,1)S(1)} %bitcast.14), channel_id=1, source_target_pairs={{0,1},{1,0},{2,3},{3,2},{4,5},{5,4},{6,7},{7,6},{8,9},{9,8},{10,11... | collective-permute-start | bytes 1769480 | tf_op jit(solution)/shard_map/ppermute | solution.py:358
  61.9 11.9 %copy-start.2 = (f32[4,8,256]{2,1,0:T(8,128)}, f32[4,8,256]{2,1,0:T(8,128)S(1)}, u32[]{:S(2)}) copy-start(f32[4,8,256]{2,1,0:T(8,128)S(1)} %get-tuple-element.31.refs_6_.refs_0_.refs_2_) | copy-start | bytes 98308
  61.9 7.9 %collective-permute-start.9 = (f32[4,8,256]{2,1,0:T(8,128)S(1)}, f32[4,8,256]{2,1,0:T(8,128)S(1)}, u32[]{:S(2)}, u32[]{:S(2)}) collective-permute-start(f32[4,8,256]{2,1,0:T(8,128)S(1)} %get-tuple-element.31.refs_6_.refs_0_.refs_2_), channel_id=1, source_target_pairs={{0,6},{1,7},{2,0},{3,1},{4,2},{5,3},{6,4},{7,5},{8,14},{9,15},{10,... | collective-permute-start | bytes 98312 | tf_op jit(solution)/shard_map/ppermute | solution.py:33
  64.7 5.4 %collective-permute-start.8 = (f32[4,8,256]{2,1,0:T(8,128)S(1)}, f32[4,8,256]{2,1,0:T(8,128)S(1)}, u32[]{:S(2)}, u32[]{:S(2)}) collective-permute-start(f32[4,8,256]{2,1,0:T(8,128)S(1)} %get-tuple-element.31.refs_6_.refs_0_.refs_2_), channel_id=1, source_target_pairs={{0,4},{1,5},{2,6},{3,7},{4,0},{5,1},{6,2},{7,3},{8,12},{9,13},{10,... | collective-permute-start | bytes 98312 | tf_op jit(solution)/shard_map/ppermute | solution.py:33
  65.5 5.1 %collective-permute-start.7 = (f32[4,8,256]{2,1,0:T(8,128)S(1)}, f32[4,8,256]{2,1,0:T(8,128)S(1)}, u32[]{:S(2)}, u32[]{:S(2)}) collective-permute-start(f32[4,8,256]{2,1,0:T(8,128)S(1)} %get-tuple-element.31.refs_6_.refs_0_.refs_2_), channel_id=1, source_target_pairs={{0,2},{1,3},{2,4},{3,5},{4,6},{5,7},{6,0},{7,1},{8,10},{9,11},{10,... | collective-permute-start | bytes 98312 | tf_op jit(solution)/shard_map/ppermute | solution.py:33
  66.4 4.2 %copy-start.1 = (s32[96,128]{1,0:T(8,128)S(1)}, s32[96,128]{1,0:T(8,128)}, u32[]{:S(2)}) copy-start(s32[96,128]{1,0:T(8,128)} %copy-done) | copy-start | bytes 147460
  69.9 3.9 %copy-start.5 = (f32[4,8,256]{2,1,0:T(8,128)}, f32[4,8,256]{2,1,0:T(8,128)S(1)}, u32[]{:S(2)}) copy-start(f32[4,8,256]{2,1,0:T(8,128)S(1)} %collective-permute-done.9.refs_3_.refs_5_) | copy-start | bytes 98308
  70.2 3.6 %copy-start.7 = (f32[4,8,256]{2,1,0:T(8,128)}, f32[4,8,256]{2,1,0:T(8,128)S(1)}, u32[]{:S(2)}) copy-start(f32[4,8,256]{2,1,0:T(8,128)S(1)} %collective-permute-done.8.refs_2_.refs_4_) | copy-start | bytes 98308
  70.7 3.1 %copy-start.9 = (f32[4,8,256]{2,1,0:T(8,128)}, f32[4,8,256]{2,1,0:T(8,128)S(1)}, u32[]{:S(2)}) copy-start(f32[4,8,256]{2,1,0:T(8,128)S(1)} %collective-permute-done.7.refs_1_.refs_3_) | copy-start | bytes 98308
  73.4 3.0 %collective-permute-start.16 = (bf16[32,24,576]{2,1,0:T(8,128)(2,1)S(1)}, bf16[32,24,576]{2,1,0:T(8,128)(2,1)S(1)}, u32[]{:S(2)}, u32[]{:S(2)}) collective-permute-start(bf16[32,24,576]{2,1,0:T(8,128)(2,1)S(1)} %bitcast.20), channel_id=1, source_target_pairs={{0,1},{1,0},{2,3},{3,2},{4,5},{5,4},{6,7},{7,6},{8,9},{9,8},{10,11... | collective-permute-start | bytes 2654216 | tf_op jit(solution)/shard_map/ppermute | solution.py:399
  76.4 6.8 %copy-start.3 = (f32[4,8,256]{2,1,0:T(8,128)S(1)}, f32[4,8,256]{2,1,0:T(8,128)}, u32[]{:S(2)}) copy-start(f32[4,8,256]{2,1,0:T(8,128)} %copy-done.2) | copy-start | bytes 98308
  76.4 6.8 %copy-start.6 = (f32[4,8,256]{2,1,0:T(8,128)S(1)}, f32[4,8,256]{2,1,0:T(8,128)}, u32[]{:S(2)}) copy-start(f32[4,8,256]{2,1,0:T(8,128)} %copy-done.5) | copy-start | bytes 98308
  76.5 6.8 %copy-start.8 = (f32[4,8,256]{2,1,0:T(8,128)S(1)}, f32[4,8,256]{2,1,0:T(8,128)}, u32[]{:S(2)}) copy-start(f32[4,8,256]{2,1,0:T(8,128)} %copy-done.7) | copy-start | bytes 98308
  76.5 6.8 %copy-start.10 = (f32[4,8,256]{2,1,0:T(8,128)S(1)}, f32[4,8,256]{2,1,0:T(8,128)}, u32[]{:S(2)}) copy-start(f32[4,8,256]{2,1,0:T(8,128)} %copy-done.9) | copy-start | bytes 98308
  77.7 32.9 %all-to-all-start.2 = ((bf16[32,24,576]{2,1,0:T(8,128)(2,1)}), bf16[32,24,576]{2,1,0:T(8,128)(2,1)S(1)}, u32[]{:S(2)}, u32[]{:S(2)}) async-start(bf16[32,24,576]{2,1,0:T(8,128)(2,1)} %fusion.1), calls=%async_computation.2 | async-start | bytes 1966080 | tf_op jit(solution)/shard_map/all_to_all | solution.py:408
  85.0 25.5 %copy-start.4 = (bf16[768,256]{1,0:T(8,128)(2,1)S(1)}, bf16[768,256]{1,0:T(8,128)(2,1)}, u32[]{:S(2)}) copy-start(bf16[768,256]{1,0:T(8,128)(2,1)} %get-tuple-element.48.hot_ref) | copy-start | bytes 1179652
  85.0 10.0 %collective-permute-start.14 = (bf16[576,256]{1,0:T(8,128)(2,1)S(1)}, bf16[576,256]{1,0:T(8,128)(2,1)S(1)}, u32[]{:S(2)}, u32[]{:S(2)}) collective-permute-start(bf16[576,256]{1,0:T(8,128)(2,1)S(1)} %get-tuple-element.45), channel_id=1, source_target_pairs={{0,6},{1,7},{2,0},{3,1},{4,2},{5,3},{6,4},{7,5},{8,14},{9,15},{10,... | collective-permute-start | bytes 884744 | tf_op jit(solution)/shard_map/ppermute | solution.py:33
  86.9 11.2 %collective-permute-start.10 = (bf16[512,256]{1,0:T(8,128)(2,1)S(1)}, bf16[512,256]{1,0:T(8,128)(2,1)S(1)}, u32[]{:S(2)}, u32[]{:S(2)}) collective-permute-start(bf16[512,256]{1,0:T(8,128)(2,1)S(1)} %get-tuple-element.40), channel_id=1, source_target_pairs={{0,2},{1,3},{2,4},{3,5},{4,6},{5,7},{6,0},{7,1},{8,10},{9,11},{10,... | collective-permute-start | bytes 786440 | tf_op jit(solution)/shard_map/ppermute | solution.py:33
  87.1 13.5 %collective-permute-start.12 = (bf16[512,256]{1,0:T(8,128)(2,1)S(1)}, bf16[512,256]{1,0:T(8,128)(2,1)S(1)}, u32[]{:S(2)}, u32[]{:S(2)}) collective-permute-start(bf16[512,256]{1,0:T(8,128)(2,1)S(1)} %get-tuple-element.41), channel_id=1, source_target_pairs={{0,6},{1,7},{2,0},{3,1},{4,2},{5,3},{6,4},{7,5},{8,14},{9,15},{10,... | collective-permute-start | bytes 786440 | tf_op jit(solution)/shard_map/ppermute | solution.py:33
  90.1 13.5 %collective-permute-start.13 = (bf16[576,256]{1,0:T(8,128)(2,1)S(1)}, bf16[576,256]{1,0:T(8,128)(2,1)S(1)}, u32[]{:S(2)}, u32[]{:S(2)}) collective-permute-start(bf16[576,256]{1,0:T(8,128)(2,1)S(1)} %get-tuple-element.43), channel_id=1, source_target_pairs={{0,2},{1,3},{2,4},{3,5},{4,6},{5,7},{6,0},{7,1},{8,10},{9,11},{10,... | collective-permute-start | bytes 884744 | tf_op jit(solution)/shard_map/ppermute | solution.py:33
  95.0 12.8 %collective-permute-start.15 = (bf16[576,256]{1,0:T(8,128)(2,1)S(1)}, bf16[576,256]{1,0:T(8,128)(2,1)S(1)}, u32[]{:S(2)}, u32[]{:S(2)}) collective-permute-start(bf16[576,256]{1,0:T(8,128)(2,1)S(1)} %add_convert_fusion), channel_id=1, source_target_pairs={{0,6},{1,7},{2,0},{3,1},{4,2},{5,3},{6,4},{7,5},{8,14},{9,15},{10,... | collective-permute-start | bytes 884744 | tf_op jit(solution)/shard_map/ppermute | solution.py:33
  98.2 9.7 %collective-permute-start.11 = (bf16[512,256]{1,0:T(8,128)(2,1)S(1)}, bf16[512,256]{1,0:T(8,128)(2,1)S(1)}, u32[]{:S(2)}, u32[]{:S(2)}) collective-permute-start(bf16[512,256]{1,0:T(8,128)(2,1)S(1)} %add_convert_fusion.1), channel_id=1, source_target_pairs={{0,2},{1,3},{2,4},{3,5},{4,6},{5,7},{6,0},{7,1},{8,10},{9,11},{10,... | collective-permute-start | bytes 786440 | tf_op jit(solution)/shard_map/ppermute | solution.py:33

commit v5 on v4

--- a/solution.py
+++ b/solution.py
@@ -53,6 +53,39 @@
 
 def dot32(a, b):
     return jnp.dot(a, b, preferred_element_type=f32)
+
+
+def to_parcels(rows, shape, slot_limit):
+    owners, height, lanes = shape
+    count = rows.shape[0] // owners
+    tokens = count // slot_limit
+    full = rows.shape[1] // lanes
+    parts = [
+        rows[:, c * lanes : (c + 1) * lanes].reshape(owners, count, lanes) for c in range(full)
+    ]
+    tail = rows[:, full * lanes :].reshape(owners, count, rows.shape[1] - full * lanes)
+    tails = [tail[:, j * tokens : (j + 1) * tokens] for j in range(slot_limit)]
+    tails += [jnp.zeros_like(tails[0])] * (slot_limit % 2)
+    for j in range(0, len(tails), 2):
+        parts.append(jnp.concatenate(tails[j : j + 2], axis=2))
+    return jnp.concatenate(parts, axis=1).astype(bf16)
+
+
+def from_parcels(parcel_ref, count, slot_limit):
+    owners, height, lanes = parcel_ref.shape
+    tokens = count // slot_limit
+    parcels = parcel_ref[...].astype(f32)
+    full = height // count
+    parts = [
+        parcels[:, c * count : (c + 1) * count].reshape(owners * count, lanes) for c in range(full)
+    ]
+    tails = []
+    for j in range(slot_limit):
+        first = full * count + j // 2 * tokens
+        pair = parcels[:, first : first + tokens]
+        tails.append(pair[:, :, j % 2 * (lanes // 2) : (j % 2 + 1) * (lanes // 2)])
+    parts.append(jnp.concatenate(tails, axis=1).reshape(owners * count, lanes // 2))
+    return jnp.concatenate(parts, axis=1).astype(bf16)
 
 
 def pack_kernel(tokens, slot_limit, asked_ref, cache_ref, q_ref, g_ref, *refs):
@@ -78,28 +111,28 @@
         slot += dot32(bit_matrix(row == lane * slot_limit + j), level)
     slot = slot.astype(bf16)
 
-    def hot_matrix(size, offset):
-        row, lane = iotas((block_count, block_count * size))
-        start = row * size
-        hot = expand(dot32(slot, bit_matrix((lane >= start) & (lane < start + size))), tokens)
-        row, lane = iotas(hot.shape)
-        same = (row & (tokens - 1)) + offset == (lane & (size - 1))
-        return jnp.where(same, hot, 0.0).astype(bf16)
-
-    hot_ref[...] = hot_matrix(tokens, 0)
+    row, lane = iotas((block_count, block_count * tokens))
+    start = row * tokens
+    hot = expand(dot32(slot, bit_matrix((lane >= start) & (lane < start + tokens))), tokens)
+    row, lane = iotas(hot.shape)
+    hot = jnp.where((row & (tokens - 1)) == (lane & (tokens - 1)), hot, 0.0).astype(bf16)
+    hot_ref[...] = hot
     copies.append(pltpu.make_async_copy(hot_ref, hot_out, sems.at[3]))
     copies[3].start()
-    hot = hot_matrix(pair, tp % CORES * tokens)
     copies[0].wait()
-    rows = rows_ref[...].reshape(block_count * pair, rows_ref.shape[2])
-    out_ref[...] = dot32(hot, rows).astype(bf16)
+    rows = rows_ref[...].astype(f32)
+    rows = jnp.where(tp % CORES == 0, rows[:, :tokens], rows[:, tokens:])
+    rows = rows.reshape(block_count * tokens, rows_ref.shape[2]).astype(bf16)
+    out_ref[...] = to_parcels(dot32(hot, rows), out_ref.shape, slot_limit)
     for copy in copies[1:]:
         copy.wait()
 
 
-def owner_kernel(hot_ref, rows_ref, out_ref):
+def owner_kernel(slot_limit, hot_ref, parcel_ref, out_ref):
+    count = hot_ref.shape[0] // parcel_ref.shape[0]
+    rows = from_parcels(parcel_ref, count, slot_limit)
     total = lax.dot_general(
-        hot_ref[...], rows_ref[...], (((0,), (0,)), ((), ())), preferred_element_type=f32
+        hot_ref[...], rows, (((0,), (0,)), ((), ())), preferred_element_type=f32
     )
     out_ref[...] = total.astype(bf16)
 
@@ -110,9 +143,11 @@
     return bit_matrix(ids * tokens + (row & (tokens - 1)) == lane)
 
 
-def unpack_kernel(tokens, plan_ref, rows_ref, *refs):
-    hot = slot_hot(plan_ref[:USED, 1:2], tokens, rows_ref.shape[0])
-    refs[-1][...] = dot32(hot, rows_ref[...]).astype(bf16)
+def unpack_kernel(tokens, slot_limit, plan_ref, parcel_ref, *refs):
+    count = slot_limit * tokens
+    hot = slot_hot(plan_ref[:USED, 1:2], tokens, parcel_ref.shape[0] * count)
+    rows = from_parcels(parcel_ref, count, slot_limit)
+    refs[-1][...] = dot32(hot, rows).astype(bf16)
 
 
 def score_half(tokens, half, plan_ref, key_ref, q_refs, g_refs, p_ref, gw_ref):
@@ -163,10 +198,7 @@
 
 def local_kernel(*refs):
     key_refs, p_refs, gw_refs = refs[:CORES], refs[CORES : 2 * CORES], refs[2 * CORES : 3 * CORES]
-    stat_ref, value_ref, grad_out, grad_ref, sems = refs[3 * CORES :]
-    copies = [
-        pltpu.make_async_copy(grad_ref.at[k], grad_out.at[k], sems.at[k]) for k in range(XN)
-    ]
+    stat_ref, value_ref, grad_ref = refs[3 * CORES :]
     keys_t = [key_ref[...].T for key_ref in key_refs]
     for k in range(XN):
         stats = stat_ref[k]
@@ -178,9 +210,6 @@
             grad.append(dot32(keys_t[h], (p * (gw_refs[h][k] - inner)).astype(bf16)))
         value_ref[k] = (value[0] + value[1]).astype(bf16)
         grad_ref[k] = (grad[0] + grad[1]).astype(bf16)
-        copies[k].start()
-    for copy in copies:
-        copy.wait()
 
 
 def row_stats(stat_refs, k):
@@ -192,10 +221,16 @@
     return stats[0], inner, factors[0] / total
 
 
-def key_grad_kernel(tokens, half, *refs):
+def key_grad_kernel(tokens, slot_limit, half, *refs):
     p_ref, gw_ref = refs[:2]
     stat_refs, q_refs, g_refs = (refs[2 + i * XN : 2 + (i + 1) * XN] for i in range(3))
-    last_ref, sum_ref = refs[2 + 3 * XN], refs[-1]
+    last_ref, part_ref = refs[2 + 3 * XN : 4 + 3 * XN]
+    if half == 0:
+        out_ref, part_out, sum_ref, sem = refs[-4:]
+    else:
+        out_ref, part_out, hot_ref, sum_ref, sem = refs[-5:]
+    copy = pltpu.make_async_copy(part_ref, part_out, sem)
+    copy.start()
     value_width = g_refs[0].shape[1]
     key_grad, value_grad = [], []
     for k in range(XN):
@@ -209,28 +244,33 @@
     sum_ref[:, :value_width] = (key_grad[:, :value_width] + value_grad).astype(bf16)
     sum_ref[:, value_width:] = key_grad[:, value_width:].astype(bf16)
     if half == 0:
-        hot_ref, out_ref = last_ref, refs[-2]
+        hot_ref = last_ref
     else:
-        out_ref, hot_ref = refs[-3:-1]
         hot_ref[...] = slot_hot(last_ref[:, 0:1], tokens, sum_ref.shape[0])
-    out_ref[...] = dot32(hot_ref[...], sum_ref[...]).astype(bf16)
-
-
-def scale_kernel(*refs):
-    stat_refs, (value_ref, grad_in), outs = refs[:XN], refs[XN : XN + 2], refs[XN + 2 : -2]
-    grad_ref, sems = refs[-2:]
-    att_refs, qg_refs = outs[:XN], outs[XN:]
-    copies = [pltpu.make_async_copy(grad_in.at[k], grad_ref.at[k], sems.at[k]) for k in range(XN)]
-    for copy in copies:
+    rows = dot32(hot_ref[...], sum_ref[...])
+    out_ref[...] = to_parcels(rows, out_ref.shape, slot_limit)
+    copy.wait()
+
+
+def scale_kernel(blocks, *refs):
+    stat_refs, ins, outs = refs[:XN], refs[XN : XN + 2], refs[XN + 2 : -3]
+    value_ref, grad_ref, sems = refs[-3:]
+    copies = {
+        (k, i): pltpu.make_async_copy(src.at[k], dst.at[k], sems.at[k, i])
+        for k in blocks
+        for i, (src, dst) in enumerate(zip(ins, (value_ref, grad_ref)))
+    }
+    for copy in copies.values():
         copy.start()
-    for k in range(XN):
-        copies[k].wait()
+    for att_ref, qg_ref, k in zip(outs[::2], outs[1::2], blocks):
+        copies[k, 0].wait()
+        copies[k, 1].wait()
         mine, inner, factor = row_stats(stat_refs, k)
         shift = mine[2:3] / mine[1:2] - inner
         value = value_ref[k].astype(f32)
-        att_refs[k][...] = (value[: att_refs[k].shape[0]] * factor).astype(bf16)
+        att_ref[...] = (value[: att_ref.shape[0]] * factor).astype(bf16)
         qg = (grad_ref[k].astype(f32) + value * shift) * (factor * score_scale)
-        qg_refs[k][...] = qg.astype(bf16)
+        qg_ref[...] = qg.astype(bf16)
 
 
 def combine_kernel(*refs):
@@ -294,7 +334,9 @@
     half = USED * tokens
     keys = CORES * half
     held = block_count * tokens
-    parcels = (owners, slot_limit * tokens, width)
+    whole, tail = divmod(width, 128)
+    height = (whole * slot_limit + -(-slot_limit * tail // 128)) * tokens
+    parcels = (owners, height, 128)
 
     block_range = jnp.arange(owners * block_count, dtype=jnp.int32)
     wanted = jnp.any(selected.reshape(-1)[:, None] == block_range[None, :], axis=0)
@@ -325,7 +367,7 @@
     packed, asked_hot, q0, g0 = call(
         functools.partial(pack_kernel, tokens, slot_limit),
         [
-            shaped((slots * tokens, width)),
+            shaped(parcels),
             shaped((slots * tokens, held)),
             shaped((rows, width)),
             shaped((rows, value_width)),
@@ -341,7 +383,7 @@
         far_in=3,
         far_out=(1,),
     )
-    fetched = lax.all_to_all(packed.reshape(parcels), "ctx", 0, 0, tiled=True)
+    fetched = lax.all_to_all(packed, "ctx", 0, 0, tiled=True)
 
     q1, q3 = send_x(q0, 1), send_x(q0, -1)
     g1, g3 = send_x(g0, 1), send_x(g0, -1)
@@ -349,9 +391,9 @@
     gathered = [q0, q1, q2, q3, g0, g1, g2, g3]
 
     (own_keys,) = call(
-        functools.partial(unpack_kernel, tokens),
+        functools.partial(unpack_kernel, tokens, slot_limit),
         [shaped((half, width))],
-        [plan, fetched.reshape(slots * tokens, width)],
+        [plan, fetched],
         "unpack",
         unused=(q1, q2, q3, g1, g2, g3),
     )
@@ -376,47 +418,52 @@
     )
     all_stats = [stats] + [send_x(stats, k) for k in range(1, XN)]
     part_shape = (XN, width, rows)
-    part_scratch = [pltpu.VMEM(part_shape, bf16), pltpu.SemaphoreType.DMA((XN,))]
+    part_scratch = [
+        pltpu.VMEM(part_shape, bf16),
+        pltpu.VMEM(part_shape, bf16),
+        pltpu.SemaphoreType.DMA((XN, 2)),
+    ]
     value_part, grad_part = call(
         local_kernel,
         [shaped(part_shape)] * 2,
         [own_keys, other_keys, own_p, other_p, own_gw, other_gw, stats],
         "local",
+    )
+
+    grad_shape = shaped(parcels)
+    sum_scratch = [pltpu.VMEM((half, width), bf16), pltpu.SemaphoreType.DMA(())]
+    other_grad, value_part, spread_hot = call(
+        functools.partial(key_grad_kernel, tokens, slot_limit, 1),
+        [grad_shape, shaped(part_shape), shaped((slots * tokens, half))],
+        [other_p, other_gw, *all_stats, *gathered, plan, value_part],
+        "other_grads",
         far_out=(1,),
-        scratch=part_scratch,
-    )
-
-    grad_shape = shaped((slots * tokens, width))
-    sum_scratch = [pltpu.VMEM((half, width), bf16)]
-    other_grad, spread_hot = call(
-        functools.partial(key_grad_kernel, tokens, 1),
-        [grad_shape, shaped((slots * tokens, half))],
-        [other_p, other_gw, *all_stats, *gathered, plan],
-        "other_grads",
-        unused=(value_part,),
         scratch=sum_scratch,
     )
-    from_core = lax.ppermute(other_grad.reshape(parcels), "tp", CORE_SWAP)
-    (own_grad,) = call(
-        functools.partial(key_grad_kernel, tokens, 0),
-        [grad_shape],
-        [own_p, own_gw, *all_stats, *gathered, spread_hot],
+    from_core = lax.ppermute(other_grad, "tp", CORE_SWAP)
+    own_grad, grad_part = call(
+        functools.partial(key_grad_kernel, tokens, slot_limit, 0),
+        [grad_shape, shaped(part_shape)],
+        [own_p, own_gw, *all_stats, *gathered, spread_hot, grad_part],
         "own_grads",
+        far_out=(1,),
         scratch=sum_scratch,
     )
-    returning = (own_grad.reshape(parcels).astype(f32) + from_core.astype(f32)).astype(bf16)
+    returning = (own_grad.astype(f32) + from_core.astype(f32)).astype(bf16)
     returned = lax.all_to_all(returning, "ctx", 0, 0, tiled=True)
 
-    out_shapes = [(value_width, rows)] * XN + [(width, rows)] * XN
-    outs = call(
-        scale_kernel,
-        [shaped(x) for x in out_shapes],
-        [*all_stats, value_part, grad_part],
-        "scale",
-        far_in=1,
-        scratch=part_scratch,
-    )
-    att, qg = outs[:XN], outs[XN:]
+    att, qg = {}, {}
+    for blocks in ((2,), (3, 1, 0)):
+        outs = call(
+            functools.partial(scale_kernel, blocks),
+            [shaped((value_width, rows)), shaped((width, rows))] * len(blocks),
+            [*all_stats, value_part, grad_part],
+            "scale",
+            far_in=2,
+            scratch=part_scratch,
+        )
+        att.update(zip(blocks, outs[::2]))
+        qg.update(zip(blocks, outs[1::2]))
     att_far, qg_far = send_x(att[2], 1), send_x(qg[2], -1)
     qg_left, att_right = send_x(qg[3], 1), send_x(att[1], -1)
     att_left = (att[3].astype(f32) + att_far.astype(f32)).astype(bf16)
@@ -428,9 +475,9 @@
         "combine",
     )
     (cache_grad,) = call(
-        owner_kernel,
+        functools.partial(owner_kernel, slot_limit),
         [shaped((held, width))],
-        [asked_hot, returned.reshape(slots * tokens, width)],
+        [asked_hot, returned],
         "owner_sum",
     )
     return (

time: 112 us -> 110 us (0.982)
  waiting for transfers between devices: 38.9 us -> 35.2 us
  starting transfers between devices: 44.7 us -> 46.4 us
    all_to_all x1, waiting for transfers between devices: 2.25 us -> 0.85 us  [on_device(): fetched = lax.all_to_all(packed, 'ctx', 0, 0, tiled=True)]
    all_to_all x1, starting transfers between devices: 5.57 us -> 6.74 us  [on_device(): returned = lax.all_to_all(returning, 'ctx', 0, 0, tiled=True)]
    ppermute x15, waiting for transfers between devices: 30 us -> 28.9 us  [send_x(): return lax.ppermute(value, 'tp', x_shift(k % XN))]
    all_to_all x1, waiting for transfers between devices: 1.66 us -> 0.5 us  [on_device(): returned = lax.all_to_all(returning, 'ctx', 0, 0, tiled=True)]
    pallas_call x10 -> x11, Pallas kernels: 20.4 us -> 20.6 us  [call(): pl.pallas_call(kernel, out_shape=[pltpu.HBM(x.shape, x.dtype) if i in far...]
where the time goes in v5:
time: 110 us
  starting transfers between devices  46.4 us (42%)
  waiting for transfers between devices  35.2 us (32%)
  Pallas kernels  20.6 us (19%)
  other arithmetic  4.3 us (4%)
  local copies, waits for them, and re-layouts  2.41 us (2%)
    ppermute x15, waiting for transfers between devices, send_x(): return lax.ppermute(value, 'tp', x_shift(k % XN))  28.9 us
    ppermute x15, starting transfers between devices, send_x(): return lax.ppermute(value, 'tp', x_shift(k % XN))  22.4 us
    pallas_call x11, Pallas kernels, call(): pl.pallas_call(kernel, out_shape=[pltpu.HBM(x.shape, x.dtype) if i in far...  20.6 us
    all_to_all x1, starting transfers between devices, on_device(): lax.all_to_all(wanted.astype(jnp.int32)[:, None, :], 'ctx', split_axis=0,...  11.7 us
    all_to_all x1, starting transfers between devices, on_device(): returned = lax.all_to_all(returning, 'ctx', 0, 0, tiled=True)  6.74 us
    all_to_all x1, starting transfers between devices, on_device(): fetched = lax.all_to_all(packed, 'ctx', 0, 0, tiled=True)  5.03 us
    all_to_all x1, waiting for transfers between devices, on_device(): lax.all_to_all(wanted.astype(jnp.int32)[:, None, :], 'ctx', split_axis=0,...  4.8 us
  transfers between devices with their start and end apart: 20, of which 12 were waited for; matrix products, arithmetic and copies ran while one was open for 3% of the time, Pallas kernels for 10%

profile of v5, /device:TPU:8, one launch (start us, length us, event | category | flops | bytes accessed | tf_op | source)
XLA Modules:
  0.0 109.8 jit_solution(9043206216901526901)
XLA Ops:
  0.6 0.8 eq.26
  1.4 0.4 fusion
  1.8 0.7 reshape.154
  2.5 11.7 %all-to-all-start = ((s32[32,1,32]{2,1,0:T(1,128)}), s32[32,1,32]{2,1,0:T(1,128)S(1)}, u32[]{:S(2)}, u32[]{:S(2)}) async-start(s32[32,1,32]{2,1,0:T(1,128)} %reshape.154), calls=%async_computation | async-start | bytes 32768 | tf_op jit(solution)/shard_map/all_to_all | solution.py:344
  14.3 0.2 reduce_window_sum.18
  14.5 0.2 fusion.2
  15.8 0.9 compare_reduce_fusion
  16.9 0.7 fusion.4
  17.8 4.8 %all-to-all-done.asked_ref = s32[32,1,32]{2,1,0:T(1,128)S(1)} async-done(((s32[32,1,32]{2,1,0:T(1,128)}), s32[32,1,32]{2,1,0:T(1,128)S(1)}, u32[]{:S(2)}, u32[]{:S(2)}) %all-to-all-start) | async-done | bytes 4128 | tf_op jit(solution)/shard_map/all_to_all | solution.py:344
  22.6 2.6 %pack.1 = (bf16[32,112,128]{2,1,0:T(8,128)(2,1)}, bf16[768,256]{1,0:T(8,128)(2,1)}, bf16[256,576]{1,0:T(8,128)(2,1)S(1)}, bf16[256,512]{1,0:T(8,128)(2,1)S(1)}) custom-call(s32[32,1,32]{2,1,0:T(1,128)S(1)} %all-to-all-done.asked_ref, bf16[32,64,576]{2,1,0:T(8,128)(2,1)} %cache_ref.1, bf16[256,576]{1,0:T(8,128)(2,1)} %bitcast.11, bf16[256,512]{1,0:T(8,128)(2,1)} %bitcast.13, ...), custom_call_target="tpu_custom_call" | custom-call | tf_op jit(solution)/shard_map/pack/pallas_call | solution.py:294
  25.3 5.0 %all-to-all-start.1 = ((bf16[32,112,128]{2,1,0:T(8,128)(2,1)}), bf16[32,112,128]{2,1,0:T(8,128)(2,1)S(1)}, u32[]{:S(2)}, u32[]{:S(2)}) async-start(bf16[32,112,128]{2,1,0:T(8,128)(2,1)} %get-tuple-element.30), calls=%async_computation.1 | async-start | bytes 1835008 | tf_op jit(solution)/shard_map/all_to_all | solution.py:386
  30.3 1.6 %collective-permute-start = (bf16[256,576]{1,0:T(8,128)(2,1)S(1)}, bf16[256,576]{1,0:T(8,128)(2,1)S(1)}, u32[]{:S(2)}, u32[]{:S(2)}) collective-permute-start(bf16[256,576]{1,0:T(8,128)(2,1)S(1)} %get-tuple-element.31.refs_0_.refs_6_), channel_id=1, source_target_pairs={{0,2},{1,3},{2,4},{3,5},{4,6},{5,7},{6,0},{7,1},{8,10},{9,11},{10,... | collective-permute-start | bytes 884744 | tf_op jit(solution)/shard_map/ppermute | solution.py:33
  31.9 1.7 %collective-permute-start.4 = (bf16[256,512]{1,0:T(8,128)(2,1)S(1)}, bf16[256,512]{1,0:T(8,128)(2,1)S(1)}, u32[]{:S(2)}, u32[]{:S(2)}) collective-permute-start(bf16[256,512]{1,0:T(8,128)(2,1)S(1)} %get-tuple-element.32.refs_4_.refs_10_), channel_id=1, source_target_pairs={{0,6},{1,7},{2,0},{3,1},{4,2},{5,3},{6,4},{7,5},{8,14},{9,15},{10,... | collective-permute-start | bytes 786440 | tf_op jit(solution)/shard_map/ppermute | solution.py:33
  33.6 1.5 %collective-permute-start.2 = (bf16[256,576]{1,0:T(8,128)(2,1)S(1)}, bf16[256,576]{1,0:T(8,128)(2,1)S(1)}, u32[]{:S(2)}, u32[]{:S(2)}) collective-permute-start(bf16[256,576]{1,0:T(8,128)(2,1)S(1)} %get-tuple-element.31.refs_0_.refs_6_), channel_id=1, source_target_pairs={{0,6},{1,7},{2,0},{3,1},{4,2},{5,3},{6,4},{7,5},{8,14},{9,15},{10,... | collective-permute-start | bytes 884744 | tf_op jit(solution)/shard_map/ppermute | solution.py:33
  35.2 4.7 %collective-permute-done.refs_0_.refs_1_.refs_7_ = bf16[256,576]{1,0:T(8,128)(2,1)S(1)} collective-permute-done((bf16[256,576]{1,0:T(8,128)(2,1)S(1)}, bf16[256,576]{1,0:T(8,128)(2,1)S(1)}, u32[]{:S(2)}, u32[]{:S(2)}) %collective-permute-start) | collective-permute-done | bytes 294944 | tf_op jit(solution)/shard_map/ppermute | solution.py:33
  39.9 0.3 collective-permute-start.1
  40.2 1.5 %collective-permute-start.3 = (bf16[256,512]{1,0:T(8,128)(2,1)S(1)}, bf16[256,512]{1,0:T(8,128)(2,1)S(1)}, u32[]{:S(2)}, u32[]{:S(2)}) collective-permute-start(bf16[256,512]{1,0:T(8,128)(2,1)S(1)} %get-tuple-element.32.refs_4_.refs_10_), channel_id=1, source_target_pairs={{0,2},{1,3},{2,4},{3,5},{4,6},{5,7},{6,0},{7,1},{8,10},{9,11},{10,... | collective-permute-start | bytes 786440 | tf_op jit(solution)/shard_map/ppermute | solution.py:33
  41.7 2.4 %collective-permute-start.5 = (bf16[256,512]{1,0:T(8,128)(2,1)S(1)}, bf16[256,512]{1,0:T(8,128)(2,1)S(1)}, u32[]{:S(2)}, u32[]{:S(2)}) collective-permute-start(bf16[256,512]{1,0:T(8,128)(2,1)S(1)} %collective-permute-done.4.refs_5_.refs_7_.refs_13_), channel_id=1, source_target_pairs={{0,6},{1,7},{2,0},{3,1},{4,2},{5,3},{6,4},{7,5},{8,14},{9,15},{10,... | collective-permute-start | bytes 786440 | tf_op jit(solution)/shard_map/ppermute | solution.py:33
  44.1 10.0 %collective-permute-done.3.refs_3_.refs_5_.refs_11_ = bf16[256,512]{1,0:T(8,128)(2,1)S(1)} collective-permute-done((bf16[256,512]{1,0:T(8,128)(2,1)S(1)}, bf16[256,512]{1,0:T(8,128)(2,1)S(1)}, u32[]{:S(2)}, u32[]{:S(2)}) %collective-permute-start.3) | collective-permute-done | bytes 262176 | tf_op jit(solution)/shard_map/ppermute | solution.py:33
  54.1 0.9 all-to-all-done.1.parcel_ref
  55.0 0.9 unpack.1.key_ref.refs_0_
  55.9 0.3 collective-permute-start.6
  56.2 1.9 %own_scores.1 = (bf16[4,512,256]{2,1,0:T(8,128)(2,1)S(1)}, f32[4,512,256]{2,1,0:T(8,128)S(1)}, f32[4,8,256]{2,1,0:T(8,128)S(1)}) custom-call(s32[96,128]{1,0:T(8,128)S(1)} %pad.9.refs_0_.plan_ref.refs_14_, bf16[512,576]{1,0:T(8,128)(2,1)S(1)} %unpack.1.key_ref.refs_0_, bf16[256,576]{1,0:T(8,128)(2,1)S(1)} %get-tuple-element.31.refs_0_.refs_6_, ...), custom_call_target="tpu_custom_call" | custom-call | tf_op jit(solution)/shard_map/own_scores/pallas_call | solution.py:294
  58.1 0.2 collective-permute-done.6
  58.2 1.9 %other_scores.1 = (bf16[4,512,256]{2,1,0:T(8,128)(2,1)S(1)}, f32[4,512,256]{2,1,0:T(8,128)S(1)}, f32[4,8,256]{2,1,0:T(8,128)S(1)}) custom-call(s32[96,128]{1,0:T(8,128)S(1)} %pad.9.refs_0_.plan_ref.refs_14_, bf16[512,576]{1,0:T(8,128)(2,1)S(1)} %bitcast.9, bf16[256,576]{1,0:T(8,128)(2,1)S(1)} %get-tuple-element.31.refs_0_.refs_6_, ...), custom_call_target="tpu_custom_call" | custom-call | tf_op jit(solution)/shard_map/other_scores/pallas_call | solution.py:294
  60.2 2.8 %collective-permute-start.9 = (f32[4,8,256]{2,1,0:T(8,128)S(1)}, f32[4,8,256]{2,1,0:T(8,128)S(1)}, u32[]{:S(2)}, u32[]{:S(2)}) collective-permute-start(f32[4,8,256]{2,1,0:T(8,128)S(1)} %get-tuple-element.34.refs_6_.refs_2_.refs_0_), channel_id=1, source_target_pairs={{0,6},{1,7},{2,0},{3,1},{4,2},{5,3},{6,4},{7,5},{8,14},{9,15},{10,... | collective-permute-start | bytes 98312 | tf_op jit(solution)/shard_map/ppermute | solution.py:33
  63.0 0.8 collective-permute-start.8
  63.8 0.9 collective-permute-start.7
  64.7 2.6 %local.1 = (bf16[4,576,256]{2,1,0:T(8,128)(2,1)S(1)}, bf16[4,576,256]{2,1,0:T(8,128)(2,1)S(1)}) custom-call(bf16[512,576]{1,0:T(8,128)(2,1)S(1)} %unpack.1.key_ref.refs_0_, bf16[512,576]{1,0:T(8,128)(2,1)S(1)} %bitcast.10, bf16[4,512,256]{2,1,0:T(8,128)(2,1)S(1)} %get-tuple-element.37.refs_2_.refs_0_, ...), custom_call_target="tpu_custom_call" | custom-call | tf_op jit(solution)/shard_map/local/pallas_call | solution.py:294
  67.4 1.1 collective-permute-done.8.refs_4_.refs_2_
  68.4 0.5 collective-permute-done.7.refs_3_.refs_1_
  68.9 2.8 %other_grads.1 = (bf16[32,112,128]{2,1,0:T(8,128)(2,1)S(1)}, bf16[4,576,256]{2,1,0:T(8,128)(2,1)}, bf16[768,512]{1,0:T(8,128)(2,1)S(1)}) custom-call(bf16[4,512,256]{2,1,0:T(8,128)(2,1)S(1)} %get-tuple-element.35.refs_3_.refs_0_, f32[4,512,256]{2,1,0:T(8,128)S(1)} %get-tuple-element.36.refs_5_.refs_1_, ...), custom_call_target="tpu_custom_call" | custom-call | tf_op jit(solution)/shard_map/other_grads/pallas_call | solution.py:294
  71.7 0.3 collective-permute-start.16
  72.0 2.7 %own_grads.1 = (bf16[32,112,128]{2,1,0:T(8,128)(2,1)S(1)}, bf16[4,576,256]{2,1,0:T(8,128)(2,1)}) custom-call(bf16[4,512,256]{2,1,0:T(8,128)(2,1)S(1)} %get-tuple-element.37.refs_2_.refs_0_, f32[4,512,256]{2,1,0:T(8,128)S(1)} %get-tuple-element.38.refs_4_.refs_1_, f32[4,8,256]{2,1,0:T(8,128)S(1)} %get-tuple-element.34.refs_6_.refs_2_.refs_0_, ...), custom_call_target="tpu_custom_call" | custom-call | tf_op jit(solution)/shard_map/own_grads/pallas_call | solution.py:294
  74.7 1.2 %add_convert_fusion = bf16[32,112,128]{2,1,0:T(8,128)(2,1)} fusion(bf16[32,112,128]{2,1,0:T(8,128)(2,1)S(1)} %collective-permute-done.16, bf16[32,112,128]{2,1,0:T(8,128)(2,1)S(1)} %get-tuple-element.55), kind=kLoop, calls=%fused_computation.2 | loop fusion | flops 1835008 | bytes 2752512 | tf_op jit(solution)/shard_map/convert_element_type | solution.py:452
  75.9 6.7 %all-to-all-start.2 = ((bf16[32,112,128]{2,1,0:T(8,128)(2,1)}), bf16[32,112,128]{2,1,0:T(8,128)(2,1)S(1)}, u32[]{:S(2)}, u32[]{:S(2)}) async-start(bf16[32,112,128]{2,1,0:T(8,128)(2,1)} %add_convert_fusion), calls=%async_computation.2 | async-start | bytes 1835008 | tf_op jit(solution)/shard_map/all_to_all | solution.py:453
  82.6 1.3 %scale.3 = (bf16[512,256]{1,0:T(8,128)(2,1)S(1)}, bf16[576,256]{1,0:T(8,128)(2,1)S(1)}) custom-call(f32[4,8,256]{2,1,0:T(8,128)S(1)} %get-tuple-element.34.refs_6_.refs_2_.refs_0_, f32[4,8,256]{2,1,0:T(8,128)S(1)} %collective-permute-done.7.refs_3_.refs_1_, f32[4,8,256]{2,1,0:T(8,128)S(1)} %collective-permute-done.8.refs_4_.refs_2_, ...), custom_call_target="tpu_custom_call" | custom-call | tf_op jit(solution)/shard_map/scale/pallas_call | solution.py:294
  83.9 2.1 %collective-permute-start.14 = (bf16[576,256]{1,0:T(8,128)(2,1)S(1)}, bf16[576,256]{1,0:T(8,128)(2,1)S(1)}, u32[]{:S(2)}, u32[]{:S(2)}) collective-permute-start(bf16[576,256]{1,0:T(8,128)(2,1)S(1)} %get-tuple-element.51), channel_id=1, source_target_pairs={{0,6},{1,7},{2,0},{3,1},{4,2},{5,3},{6,4},{7,5},{8,14},{9,15},{10,... | collective-permute-start | bytes 884744 | tf_op jit(solution)/shard_map/ppermute | solution.py:33
  86.0 1.6 %scale.2 = (bf16[512,256]{1,0:T(8,128)(2,1)S(1)}, bf16[576,256]{1,0:T(8,128)(2,1)S(1)}, bf16[512,256]{1,0:T(8,128)(2,1)S(1)}, bf16[576,256]{1,0:T(8,128)(2,1)S(1...) custom-call(f32[4,8,256]{2,1,0:T(8,128)S(1)} %get-tuple-element.34.refs_6_.refs_2_.refs_0_, ...), custom_call_target="tpu_custom_call" | custom-call | tf_op jit(solution)/shard_map/scale/pallas_call | solution.py:294
  87.7 3.3 %collective-permute-start.12 = (bf16[512,256]{1,0:T(8,128)(2,1)S(1)}, bf16[512,256]{1,0:T(8,128)(2,1)S(1)}, u32[]{:S(2)}, u32[]{:S(2)}) collective-permute-start(bf16[512,256]{1,0:T(8,128)(2,1)S(1)} %get-tuple-element.47), channel_id=1, source_target_pairs={{0,6},{1,7},{2,0},{3,1},{4,2},{5,3},{6,4},{7,5},{8,14},{9,15},{10,... | collective-permute-start | bytes 786440 | tf_op jit(solution)/shard_map/ppermute | solution.py:33
  91.0 2.9 %collective-permute-done.14 = bf16[576,256]{1,0:T(8,128)(2,1)S(1)} collective-permute-done((bf16[576,256]{1,0:T(8,128)(2,1)S(1)}, bf16[576,256]{1,0:T(8,128)(2,1)S(1)}, u32[]{:S(2)}, u32[]{:S(2)}) %collective-permute-start.14) | collective-permute-done | bytes 294944 | tf_op jit(solution)/shard_map/ppermute | solution.py:33
  93.9 3.3 %collective-permute-start.15 = (bf16[576,256]{1,0:T(8,128)(2,1)S(1)}, bf16[576,256]{1,0:T(8,128)(2,1)S(1)}, u32[]{:S(2)}, u32[]{:S(2)}) collective-permute-start(bf16[576,256]{1,0:T(8,128)(2,1)S(1)} %add_convert_fusion.1), channel_id=1, source_target_pairs={{0,6},{1,7},{2,0},{3,1},{4,2},{5,3},{6,4},{7,5},{8,14},{9,15},{10,... | collective-permute-start | bytes 884744 | tf_op jit(solution)/shard_map/ppermute | solution.py:33
  97.4 2.1 %collective-permute-done.12.refs_2_ = bf16[512,256]{1,0:T(8,128)(2,1)S(1)} collective-permute-done((bf16[512,256]{1,0:T(8,128)(2,1)S(1)}, bf16[512,256]{1,0:T(8,128)(2,1)S(1)}, u32[]{:S(2)}, u32[]{:S(2)}) %collective-permute-start.12) | collective-permute-done | bytes 262176 | tf_op jit(solution)/shard_map/ppermute | solution.py:33
  99.5 3.1 %collective-permute-done.13.refs_4_ = bf16[576,256]{1,0:T(8,128)(2,1)S(1)} collective-permute-done((bf16[576,256]{1,0:T(8,128)(2,1)S(1)}, bf16[576,256]{1,0:T(8,128)(2,1)S(1)}, u32[]{:S(2)}, u32[]{:S(2)}) %collective-permute-start.13) | collective-permute-done | bytes 294944 | tf_op jit(solution)/shard_map/ppermute | solution.py:33
  102.5 4.5 %collective-permute-done.11.refs_1_ = bf16[512,256]{1,0:T(8,128)(2,1)S(1)} collective-permute-done((bf16[512,256]{1,0:T(8,128)(2,1)S(1)}, bf16[512,256]{1,0:T(8,128)(2,1)S(1)}, u32[]{:S(2)}, u32[]{:S(2)}) %collective-permute-start.11) | collective-permute-done | bytes 262176 | tf_op jit(solution)/shard_map/ppermute | solution.py:33
  107.0 1.0 combine.1
  108.0 0.5 all-to-all-done.2.parcel_ref
  108.5 1.2 %owner_sum.1 = bf16[256,576]{1,0:T(8,128)(2,1)} custom-call(bf16[768,256]{1,0:T(8,128)(2,1)S(1)} %copy-done, bf16[32,112,128]{2,1,0:T(8,128)(2,1)S(1)} %all-to-all-done.2.parcel_ref), custom_call_target="tpu_custom_call" | custom-call | tf_op jit(solution)/shard_map/owner_sum/pallas_call | solution.py:294
  (38 shorter events, 1.9 us)
Async XLA Ops:
  2.5 20.2 %all-to-all-start = ((s32[32,1,32]{2,1,0:T(1,128)}), s32[32,1,32]{2,1,0:T(1,128)S(1)}, u32[]{:S(2)}, u32[]{:S(2)}) async-start(s32[32,1,32]{2,1,0:T(1,128)} %reshape.154), calls=%async_computation | async-start | bytes 32768 | tf_op jit(solution)/shard_map/all_to_all | solution.py:344
  25.3 29.7 %all-to-all-start.1 = ((bf16[32,112,128]{2,1,0:T(8,128)(2,1)}), bf16[32,112,128]{2,1,0:T(8,128)(2,1)S(1)}, u32[]{:S(2)}, u32[]{:S(2)}) async-start(bf16[32,112,128]{2,1,0:T(8,128)(2,1)} %get-tuple-element.30), calls=%async_computation.1 | async-start | bytes 1835008 | tf_op jit(solution)/shard_map/all_to_all | solution.py:386
  30.3 9.6 %collective-permute-start = (bf16[256,576]{1,0:T(8,128)(2,1)S(1)}, bf16[256,576]{1,0:T(8,128)(2,1)S(1)}, u32[]{:S(2)}, u32[]{:S(2)}) collective-permute-start(bf16[256,576]{1,0:T(8,128)(2,1)S(1)} %get-tuple-element.31.refs_0_.refs_6_), channel_id=1, source_target_pairs={{0,2},{1,3},{2,4},{3,5},{4,6},{5,7},{6,0},{7,1},{8,10},{9,11},{10,... | collective-permute-start | bytes 884744 | tf_op jit(solution)/shard_map/ppermute | solution.py:33
  31.9 9.8 %collective-permute-start.4 = (bf16[256,512]{1,0:T(8,128)(2,1)S(1)}, bf16[256,512]{1,0:T(8,128)(2,1)S(1)}, u32[]{:S(2)}, u32[]{:S(2)}) collective-permute-start(bf16[256,512]{1,0:T(8,128)(2,1)S(1)} %get-tuple-element.32.refs_4_.refs_10_), channel_id=1, source_target_pairs={{0,6},{1,7},{2,0},{3,1},{4,2},{5,3},{6,4},{7,5},{8,14},{9,15},{10,... | collective-permute-start | bytes 786440 | tf_op jit(solution)/shard_map/ppermute | solution.py:33
  33.6 20.5 %collective-permute-start.2 = (bf16[256,576]{1,0:T(8,128)(2,1)S(1)}, bf16[256,576]{1,0:T(8,128)(2,1)S(1)}, u32[]{:S(2)}, u32[]{:S(2)}) collective-permute-start(bf16[256,576]{1,0:T(8,128)(2,1)S(1)} %get-tuple-element.31.refs_0_.refs_6_), channel_id=1, source_target_pairs={{0,6},{1,7},{2,0},{3,1},{4,2},{5,3},{6,4},{7,5},{8,14},{9,15},{10,... | collective-permute-start | bytes 884744 | tf_op jit(solution)/shard_map/ppermute | solution.py:33
  39.9 14.2 %collective-permute-start.1 = (bf16[256,576]{1,0:T(8,128)(2,1)S(1)}, bf16[256,576]{1,0:T(8,128)(2,1)S(1)}, u32[]{:S(2)}, u32[]{:S(2)}) collective-permute-start(bf16[256,576]{1,0:T(8,128)(2,1)S(1)} %collective-permute-done.refs_0_.refs_1_.refs_7_), channel_id=1, source_target_pairs={{0,2},{1,3},{2,4},{3,5},{4,6},{5,7},{6,0},{7,1},{8,10},{9,11},{10,... | collective-permute-start | bytes 884744 | tf_op jit(solution)/shard_map/ppermute | solution.py:33
  40.2 13.9 %collective-permute-start.3 = (bf16[256,512]{1,0:T(8,128)(2,1)S(1)}, bf16[256,512]{1,0:T(8,128)(2,1)S(1)}, u32[]{:S(2)}, u32[]{:S(2)}) collective-permute-start(bf16[256,512]{1,0:T(8,128)(2,1)S(1)} %get-tuple-element.32.refs_4_.refs_10_), channel_id=1, source_target_pairs={{0,2},{1,3},{2,4},{3,5},{4,6},{5,7},{6,0},{7,1},{8,10},{9,11},{10,... | collective-permute-start | bytes 786440 | tf_op jit(solution)/shard_map/ppermute | solution.py:33
  41.7 12.4 %collective-permute-start.5 = (bf16[256,512]{1,0:T(8,128)(2,1)S(1)}, bf16[256,512]{1,0:T(8,128)(2,1)S(1)}, u32[]{:S(2)}, u32[]{:S(2)}) collective-permute-start(bf16[256,512]{1,0:T(8,128)(2,1)S(1)} %collective-permute-done.4.refs_5_.refs_7_.refs_13_), channel_id=1, source_target_pairs={{0,6},{1,7},{2,0},{3,1},{4,2},{5,3},{6,4},{7,5},{8,14},{9,15},{10,... | collective-permute-start | bytes 786440 | tf_op jit(solution)/shard_map/ppermute | solution.py:33
  55.9 2.4 %collective-permute-start.6 = (bf16[64,8,576]{2,1,0:T(8,128)(2,1)S(1)}, bf16[64,8,576]{2,1,0:T(8,128)(2,1)S(1)}, u32[]{:S(2)}, u32[]{:S(2)}) collective-permute-start(bf16[64,8,576]{2,1,0:T(8,128)(2,1)S(1)} %bitcast.8), channel_id=1, source_target_pairs={{0,1},{1,0},{2,3},{3,2},{4,5},{5,4},{6,7},{7,6},{8,9},{9,8},{10,11... | collective-permute-start | bytes 1769480 | tf_op jit(solution)/shard_map/ppermute | solution.py:400
  60.2 7.2 %collective-permute-start.9 = (f32[4,8,256]{2,1,0:T(8,128)S(1)}, f32[4,8,256]{2,1,0:T(8,128)S(1)}, u32[]{:S(2)}, u32[]{:S(2)}) collective-permute-start(f32[4,8,256]{2,1,0:T(8,128)S(1)} %get-tuple-element.34.refs_6_.refs_2_.refs_0_), channel_id=1, source_target_pairs={{0,6},{1,7},{2,0},{3,1},{4,2},{5,3},{6,4},{7,5},{8,14},{9,15},{10,... | collective-permute-start | bytes 98312 | tf_op jit(solution)/shard_map/ppermute | solution.py:33
  63.0 5.4 %collective-permute-start.8 = (f32[4,8,256]{2,1,0:T(8,128)S(1)}, f32[4,8,256]{2,1,0:T(8,128)S(1)}, u32[]{:S(2)}, u32[]{:S(2)}) collective-permute-start(f32[4,8,256]{2,1,0:T(8,128)S(1)} %get-tuple-element.34.refs_6_.refs_2_.refs_0_), channel_id=1, source_target_pairs={{0,4},{1,5},{2,6},{3,7},{4,0},{5,1},{6,2},{7,3},{8,12},{9,13},{10,... | collective-permute-start | bytes 98312 | tf_op jit(solution)/shard_map/ppermute | solution.py:33
  63.8 5.1 %collective-permute-start.7 = (f32[4,8,256]{2,1,0:T(8,128)S(1)}, f32[4,8,256]{2,1,0:T(8,128)S(1)}, u32[]{:S(2)}, u32[]{:S(2)}) collective-permute-start(f32[4,8,256]{2,1,0:T(8,128)S(1)} %get-tuple-element.34.refs_6_.refs_2_.refs_0_), channel_id=1, source_target_pairs={{0,2},{1,3},{2,4},{3,5},{4,6},{5,7},{6,0},{7,1},{8,10},{9,11},{10,... | collective-permute-start | bytes 98312 | tf_op jit(solution)/shard_map/ppermute | solution.py:33
  71.7 3.0 %collective-permute-start.16 = (bf16[32,112,128]{2,1,0:T(8,128)(2,1)S(1)}, bf16[32,112,128]{2,1,0:T(8,128)(2,1)S(1)}, u32[]{:S(2)}, u32[]{:S(2)}) collective-permute-start(bf16[32,112,128]{2,1,0:T(8,128)(2,1)S(1)} %get-tuple-element.56), channel_id=1, source_target_pairs={{0,1},{1,0},{2,3},{3,2},{4,5},{5,4},{6,7},{7,6},{8,9},{9,8},{10,11... | collective-permute-start | bytes 2752520 | tf_op jit(solution)/shard_map/ppermute | solution.py:443
  75.9 32.7 %all-to-all-start.2 = ((bf16[32,112,128]{2,1,0:T(8,128)(2,1)}), bf16[32,112,128]{2,1,0:T(8,128)(2,1)S(1)}, u32[]{:S(2)}, u32[]{:S(2)}) async-start(bf16[32,112,128]{2,1,0:T(8,128)(2,1)} %add_convert_fusion), calls=%async_computation.2 | async-start | bytes 1835008 | tf_op jit(solution)/shard_map/all_to_all | solution.py:453
  83.9 10.0 %collective-permute-start.14 = (bf16[576,256]{1,0:T(8,128)(2,1)S(1)}, bf16[576,256]{1,0:T(8,128)(2,1)S(1)}, u32[]{:S(2)}, u32[]{:S(2)}) collective-permute-start(bf16[576,256]{1,0:T(8,128)(2,1)S(1)} %get-tuple-element.51), channel_id=1, source_target_pairs={{0,6},{1,7},{2,0},{3,1},{4,2},{5,3},{6,4},{7,5},{8,14},{9,15},{10,... | collective-permute-start | bytes 884744 | tf_op jit(solution)/shard_map/ppermute | solution.py:33
  86.0 11.3 %collective-permute-start.10 = (bf16[512,256]{1,0:T(8,128)(2,1)S(1)}, bf16[512,256]{1,0:T(8,128)(2,1)S(1)}, u32[]{:S(2)}, u32[]{:S(2)}) collective-permute-start(bf16[512,256]{1,0:T(8,128)(2,1)S(1)} %get-tuple-element.46), channel_id=1, source_target_pairs={{0,2},{1,3},{2,4},{3,5},{4,6},{5,7},{6,0},{7,1},{8,10},{9,11},{10,... | collective-permute-start | bytes 786440 | tf_op jit(solution)/shard_map/ppermute | solution.py:33
  87.6 20.9 %copy-start = (bf16[768,256]{1,0:T(8,128)(2,1)S(1)}, bf16[768,256]{1,0:T(8,128)(2,1)}, u32[]{:S(2)}) copy-start(bf16[768,256]{1,0:T(8,128)(2,1)} %get-tuple-element.54.hot_ref) | copy-start | bytes 1179652
  87.7 11.8 %collective-permute-start.12 = (bf16[512,256]{1,0:T(8,128)(2,1)S(1)}, bf16[512,256]{1,0:T(8,128)(2,1)S(1)}, u32[]{:S(2)}, u32[]{:S(2)}) collective-permute-start(bf16[512,256]{1,0:T(8,128)(2,1)S(1)} %get-tuple-element.47), channel_id=1, source_target_pairs={{0,6},{1,7},{2,0},{3,1},{4,2},{5,3},{6,4},{7,5},{8,14},{9,15},{10,... | collective-permute-start | bytes 786440 | tf_op jit(solution)/shard_map/ppermute | solution.py:33
  91.0 11.6 %collective-permute-start.13 = (bf16[576,256]{1,0:T(8,128)(2,1)S(1)}, bf16[576,256]{1,0:T(8,128)(2,1)S(1)}, u32[]{:S(2)}, u32[]{:S(2)}) collective-permute-start(bf16[576,256]{1,0:T(8,128)(2,1)S(1)} %get-tuple-element.49), channel_id=1, source_target_pairs={{0,2},{1,3},{2,4},{3,5},{4,6},{5,7},{6,0},{7,1},{8,10},{9,11},{10,... | collective-permute-start | bytes 884744 | tf_op jit(solution)/shard_map/ppermute | solution.py:33
  93.9 13.1 %collective-permute-start.15 = (bf16[576,256]{1,0:T(8,128)(2,1)S(1)}, bf16[576,256]{1,0:T(8,128)(2,1)S(1)}, u32[]{:S(2)}, u32[]{:S(2)}) collective-permute-start(bf16[576,256]{1,0:T(8,128)(2,1)S(1)} %add_convert_fusion.1), channel_id=1, source_target_pairs={{0,6},{1,7},{2,0},{3,1},{4,2},{5,3},{6,4},{7,5},{8,14},{9,15},{10,... | collective-permute-start | bytes 884744 | tf_op jit(solution)/shard_map/ppermute | solution.py:33
  97.3 9.7 %collective-permute-start.11 = (bf16[512,256]{1,0:T(8,128)(2,1)S(1)}, bf16[512,256]{1,0:T(8,128)(2,1)S(1)}, u32[]{:S(2)}, u32[]{:S(2)}) collective-permute-start(bf16[512,256]{1,0:T(8,128)(2,1)S(1)} %add_convert_fusion.2), channel_id=1, source_target_pairs={{0,2},{1,3},{2,4},{3,5},{4,6},{5,7},{6,0},{7,1},{8,10},{9,11},{10,... | collective-permute-start | bytes 786440 | tf_op jit(solution)/shard_map/ppermute | solution.py:33

commit v6 on v5

--- a/solution.py
+++ b/solution.py
@@ -12,6 +12,7 @@
 QUERIES = 16
 XN = 4
 CORES = 2
+PARTS = 4
 
 score_scale = 192.0 ** (-0.5)
 log2e = 1.0 / math.log(2.0)
@@ -88,19 +89,8 @@
     return jnp.concatenate(parts, axis=1).astype(bf16)
 
 
-def pack_kernel(tokens, slot_limit, asked_ref, cache_ref, q_ref, g_ref, *refs):
-    out_ref, hot_out, q_out, g_out, rows_ref, hot_ref, sems = refs[-7:]
+def asked_rows(asked_ref, slot_limit, tokens):
     owners, _, block_count = asked_ref.shape
-    pair = CORES * tokens
-    tp = lax.axis_index("tp")
-    first = pl.multiple_of(tp // CORES * pair, pair)
-    copies = [
-        pltpu.make_async_copy(cache_ref.at[:, pl.ds(first, pair), :], rows_ref, sems.at[0]),
-        pltpu.make_async_copy(q_ref, q_out, sems.at[1]),
-        pltpu.make_async_copy(g_ref, g_out, sems.at[2]),
-    ]
-    for copy in copies:
-        copy.start()
     wanted = asked_ref[:, 0, :].astype(f32)
     row, lane = iotas((block_count, block_count))
     rank = dot32(wanted.astype(bf16), bit_matrix(row < lane))
@@ -109,32 +99,54 @@
     for j in range(slot_limit):
         level = jnp.where(rank == j, wanted, 0.0).astype(bf16)
         slot += dot32(bit_matrix(row == lane * slot_limit + j), level)
-    slot = slot.astype(bf16)
-
     row, lane = iotas((block_count, block_count * tokens))
     start = row * tokens
-    hot = expand(dot32(slot, bit_matrix((lane >= start) & (lane < start + tokens))), tokens)
+    columns = bit_matrix((lane >= start) & (lane < start + tokens))
+    hot = expand(dot32(slot.astype(bf16), columns), tokens)
     row, lane = iotas(hot.shape)
-    hot = jnp.where((row & (tokens - 1)) == (lane & (tokens - 1)), hot, 0.0).astype(bf16)
-    hot_ref[...] = hot
-    copies.append(pltpu.make_async_copy(hot_ref, hot_out, sems.at[3]))
-    copies[3].start()
+    return jnp.where((row & (tokens - 1)) == (lane & (tokens - 1)), hot, 0.0).astype(bf16)
+
+
+def pack_kernel(tokens, slot_limit, asked_ref, cache_ref, q_ref, g_ref, *refs):
+    out_ref, q_out, g_out, rows_ref, parcel_ref, sems = refs[-6:]
+    block_count = cache_ref.shape[0]
+    pair = CORES * tokens
+    tp = lax.axis_index("tp")
+    first = pl.multiple_of(tp // CORES * pair, pair)
+    copies = [
+        pltpu.make_async_copy(cache_ref.at[:, pl.ds(first, pair), :], rows_ref, sems.at[0]),
+        pltpu.make_async_copy(q_ref, q_out, sems.at[1]),
+        pltpu.make_async_copy(g_ref, g_out, sems.at[2]),
+    ]
+    for copy in copies:
+        copy.start()
+    hot = asked_rows(asked_ref, slot_limit, tokens)
     copies[0].wait()
     rows = rows_ref[...].astype(f32)
     rows = jnp.where(tp % CORES == 0, rows[:, :tokens], rows[:, tokens:])
     rows = rows.reshape(block_count * tokens, rows_ref.shape[2]).astype(bf16)
-    out_ref[...] = to_parcels(dot32(hot, rows), out_ref.shape, slot_limit)
+    owners, height, lanes = out_ref.shape
+    size, count = owners // PARTS, hot.shape[0] // PARTS
+    for i in range(PARTS):
+        part = pl.ds(i * size, size)
+        moved = dot32(hot[i * count : (i + 1) * count], rows)
+        parcel_ref[part] = to_parcels(moved, (size, height, lanes), slot_limit)
+        copies.append(
+            pltpu.make_async_copy(parcel_ref.at[part], out_ref.at[part], sems.at[3 + i])
+        )
+        copies[-1].start()
     for copy in copies[1:]:
         copy.wait()
 
 
+def asked_kernel(tokens, slot_limit, asked_ref, out_ref):
+    out_ref[...] = asked_rows(asked_ref, slot_limit, tokens).T
+
+
 def owner_kernel(slot_limit, hot_ref, parcel_ref, out_ref):
-    count = hot_ref.shape[0] // parcel_ref.shape[0]
+    count = hot_ref.shape[1] // parcel_ref.shape[0]
     rows = from_parcels(parcel_ref, count, slot_limit)
-    total = lax.dot_general(
-        hot_ref[...], rows, (((0,), (0,)), ((), ())), preferred_element_type=f32
-    )
-    out_ref[...] = total.astype(bf16)
+    out_ref[...] = dot32(hot_ref[...], rows).astype(bf16)
 
 
 def slot_hot(ids, tokens, lanes):
@@ -364,24 +376,19 @@
     plan = jnp.concatenate([slot_order[:, None], plan], axis=1)
     plan = jnp.pad(plan, ((0, 0), (0, 128 - plan.shape[1])))
 
-    packed, asked_hot, q0, g0 = call(
+    packed, q0, g0 = call(
         functools.partial(pack_kernel, tokens, slot_limit),
-        [
-            shaped(parcels),
-            shaped((slots * tokens, held)),
-            shaped((rows, width)),
-            shaped((rows, value_width)),
-        ],
+        [shaped(parcels), shaped((rows, width)), shaped((rows, value_width))],
         [asked, latent_cache, query_rows, grad_rows],
         "pack",
         unused=(plan,),
         scratch=[
             pltpu.VMEM((block_count, CORES * tokens, width), bf16),
-            pltpu.VMEM((slots * tokens, held), bf16),
-            pltpu.SemaphoreType.DMA((4,)),
+            pltpu.VMEM(parcels, bf16),
+            pltpu.SemaphoreType.DMA((3 + PARTS,)),
         ],
         far_in=3,
-        far_out=(1,),
+        far_out=(0,),
     )
     fetched = lax.all_to_all(packed, "ctx", 0, 0, tiled=True)
 
@@ -474,6 +481,12 @@
         [att[0], send_x(att_left, 1), att_right, qg[0], qg_left, send_x(qg_right, -1)],
         "combine",
     )
+    (asked_hot,) = call(
+        functools.partial(asked_kernel, tokens, slot_limit),
+        [shaped((held, slots * tokens))],
+        [asked],
+        "asked",
+    )
     (cache_grad,) = call(
         functools.partial(owner_kernel, slot_limit),
         [shaped((held, width))],

time: 110 us -> 110 us (level)
  waiting for transfers between devices: 35.2 us -> 32.2 us
  starting transfers between devices: 46.4 us -> 48.5 us
    ppermute x15, waiting for transfers between devices: 28.9 us -> 26.2 us  [send_x(): return lax.ppermute(value, 'tp', x_shift(k % XN))]
    ppermute x15, starting transfers between devices: 22.4 us -> 24.4 us  [send_x(): return lax.ppermute(value, 'tp', x_shift(k % XN))]
    pallas_call x11 -> x12, Pallas kernels: 20.6 us -> 21 us  [call(): pl.pallas_call(kernel, out_shape=[pltpu.HBM(x.shape, x.dtype) if i in far...]
  transfers between devices with their start and end apart: 20 -> 20, of which waited for: 12 -> 10; matrix products, arithmetic and copies ran while one was open for 3% -> 3% of each run, Pallas kernels for 10% -> 11%
where the time goes in v6:
time: 110 us; the launch traced here: 109 us
  starting transfers between devices  48.5 us (44%)
  waiting for transfers between devices  32.2 us (29%)
  Pallas kernels  21 us (19%)
  other arithmetic  4.31 us (4%)
  local copies, waits for them, and re-layouts  2.4 us (2%)
    ppermute x15, waiting for transfers between devices, send_x(): return lax.ppermute(value, 'tp', x_shift(k % XN))  26.2 us
    ppermute x15, starting transfers between devices, send_x(): return lax.ppermute(value, 'tp', x_shift(k % XN))  24.4 us
    pallas_call x12, Pallas kernels, call(): pl.pallas_call(kernel, out_shape=[pltpu.HBM(x.shape, x.dtype) if i in far...  21 us
    all_to_all x1, starting transfers between devices, on_device(): lax.all_to_all(wanted.astype(jnp.int32)[:, None, :], 'ctx', split_axis=0,...  11.7 us
    all_to_all x1, starting transfers between devices, on_device(): returned = lax.all_to_all(returning, 'ctx', 0, 0, tiled=True)  6.83 us
    all_to_all x1, starting transfers between devices, on_device(): fetched = lax.all_to_all(packed, 'ctx', 0, 0, tiled=True)  5.02 us
    all_to_all x1, waiting for transfers between devices, on_device(): lax.all_to_all(wanted.astype(jnp.int32)[:, None, :], 'ctx', split_axis=0,...  4.8 us
  transfers between devices with their start and end apart: 20, of which 10 were waited for; matrix products, arithmetic and copies ran while one was open for 3% of the time, Pallas kernels for 11%

profile of v6, /device:TPU:8, one launch (start us, length us, event | category | flops | bytes accessed | tf_op | source)
XLA Modules:
  0.0 109.3 jit_solution(1422832659877669954)
XLA Ops:
  0.6 0.8 eq.26
  1.4 0.4 fusion
  1.8 0.7 reshape.154
  2.5 11.7 %all-to-all-start = ((s32[32,1,32]{2,1,0:T(1,128)}), s32[32,1,32]{2,1,0:T(1,128)S(1)}, u32[]{:S(2)}, u32[]{:S(2)}) async-start(s32[32,1,32]{2,1,0:T(1,128)} %reshape.154), calls=%async_computation | async-start | bytes 32768 | tf_op jit(solution)/shard_map/all_to_all | solution.py:356
  14.3 0.2 reduce_window_sum.18
  14.5 0.2 select_reduce_fusion
  14.6 0.2 fusion.2
  15.8 0.9 compare_reduce_fusion
  16.9 0.7 fusion.4
  17.8 4.8 %all-to-all-done.asked_ref = s32[32,1,32]{2,1,0:T(1,128)S(1)} async-done(((s32[32,1,32]{2,1,0:T(1,128)}), s32[32,1,32]{2,1,0:T(1,128)S(1)}, u32[]{:S(2)}, u32[]{:S(2)}) %all-to-all-start) | async-done | bytes 4128 | tf_op jit(solution)/shard_map/all_to_all | solution.py:356
  22.6 2.5 %pack.1 = (bf16[32,112,128]{2,1,0:T(8,128)(2,1)}, bf16[256,576]{1,0:T(8,128)(2,1)S(1)}, bf16[256,512]{1,0:T(8,128)(2,1)S(1)}) custom-call(s32[32,1,32]{2,1,0:T(1,128)S(1)} %all-to-all-done.asked_ref, bf16[32,64,576]{2,1,0:T(8,128)(2,1)} %cache_ref.1, bf16[256,576]{1,0:T(8,128)(2,1)} %bitcast.11, bf16[256,512]{1,0:T(8,128)(2,1)} %bitcast.13, ...), custom_call_target="tpu_custom_call" | custom-call | tf_op jit(solution)/shard_map/pack/pallas_call | solution.py:306
  25.2 5.0 %all-to-all-start.1 = ((bf16[32,112,128]{2,1,0:T(8,128)(2,1)}), bf16[32,112,128]{2,1,0:T(8,128)(2,1)S(1)}, u32[]{:S(2)}, u32[]{:S(2)}) async-start(bf16[32,112,128]{2,1,0:T(8,128)(2,1)} %get-tuple-element.29), calls=%async_computation.1 | async-start | bytes 1835008 | tf_op jit(solution)/shard_map/all_to_all | solution.py:393
  30.2 1.6 %collective-permute-start = (bf16[256,576]{1,0:T(8,128)(2,1)S(1)}, bf16[256,576]{1,0:T(8,128)(2,1)S(1)}, u32[]{:S(2)}, u32[]{:S(2)}) collective-permute-start(bf16[256,576]{1,0:T(8,128)(2,1)S(1)} %get-tuple-element.30.refs_0_.refs_6_), channel_id=1, source_target_pairs={{0,2},{1,3},{2,4},{3,5},{4,6},{5,7},{6,0},{7,1},{8,10},{9,11},{10,... | collective-permute-start | bytes 884744 | tf_op jit(solution)/shard_map/ppermute | solution.py:34
  31.8 1.7 %collective-permute-start.4 = (bf16[256,512]{1,0:T(8,128)(2,1)S(1)}, bf16[256,512]{1,0:T(8,128)(2,1)S(1)}, u32[]{:S(2)}, u32[]{:S(2)}) collective-permute-start(bf16[256,512]{1,0:T(8,128)(2,1)S(1)} %get-tuple-element.31.refs_4_.refs_10_), channel_id=1, source_target_pairs={{0,6},{1,7},{2,0},{3,1},{4,2},{5,3},{6,4},{7,5},{8,14},{9,15},{10,... | collective-permute-start | bytes 786440 | tf_op jit(solution)/shard_map/ppermute | solution.py:34
  33.5 1.5 %collective-permute-start.2 = (bf16[256,576]{1,0:T(8,128)(2,1)S(1)}, bf16[256,576]{1,0:T(8,128)(2,1)S(1)}, u32[]{:S(2)}, u32[]{:S(2)}) collective-permute-start(bf16[256,576]{1,0:T(8,128)(2,1)S(1)} %get-tuple-element.30.refs_0_.refs_6_), channel_id=1, source_target_pairs={{0,6},{1,7},{2,0},{3,1},{4,2},{5,3},{6,4},{7,5},{8,14},{9,15},{10,... | collective-permute-start | bytes 884744 | tf_op jit(solution)/shard_map/ppermute | solution.py:34
  35.0 4.7 %collective-permute-done.refs_0_.refs_1_.refs_7_ = bf16[256,576]{1,0:T(8,128)(2,1)S(1)} collective-permute-done((bf16[256,576]{1,0:T(8,128)(2,1)S(1)}, bf16[256,576]{1,0:T(8,128)(2,1)S(1)}, u32[]{:S(2)}, u32[]{:S(2)}) %collective-permute-start) | collective-permute-done | bytes 294944 | tf_op jit(solution)/shard_map/ppermute | solution.py:34
  39.8 0.3 collective-permute-start.1
  40.1 1.5 %collective-permute-start.3 = (bf16[256,512]{1,0:T(8,128)(2,1)S(1)}, bf16[256,512]{1,0:T(8,128)(2,1)S(1)}, u32[]{:S(2)}, u32[]{:S(2)}) collective-permute-start(bf16[256,512]{1,0:T(8,128)(2,1)S(1)} %get-tuple-element.31.refs_4_.refs_10_), channel_id=1, source_target_pairs={{0,2},{1,3},{2,4},{3,5},{4,6},{5,7},{6,0},{7,1},{8,10},{9,11},{10,... | collective-permute-start | bytes 786440 | tf_op jit(solution)/shard_map/ppermute | solution.py:34
  41.5 2.4 %collective-permute-start.5 = (bf16[256,512]{1,0:T(8,128)(2,1)S(1)}, bf16[256,512]{1,0:T(8,128)(2,1)S(1)}, u32[]{:S(2)}, u32[]{:S(2)}) collective-permute-start(bf16[256,512]{1,0:T(8,128)(2,1)S(1)} %collective-permute-done.4.refs_5_.refs_7_.refs_13_), channel_id=1, source_target_pairs={{0,6},{1,7},{2,0},{3,1},{4,2},{5,3},{6,4},{7,5},{8,14},{9,15},{10,... | collective-permute-start | bytes 786440 | tf_op jit(solution)/shard_map/ppermute | solution.py:34
  43.9 10.0 %collective-permute-done.3.refs_3_.refs_5_.refs_11_ = bf16[256,512]{1,0:T(8,128)(2,1)S(1)} collective-permute-done((bf16[256,512]{1,0:T(8,128)(2,1)S(1)}, bf16[256,512]{1,0:T(8,128)(2,1)S(1)}, u32[]{:S(2)}, u32[]{:S(2)}) %collective-permute-start.3) | collective-permute-done | bytes 262176 | tf_op jit(solution)/shard_map/ppermute | solution.py:34
  54.0 0.9 all-to-all-done.1.parcel_ref
  54.9 0.9 unpack.1.key_ref.refs_0_
  55.7 0.3 collective-permute-start.6
  56.0 1.9 %own_scores.1 = (bf16[4,512,256]{2,1,0:T(8,128)(2,1)S(1)}, f32[4,512,256]{2,1,0:T(8,128)S(1)}, f32[4,8,256]{2,1,0:T(8,128)S(1)}) custom-call(s32[96,128]{1,0:T(8,128)S(1)} %pad.9.refs_0_.plan_ref.refs_14_, bf16[512,576]{1,0:T(8,128)(2,1)S(1)} %unpack.1.key_ref.refs_0_, bf16[256,576]{1,0:T(8,128)(2,1)S(1)} %get-tuple-element.30.refs_0_.refs_6_, ...), custom_call_target="tpu_custom_call" | custom-call | tf_op jit(solution)/shard_map/own_scores/pallas_call | solution.py:306
  57.9 0.2 collective-permute-done.6
  58.1 1.9 %other_scores.1 = (bf16[4,512,256]{2,1,0:T(8,128)(2,1)S(1)}, f32[4,512,256]{2,1,0:T(8,128)S(1)}, f32[4,8,256]{2,1,0:T(8,128)S(1)}) custom-call(s32[96,128]{1,0:T(8,128)S(1)} %pad.9.refs_0_.plan_ref.refs_14_, bf16[512,576]{1,0:T(8,128)(2,1)S(1)} %bitcast.9, bf16[256,576]{1,0:T(8,128)(2,1)S(1)} %get-tuple-element.30.refs_0_.refs_6_, ...), custom_call_target="tpu_custom_call" | custom-call | tf_op jit(solution)/shard_map/other_scores/pallas_call | solution.py:306
  60.0 1.6 %collective-permute-start.7 = (f32[4,8,256]{2,1,0:T(8,128)S(1)}, f32[4,8,256]{2,1,0:T(8,128)S(1)}, u32[]{:S(2)}, u32[]{:S(2)}) collective-permute-start(f32[4,8,256]{2,1,0:T(8,128)S(1)} %get-tuple-element.33.refs_6_.refs_2_.refs_0_), channel_id=1, source_target_pairs={{0,2},{1,3},{2,4},{3,5},{4,6},{5,7},{6,0},{7,1},{8,10},{9,11},{10,... | collective-permute-start | bytes 98312 | tf_op jit(solution)/shard_map/ppermute | solution.py:34
  61.6 2.7 %collective-permute-start.8 = (f32[4,8,256]{2,1,0:T(8,128)S(1)}, f32[4,8,256]{2,1,0:T(8,128)S(1)}, u32[]{:S(2)}, u32[]{:S(2)}) collective-permute-start(f32[4,8,256]{2,1,0:T(8,128)S(1)} %get-tuple-element.33.refs_6_.refs_2_.refs_0_), channel_id=1, source_target_pairs={{0,4},{1,5},{2,6},{3,7},{4,0},{5,1},{6,2},{7,3},{8,12},{9,13},{10,... | collective-permute-start | bytes 98312 | tf_op jit(solution)/shard_map/ppermute | solution.py:34
  64.3 1.4 %collective-permute-start.9 = (f32[4,8,256]{2,1,0:T(8,128)S(1)}, f32[4,8,256]{2,1,0:T(8,128)S(1)}, u32[]{:S(2)}, u32[]{:S(2)}) collective-permute-start(f32[4,8,256]{2,1,0:T(8,128)S(1)} %get-tuple-element.33.refs_6_.refs_2_.refs_0_), channel_id=1, source_target_pairs={{0,6},{1,7},{2,0},{3,1},{4,2},{5,3},{6,4},{7,5},{8,14},{9,15},{10,... | collective-permute-start | bytes 98312 | tf_op jit(solution)/shard_map/ppermute | solution.py:34
  65.8 2.6 %local.1 = (bf16[4,576,256]{2,1,0:T(8,128)(2,1)S(1)}, bf16[4,576,256]{2,1,0:T(8,128)(2,1)S(1)}) custom-call(bf16[512,576]{1,0:T(8,128)(2,1)S(1)} %unpack.1.key_ref.refs_0_, bf16[512,576]{1,0:T(8,128)(2,1)S(1)} %bitcast.10, bf16[4,512,256]{2,1,0:T(8,128)(2,1)S(1)} %get-tuple-element.36.refs_2_.refs_0_, ...), custom_call_target="tpu_custom_call" | custom-call | tf_op jit(solution)/shard_map/local/pallas_call | solution.py:306
  68.5 2.8 %other_grads.1 = (bf16[32,112,128]{2,1,0:T(8,128)(2,1)S(1)}, bf16[4,576,256]{2,1,0:T(8,128)(2,1)}, bf16[768,512]{1,0:T(8,128)(2,1)S(1)}) custom-call(bf16[4,512,256]{2,1,0:T(8,128)(2,1)S(1)} %get-tuple-element.34.refs_3_.refs_0_, f32[4,512,256]{2,1,0:T(8,128)S(1)} %get-tuple-element.35.refs_5_.refs_1_, ...), custom_call_target="tpu_custom_call" | custom-call | tf_op jit(solution)/shard_map/other_grads/pallas_call | solution.py:306
  71.2 0.3 collective-permute-start.16
  71.5 2.7 %own_grads.1 = (bf16[32,112,128]{2,1,0:T(8,128)(2,1)S(1)}, bf16[4,576,256]{2,1,0:T(8,128)(2,1)}) custom-call(bf16[4,512,256]{2,1,0:T(8,128)(2,1)S(1)} %get-tuple-element.36.refs_2_.refs_0_, f32[4,512,256]{2,1,0:T(8,128)S(1)} %get-tuple-element.37.refs_4_.refs_1_, f32[4,8,256]{2,1,0:T(8,128)S(1)} %get-tuple-element.33.refs_6_.refs_2_.refs_0_, ...), custom_call_target="tpu_custom_call" | custom-call | tf_op jit(solution)/shard_map/own_grads/pallas_call | solution.py:306
  74.2 1.2 %add_convert_fusion = bf16[32,112,128]{2,1,0:T(8,128)(2,1)} fusion(bf16[32,112,128]{2,1,0:T(8,128)(2,1)S(1)} %collective-permute-done.16, bf16[32,112,128]{2,1,0:T(8,128)(2,1)S(1)} %get-tuple-element.53), kind=kLoop, calls=%fused_computation.2 | loop fusion | flops 1835008 | bytes 2752512 | tf_op jit(solution)/shard_map/convert_element_type | solution.py:459
  75.4 6.8 %all-to-all-start.2 = ((bf16[32,112,128]{2,1,0:T(8,128)(2,1)}), bf16[32,112,128]{2,1,0:T(8,128)(2,1)S(1)}, u32[]{:S(2)}, u32[]{:S(2)}) async-start(bf16[32,112,128]{2,1,0:T(8,128)(2,1)} %add_convert_fusion), calls=%async_computation.2 | async-start | bytes 1835008 | tf_op jit(solution)/shard_map/all_to_all | solution.py:460
  82.2 1.3 %scale.3 = (bf16[512,256]{1,0:T(8,128)(2,1)S(1)}, bf16[576,256]{1,0:T(8,128)(2,1)S(1)}) custom-call(f32[4,8,256]{2,1,0:T(8,128)S(1)} %get-tuple-element.33.refs_6_.refs_2_.refs_0_, f32[4,8,256]{2,1,0:T(8,128)S(1)} %collective-permute-done.7.refs_3_.refs_1_, f32[4,8,256]{2,1,0:T(8,128)S(1)} %collective-permute-done.8.refs_4_.refs_2_, ...), custom_call_target="tpu_custom_call" | custom-call | tf_op jit(solution)/shard_map/scale/pallas_call | solution.py:306
  83.5 2.5 %collective-permute-start.14 = (bf16[576,256]{1,0:T(8,128)(2,1)S(1)}, bf16[576,256]{1,0:T(8,128)(2,1)S(1)}, u32[]{:S(2)}, u32[]{:S(2)}) collective-permute-start(bf16[576,256]{1,0:T(8,128)(2,1)S(1)} %get-tuple-element.50), channel_id=1, source_target_pairs={{0,6},{1,7},{2,0},{3,1},{4,2},{5,3},{6,4},{7,5},{8,14},{9,15},{10,... | collective-permute-start | bytes 884744 | tf_op jit(solution)/shard_map/ppermute | solution.py:34
  86.0 1.6 %scale.2 = (bf16[512,256]{1,0:T(8,128)(2,1)S(1)}, bf16[576,256]{1,0:T(8,128)(2,1)S(1)}, bf16[512,256]{1,0:T(8,128)(2,1)S(1)}, bf16[576,256]{1,0:T(8,128)(2,1)S(1...) custom-call(f32[4,8,256]{2,1,0:T(8,128)S(1)} %get-tuple-element.33.refs_6_.refs_2_.refs_0_, ...), custom_call_target="tpu_custom_call" | custom-call | tf_op jit(solution)/shard_map/scale/pallas_call | solution.py:306
  87.6 1.4 %collective-permute-start.13 = (bf16[576,256]{1,0:T(8,128)(2,1)S(1)}, bf16[576,256]{1,0:T(8,128)(2,1)S(1)}, u32[]{:S(2)}, u32[]{:S(2)}) collective-permute-start(bf16[576,256]{1,0:T(8,128)(2,1)S(1)} %get-tuple-element.48), channel_id=1, source_target_pairs={{0,2},{1,3},{2,4},{3,5},{4,6},{5,7},{6,0},{7,1},{8,10},{9,11},{10,... | collective-permute-start | bytes 884744 | tf_op jit(solution)/shard_map/ppermute | solution.py:34
  89.0 2.0 %collective-permute-start.12 = (bf16[512,256]{1,0:T(8,128)(2,1)S(1)}, bf16[512,256]{1,0:T(8,128)(2,1)S(1)}, u32[]{:S(2)}, u32[]{:S(2)}) collective-permute-start(bf16[512,256]{1,0:T(8,128)(2,1)S(1)} %get-tuple-element.46), channel_id=1, source_target_pairs={{0,6},{1,7},{2,0},{3,1},{4,2},{5,3},{6,4},{7,5},{8,14},{9,15},{10,... | collective-permute-start | bytes 786440 | tf_op jit(solution)/shard_map/ppermute | solution.py:34
  91.0 2.5 %collective-permute-done.14 = bf16[576,256]{1,0:T(8,128)(2,1)S(1)} collective-permute-done((bf16[576,256]{1,0:T(8,128)(2,1)S(1)}, bf16[576,256]{1,0:T(8,128)(2,1)S(1)}, u32[]{:S(2)}, u32[]{:S(2)}) %collective-permute-start.14) | collective-permute-done | bytes 294944 | tf_op jit(solution)/shard_map/ppermute | solution.py:34
  93.6 3.7 %collective-permute-start.15 = (bf16[576,256]{1,0:T(8,128)(2,1)S(1)}, bf16[576,256]{1,0:T(8,128)(2,1)S(1)}, u32[]{:S(2)}, u32[]{:S(2)}) collective-permute-start(bf16[576,256]{1,0:T(8,128)(2,1)S(1)} %add_convert_fusion.1), channel_id=1, source_target_pairs={{0,6},{1,7},{2,0},{3,1},{4,2},{5,3},{6,4},{7,5},{8,14},{9,15},{10,... | collective-permute-start | bytes 884744 | tf_op jit(solution)/shard_map/ppermute | solution.py:34
  97.4 0.6 asked.1.hot_ref
  98.0 1.1 %collective-permute-done.12.refs_2_ = bf16[512,256]{1,0:T(8,128)(2,1)S(1)} collective-permute-done((bf16[512,256]{1,0:T(8,128)(2,1)S(1)}, bf16[512,256]{1,0:T(8,128)(2,1)S(1)}, u32[]{:S(2)}, u32[]{:S(2)}) %collective-permute-start.12) | collective-permute-done | bytes 262176 | tf_op jit(solution)/shard_map/ppermute | solution.py:34
  99.1 3.6 %collective-permute-done.13.refs_4_ = bf16[576,256]{1,0:T(8,128)(2,1)S(1)} collective-permute-done((bf16[576,256]{1,0:T(8,128)(2,1)S(1)}, bf16[576,256]{1,0:T(8,128)(2,1)S(1)}, u32[]{:S(2)}, u32[]{:S(2)}) %collective-permute-start.13) | collective-permute-done | bytes 294944 | tf_op jit(solution)/shard_map/ppermute | solution.py:34
  102.7 4.3 %collective-permute-done.11.refs_1_ = bf16[512,256]{1,0:T(8,128)(2,1)S(1)} collective-permute-done((bf16[512,256]{1,0:T(8,128)(2,1)S(1)}, bf16[512,256]{1,0:T(8,128)(2,1)S(1)}, u32[]{:S(2)}, u32[]{:S(2)}) %collective-permute-start.11) | collective-permute-done | bytes 262176 | tf_op jit(solution)/shard_map/ppermute | solution.py:34
  107.0 1.0 combine.1
  108.1 1.2 %owner_sum.1 = bf16[256,576]{1,0:T(8,128)(2,1)} custom-call(bf16[256,768]{1,0:T(8,128)(2,1)S(1)} %asked.1.hot_ref, bf16[32,112,128]{2,1,0:T(8,128)(2,1)S(1)} %all-to-all-done.2.parcel_ref), custom_call_target="tpu_custom_call" | custom-call | tf_op jit(solution)/shard_map/owner_sum/pallas_call | solution.py:306
  (37 shorter events, 1.9 us)
Async XLA Ops:
  2.5 20.2 %all-to-all-start = ((s32[32,1,32]{2,1,0:T(1,128)}), s32[32,1,32]{2,1,0:T(1,128)S(1)}, u32[]{:S(2)}, u32[]{:S(2)}) async-start(s32[32,1,32]{2,1,0:T(1,128)} %reshape.154), calls=%async_computation | async-start | bytes 32768 | tf_op jit(solution)/shard_map/all_to_all | solution.py:356
  25.2 29.7 %all-to-all-start.1 = ((bf16[32,112,128]{2,1,0:T(8,128)(2,1)}), bf16[32,112,128]{2,1,0:T(8,128)(2,1)S(1)}, u32[]{:S(2)}, u32[]{:S(2)}) async-start(bf16[32,112,128]{2,1,0:T(8,128)(2,1)} %get-tuple-element.29), calls=%async_computation.1 | async-start | bytes 1835008 | tf_op jit(solution)/shard_map/all_to_all | solution.py:393
  30.2 9.6 %collective-permute-start = (bf16[256,576]{1,0:T(8,128)(2,1)S(1)}, bf16[256,576]{1,0:T(8,128)(2,1)S(1)}, u32[]{:S(2)}, u32[]{:S(2)}) collective-permute-start(bf16[256,576]{1,0:T(8,128)(2,1)S(1)} %get-tuple-element.30.refs_0_.refs_6_), channel_id=1, source_target_pairs={{0,2},{1,3},{2,4},{3,5},{4,6},{5,7},{6,0},{7,1},{8,10},{9,11},{10,... | collective-permute-start | bytes 884744 | tf_op jit(solution)/shard_map/ppermute | solution.py:34
  31.8 9.8 %collective-permute-start.4 = (bf16[256,512]{1,0:T(8,128)(2,1)S(1)}, bf16[256,512]{1,0:T(8,128)(2,1)S(1)}, u32[]{:S(2)}, u32[]{:S(2)}) collective-permute-start(bf16[256,512]{1,0:T(8,128)(2,1)S(1)} %get-tuple-element.31.refs_4_.refs_10_), channel_id=1, source_target_pairs={{0,6},{1,7},{2,0},{3,1},{4,2},{5,3},{6,4},{7,5},{8,14},{9,15},{10,... | collective-permute-start | bytes 786440 | tf_op jit(solution)/shard_map/ppermute | solution.py:34
  33.5 20.5 %collective-permute-start.2 = (bf16[256,576]{1,0:T(8,128)(2,1)S(1)}, bf16[256,576]{1,0:T(8,128)(2,1)S(1)}, u32[]{:S(2)}, u32[]{:S(2)}) collective-permute-start(bf16[256,576]{1,0:T(8,128)(2,1)S(1)} %get-tuple-element.30.refs_0_.refs_6_), channel_id=1, source_target_pairs={{0,6},{1,7},{2,0},{3,1},{4,2},{5,3},{6,4},{7,5},{8,14},{9,15},{10,... | collective-permute-start | bytes 884744 | tf_op jit(solution)/shard_map/ppermute | solution.py:34
  39.8 14.2 %collective-permute-start.1 = (bf16[256,576]{1,0:T(8,128)(2,1)S(1)}, bf16[256,576]{1,0:T(8,128)(2,1)S(1)}, u32[]{:S(2)}, u32[]{:S(2)}) collective-permute-start(bf16[256,576]{1,0:T(8,128)(2,1)S(1)} %collective-permute-done.refs_0_.refs_1_.refs_7_), channel_id=1, source_target_pairs={{0,2},{1,3},{2,4},{3,5},{4,6},{5,7},{6,0},{7,1},{8,10},{9,11},{10,... | collective-permute-start | bytes 884744 | tf_op jit(solution)/shard_map/ppermute | solution.py:34
  40.1 13.9 %collective-permute-start.3 = (bf16[256,512]{1,0:T(8,128)(2,1)S(1)}, bf16[256,512]{1,0:T(8,128)(2,1)S(1)}, u32[]{:S(2)}, u32[]{:S(2)}) collective-permute-start(bf16[256,512]{1,0:T(8,128)(2,1)S(1)} %get-tuple-element.31.refs_4_.refs_10_), channel_id=1, source_target_pairs={{0,2},{1,3},{2,4},{3,5},{4,6},{5,7},{6,0},{7,1},{8,10},{9,11},{10,... | collective-permute-start | bytes 786440 | tf_op jit(solution)/shard_map/ppermute | solution.py:34
  41.5 12.4 %collective-permute-start.5 = (bf16[256,512]{1,0:T(8,128)(2,1)S(1)}, bf16[256,512]{1,0:T(8,128)(2,1)S(1)}, u32[]{:S(2)}, u32[]{:S(2)}) collective-permute-start(bf16[256,512]{1,0:T(8,128)(2,1)S(1)} %collective-permute-done.4.refs_5_.refs_7_.refs_13_), channel_id=1, source_target_pairs={{0,6},{1,7},{2,0},{3,1},{4,2},{5,3},{6,4},{7,5},{8,14},{9,15},{10,... | collective-permute-start | bytes 786440 | tf_op jit(solution)/shard_map/ppermute | solution.py:34
  55.7 2.4 %collective-permute-start.6 = (bf16[64,8,576]{2,1,0:T(8,128)(2,1)S(1)}, bf16[64,8,576]{2,1,0:T(8,128)(2,1)S(1)}, u32[]{:S(2)}, u32[]{:S(2)}) collective-permute-start(bf16[64,8,576]{2,1,0:T(8,128)(2,1)S(1)} %bitcast.8), channel_id=1, source_target_pairs={{0,1},{1,0},{2,3},{3,2},{4,5},{5,4},{6,7},{7,6},{8,9},{9,8},{10,11... | collective-permute-start | bytes 1769480 | tf_op jit(solution)/shard_map/ppermute | solution.py:407
  60.0 8.4 %collective-permute-start.7 = (f32[4,8,256]{2,1,0:T(8,128)S(1)}, f32[4,8,256]{2,1,0:T(8,128)S(1)}, u32[]{:S(2)}, u32[]{:S(2)}) collective-permute-start(f32[4,8,256]{2,1,0:T(8,128)S(1)} %get-tuple-element.33.refs_6_.refs_2_.refs_0_), channel_id=1, source_target_pairs={{0,2},{1,3},{2,4},{3,5},{4,6},{5,7},{6,0},{7,1},{8,10},{9,11},{10,... | collective-permute-start | bytes 98312 | tf_op jit(solution)/shard_map/ppermute | solution.py:34
  61.6 6.8 %collective-permute-start.8 = (f32[4,8,256]{2,1,0:T(8,128)S(1)}, f32[4,8,256]{2,1,0:T(8,128)S(1)}, u32[]{:S(2)}, u32[]{:S(2)}) collective-permute-start(f32[4,8,256]{2,1,0:T(8,128)S(1)} %get-tuple-element.33.refs_6_.refs_2_.refs_0_), channel_id=1, source_target_pairs={{0,4},{1,5},{2,6},{3,7},{4,0},{5,1},{6,2},{7,3},{8,12},{9,13},{10,... | collective-permute-start | bytes 98312 | tf_op jit(solution)/shard_map/ppermute | solution.py:34
  64.3 4.1 %collective-permute-start.9 = (f32[4,8,256]{2,1,0:T(8,128)S(1)}, f32[4,8,256]{2,1,0:T(8,128)S(1)}, u32[]{:S(2)}, u32[]{:S(2)}) collective-permute-start(f32[4,8,256]{2,1,0:T(8,128)S(1)} %get-tuple-element.33.refs_6_.refs_2_.refs_0_), channel_id=1, source_target_pairs={{0,6},{1,7},{2,0},{3,1},{4,2},{5,3},{6,4},{7,5},{8,14},{9,15},{10,... | collective-permute-start | bytes 98312 | tf_op jit(solution)/shard_map/ppermute | solution.py:34
  71.2 3.0 %collective-permute-start.16 = (bf16[32,112,128]{2,1,0:T(8,128)(2,1)S(1)}, bf16[32,112,128]{2,1,0:T(8,128)(2,1)S(1)}, u32[]{:S(2)}, u32[]{:S(2)}) collective-permute-start(bf16[32,112,128]{2,1,0:T(8,128)(2,1)S(1)} %get-tuple-element.54), channel_id=1, source_target_pairs={{0,1},{1,0},{2,3},{3,2},{4,5},{5,4},{6,7},{7,6},{8,9},{9,8},{10,11... | collective-permute-start | bytes 2752520 | tf_op jit(solution)/shard_map/ppermute | solution.py:450
  75.4 32.7 %all-to-all-start.2 = ((bf16[32,112,128]{2,1,0:T(8,128)(2,1)}), bf16[32,112,128]{2,1,0:T(8,128)(2,1)S(1)}, u32[]{:S(2)}, u32[]{:S(2)}) async-start(bf16[32,112,128]{2,1,0:T(8,128)(2,1)} %add_convert_fusion), calls=%async_computation.2 | async-start | bytes 1835008 | tf_op jit(solution)/shard_map/all_to_all | solution.py:460
  83.5 10.0 %collective-permute-start.14 = (bf16[576,256]{1,0:T(8,128)(2,1)S(1)}, bf16[576,256]{1,0:T(8,128)(2,1)S(1)}, u32[]{:S(2)}, u32[]{:S(2)}) collective-permute-start(bf16[576,256]{1,0:T(8,128)(2,1)S(1)} %get-tuple-element.50), channel_id=1, source_target_pairs={{0,6},{1,7},{2,0},{3,1},{4,2},{5,3},{6,4},{7,5},{8,14},{9,15},{10,... | collective-permute-start | bytes 884744 | tf_op jit(solution)/shard_map/ppermute | solution.py:34
  86.0 11.3 %collective-permute-start.10 = (bf16[512,256]{1,0:T(8,128)(2,1)S(1)}, bf16[512,256]{1,0:T(8,128)(2,1)S(1)}, u32[]{:S(2)}, u32[]{:S(2)}) collective-permute-start(bf16[512,256]{1,0:T(8,128)(2,1)S(1)} %get-tuple-element.45), channel_id=1, source_target_pairs={{0,2},{1,3},{2,4},{3,5},{4,6},{5,7},{6,0},{7,1},{8,10},{9,11},{10,... | collective-permute-start | bytes 786440 | tf_op jit(solution)/shard_map/ppermute | solution.py:34
  87.6 15.1 %collective-permute-start.13 = (bf16[576,256]{1,0:T(8,128)(2,1)S(1)}, bf16[576,256]{1,0:T(8,128)(2,1)S(1)}, u32[]{:S(2)}, u32[]{:S(2)}) collective-permute-start(bf16[576,256]{1,0:T(8,128)(2,1)S(1)} %get-tuple-element.48), channel_id=1, source_target_pairs={{0,2},{1,3},{2,4},{3,5},{4,6},{5,7},{6,0},{7,1},{8,10},{9,11},{10,... | collective-permute-start | bytes 884744 | tf_op jit(solution)/shard_map/ppermute | solution.py:34
  89.0 10.1 %collective-permute-start.12 = (bf16[512,256]{1,0:T(8,128)(2,1)S(1)}, bf16[512,256]{1,0:T(8,128)(2,1)S(1)}, u32[]{:S(2)}, u32[]{:S(2)}) collective-permute-start(bf16[512,256]{1,0:T(8,128)(2,1)S(1)} %get-tuple-element.46), channel_id=1, source_target_pairs={{0,6},{1,7},{2,0},{3,1},{4,2},{5,3},{6,4},{7,5},{8,14},{9,15},{10,... | collective-permute-start | bytes 786440 | tf_op jit(solution)/shard_map/ppermute | solution.py:34
  93.6 13.4 %collective-permute-start.15 = (bf16[576,256]{1,0:T(8,128)(2,1)S(1)}, bf16[576,256]{1,0:T(8,128)(2,1)S(1)}, u32[]{:S(2)}, u32[]{:S(2)}) collective-permute-start(bf16[576,256]{1,0:T(8,128)(2,1)S(1)} %add_convert_fusion.1), channel_id=1, source_target_pairs={{0,6},{1,7},{2,0},{3,1},{4,2},{5,3},{6,4},{7,5},{8,14},{9,15},{10,... | collective-permute-start | bytes 884744 | tf_op jit(solution)/shard_map/ppermute | solution.py:34
  97.3 9.7 %collective-permute-start.11 = (bf16[512,256]{1,0:T(8,128)(2,1)S(1)}, bf16[512,256]{1,0:T(8,128)(2,1)S(1)}, u32[]{:S(2)}, u32[]{:S(2)}) collective-permute-start(bf16[512,256]{1,0:T(8,128)(2,1)S(1)} %add_convert_fusion.2), channel_id=1, source_target_pairs={{0,2},{1,3},{2,4},{3,5},{4,6},{5,7},{6,0},{7,1},{8,10},{9,11},{10,... | collective-permute-start | bytes 786440 | tf_op jit(solution)/shard_map/ppermute | solution.py:34

commit v7 on v6

--- a/solution.py
+++ b/solution.py
@@ -235,32 +235,35 @@
 
 def key_grad_kernel(tokens, slot_limit, half, *refs):
     p_ref, gw_ref = refs[:2]
-    stat_refs, q_refs, g_refs = (refs[2 + i * XN : 2 + (i + 1) * XN] for i in range(3))
-    last_ref, part_ref = refs[2 + 3 * XN : 4 + 3 * XN]
+    stat_refs, refs = refs[2 : 2 + XN], refs[2 + XN :]
+    ds_ref, w_ref, sum_ref, sem = refs[-4:]
     if half == 0:
-        out_ref, part_out, sum_ref, sem = refs[-4:]
+        hot_ref, q_all, g_all, part_ref, out_ref, part_out = refs[:-4]
     else:
-        out_ref, part_out, hot_ref, sum_ref, sem = refs[-5:]
+        q_refs, g_refs = refs[:XN], refs[XN : 2 * XN]
+        plan_ref, part_ref, out_ref, part_out, hot_ref, q_all, g_all = refs[2 * XN : -4]
     copy = pltpu.make_async_copy(part_ref, part_out, sem)
     copy.start()
-    value_width = g_refs[0].shape[1]
-    key_grad, value_grad = [], []
+    value_width = g_all.shape[1]
+    rows = p_ref.shape[2]
     for k in range(XN):
+        part = slice(k * rows, (k + 1) * rows)
+        if half == 1:
+            q_all[part, :] = q_refs[k][...]
+            g_all[part, :] = g_refs[k][...]
         mine, inner, factor = row_stats(stat_refs, k)
         factor = factor * mine[3 + half : 4 + half]
         p = p_ref[k].astype(f32)
-        ds = (p * (factor * score_scale) * (gw_ref[k] - inner)).astype(bf16)
-        key_grad.append(dot32(ds, q_refs[k][...]))
-        value_grad.append(dot32((p * factor).astype(bf16), g_refs[k][...]))
-    key_grad, value_grad = sum(key_grad), sum(value_grad)
+        ds_ref[:, part] = (p * (factor * score_scale) * (gw_ref[k] - inner)).astype(bf16)
+        w_ref[:, part] = (p * factor).astype(bf16)
+    key_grad = dot32(ds_ref[...], q_all[...])
+    value_grad = dot32(w_ref[...], g_all[...])
     sum_ref[:, :value_width] = (key_grad[:, :value_width] + value_grad).astype(bf16)
     sum_ref[:, value_width:] = key_grad[:, value_width:].astype(bf16)
-    if half == 0:
-        hot_ref = last_ref
-    else:
-        hot_ref[...] = slot_hot(last_ref[:, 0:1], tokens, sum_ref.shape[0])
-    rows = dot32(hot_ref[...], sum_ref[...])
-    out_ref[...] = to_parcels(rows, out_ref.shape, slot_limit)
+    if half == 1:
+        hot_ref[...] = slot_hot(plan_ref[:, 0:1], tokens, sum_ref.shape[0])
+    moved = dot32(hot_ref[...], sum_ref[...])
+    out_ref[...] = to_parcels(moved, out_ref.shape, slot_limit)
     copy.wait()
 
 
@@ -438,10 +441,21 @@
     )
 
     grad_shape = shaped(parcels)
-    sum_scratch = [pltpu.VMEM((half, width), bf16), pltpu.SemaphoreType.DMA(())]
-    other_grad, value_part, spread_hot = call(
+    sum_scratch = [
+        pltpu.VMEM((half, XN * rows), bf16),
+        pltpu.VMEM((half, XN * rows), bf16),
+        pltpu.VMEM((half, width), bf16),
+        pltpu.SemaphoreType.DMA(()),
+    ]
+    other_grad, value_part, spread_hot, q_all, g_all = call(
         functools.partial(key_grad_kernel, tokens, slot_limit, 1),
-        [grad_shape, shaped(part_shape), shaped((slots * tokens, half))],
+        [
+            grad_shape,
+            shaped(part_shape),
+            shaped((slots * tokens, half)),
+            shaped((XN * rows, width)),
+            shaped((XN * rows, value_width)),
+        ],
         [other_p, other_gw, *all_stats, *gathered, plan, value_part],
         "other_grads",
         far_out=(1,),
@@ -451,7 +465,7 @@
     own_grad, grad_part = call(
         functools.partial(key_grad_kernel, tokens, slot_limit, 0),
         [grad_shape, shaped(part_shape)],
-        [own_p, own_gw, *all_stats, *gathered, spread_hot, grad_part],
+        [own_p, own_gw, *all_stats, spread_hot, q_all, g_all, grad_part],
         "own_grads",
         far_out=(1,),
         scratch=sum_scratch,

time: 110 us -> 110 us (level)
  no operation moved by 1% of the time
where the time goes in v7:
time: 110 us; the launch traced here: 109 us
  starting transfers between devices  48.5 us (44%)
  waiting for transfers between devices  32.2 us (29%)
  Pallas kernels  21.1 us (19%)
  other arithmetic  4.31 us (4%)
  local copies, waits for them, and re-layouts  2.4 us (2%)
    ppermute x15, waiting for transfers between devices, send_x(): return lax.ppermute(value, 'tp', x_shift(k % XN))  26.3 us
    ppermute x15, starting transfers between devices, send_x(): return lax.ppermute(value, 'tp', x_shift(k % XN))  24.4 us
    pallas_call x12, Pallas kernels, call(): pl.pallas_call(kernel, out_shape=[pltpu.HBM(x.shape, x.dtype) if i in far...  21.1 us
    all_to_all x1, starting transfers between devices, on_device(): lax.all_to_all(wanted.astype(jnp.int32)[:, None, :], 'ctx', split_axis=0,...  11.7 us
    all_to_all x1, starting transfers between devices, on_device(): returned = lax.all_to_all(returning, 'ctx', 0, 0, tiled=True)  6.82 us
    all_to_all x1, starting transfers between devices, on_device(): fetched = lax.all_to_all(packed, 'ctx', 0, 0, tiled=True)  5.02 us
    all_to_all x1, waiting for transfers between devices, on_device(): lax.all_to_all(wanted.astype(jnp.int32)[:, None, :], 'ctx', split_axis=0,...  4.8 us
  transfers between devices with their start and end apart: 20, of which 10 were waited for; matrix products, arithmetic and copies ran while one was open for 3% of the time, Pallas kernels for 11%

profile of v7, /device:TPU:8, one launch (start us, length us, event | category | flops | bytes accessed | tf_op | source)
XLA Modules:
  0.0 109.4 jit_solution(357880170949568229)
XLA Ops:
  0.6 0.8 eq.26
  1.4 0.4 fusion
  1.8 0.7 reshape.154
  2.5 11.7 %all-to-all-start = ((s32[32,1,32]{2,1,0:T(1,128)}), s32[32,1,32]{2,1,0:T(1,128)S(1)}, u32[]{:S(2)}, u32[]{:S(2)}) async-start(s32[32,1,32]{2,1,0:T(1,128)} %reshape.154), calls=%async_computation | async-start | bytes 32768 | tf_op jit(solution)/shard_map/all_to_all | solution.py:359
  14.3 0.2 reduce_window_sum.18
  14.5 0.2 select_reduce_fusion
  14.6 0.2 fusion.2
  15.8 0.9 compare_reduce_fusion
  16.9 0.7 fusion.4
  17.8 4.8 %all-to-all-done.asked_ref = s32[32,1,32]{2,1,0:T(1,128)S(1)} async-done(((s32[32,1,32]{2,1,0:T(1,128)}), s32[32,1,32]{2,1,0:T(1,128)S(1)}, u32[]{:S(2)}, u32[]{:S(2)}) %all-to-all-start) | async-done | bytes 4128 | tf_op jit(solution)/shard_map/all_to_all | solution.py:359
  22.6 2.5 %pack.1 = (bf16[32,112,128]{2,1,0:T(8,128)(2,1)}, bf16[256,576]{1,0:T(8,128)(2,1)S(1)}, bf16[256,512]{1,0:T(8,128)(2,1)S(1)}) custom-call(s32[32,1,32]{2,1,0:T(1,128)S(1)} %all-to-all-done.asked_ref, bf16[32,64,576]{2,1,0:T(8,128)(2,1)} %cache_ref.1, bf16[256,576]{1,0:T(8,128)(2,1)} %bitcast.11, bf16[256,512]{1,0:T(8,128)(2,1)} %bitcast.13, ...), custom_call_target="tpu_custom_call" | custom-call | tf_op jit(solution)/shard_map/pack/pallas_call | solution.py:309
  25.2 5.0 %all-to-all-start.1 = ((bf16[32,112,128]{2,1,0:T(8,128)(2,1)}), bf16[32,112,128]{2,1,0:T(8,128)(2,1)S(1)}, u32[]{:S(2)}, u32[]{:S(2)}) async-start(bf16[32,112,128]{2,1,0:T(8,128)(2,1)} %get-tuple-element.31), calls=%async_computation.1 | async-start | bytes 1835008 | tf_op jit(solution)/shard_map/all_to_all | solution.py:396
  30.2 1.6 %collective-permute-start = (bf16[256,576]{1,0:T(8,128)(2,1)S(1)}, bf16[256,576]{1,0:T(8,128)(2,1)S(1)}, u32[]{:S(2)}, u32[]{:S(2)}) collective-permute-start(bf16[256,576]{1,0:T(8,128)(2,1)S(1)} %get-tuple-element.32.refs_0_.refs_6_), channel_id=1, source_target_pairs={{0,2},{1,3},{2,4},{3,5},{4,6},{5,7},{6,0},{7,1},{8,10},{9,11},{10,... | collective-permute-start | bytes 884744 | tf_op jit(solution)/shard_map/ppermute | solution.py:34
  31.8 1.7 %collective-permute-start.4 = (bf16[256,512]{1,0:T(8,128)(2,1)S(1)}, bf16[256,512]{1,0:T(8,128)(2,1)S(1)}, u32[]{:S(2)}, u32[]{:S(2)}) collective-permute-start(bf16[256,512]{1,0:T(8,128)(2,1)S(1)} %get-tuple-element.33.refs_4_.refs_10_), channel_id=1, source_target_pairs={{0,6},{1,7},{2,0},{3,1},{4,2},{5,3},{6,4},{7,5},{8,14},{9,15},{10,... | collective-permute-start | bytes 786440 | tf_op jit(solution)/shard_map/ppermute | solution.py:34
  33.5 1.5 %collective-permute-start.2 = (bf16[256,576]{1,0:T(8,128)(2,1)S(1)}, bf16[256,576]{1,0:T(8,128)(2,1)S(1)}, u32[]{:S(2)}, u32[]{:S(2)}) collective-permute-start(bf16[256,576]{1,0:T(8,128)(2,1)S(1)} %get-tuple-element.32.refs_0_.refs_6_), channel_id=1, source_target_pairs={{0,6},{1,7},{2,0},{3,1},{4,2},{5,3},{6,4},{7,5},{8,14},{9,15},{10,... | collective-permute-start | bytes 884744 | tf_op jit(solution)/shard_map/ppermute | solution.py:34
  35.0 4.7 %collective-permute-done.refs_0_.refs_1_.refs_7_ = bf16[256,576]{1,0:T(8,128)(2,1)S(1)} collective-permute-done((bf16[256,576]{1,0:T(8,128)(2,1)S(1)}, bf16[256,576]{1,0:T(8,128)(2,1)S(1)}, u32[]{:S(2)}, u32[]{:S(2)}) %collective-permute-start) | collective-permute-done | bytes 294944 | tf_op jit(solution)/shard_map/ppermute | solution.py:34
  39.8 0.3 collective-permute-start.1
  40.1 1.5 %collective-permute-start.3 = (bf16[256,512]{1,0:T(8,128)(2,1)S(1)}, bf16[256,512]{1,0:T(8,128)(2,1)S(1)}, u32[]{:S(2)}, u32[]{:S(2)}) collective-permute-start(bf16[256,512]{1,0:T(8,128)(2,1)S(1)} %get-tuple-element.33.refs_4_.refs_10_), channel_id=1, source_target_pairs={{0,2},{1,3},{2,4},{3,5},{4,6},{5,7},{6,0},{7,1},{8,10},{9,11},{10,... | collective-permute-start | bytes 786440 | tf_op jit(solution)/shard_map/ppermute | solution.py:34
  41.5 2.4 %collective-permute-start.5 = (bf16[256,512]{1,0:T(8,128)(2,1)S(1)}, bf16[256,512]{1,0:T(8,128)(2,1)S(1)}, u32[]{:S(2)}, u32[]{:S(2)}) collective-permute-start(bf16[256,512]{1,0:T(8,128)(2,1)S(1)} %collective-permute-done.4.refs_5_.refs_7_.refs_13_), channel_id=1, source_target_pairs={{0,6},{1,7},{2,0},{3,1},{4,2},{5,3},{6,4},{7,5},{8,14},{9,15},{10,... | collective-permute-start | bytes 786440 | tf_op jit(solution)/shard_map/ppermute | solution.py:34
  43.9 10.0 %collective-permute-done.3.refs_3_.refs_5_.refs_11_ = bf16[256,512]{1,0:T(8,128)(2,1)S(1)} collective-permute-done((bf16[256,512]{1,0:T(8,128)(2,1)S(1)}, bf16[256,512]{1,0:T(8,128)(2,1)S(1)}, u32[]{:S(2)}, u32[]{:S(2)}) %collective-permute-start.3) | collective-permute-done | bytes 262176 | tf_op jit(solution)/shard_map/ppermute | solution.py:34
  54.0 0.9 all-to-all-done.1.parcel_ref
  54.9 0.9 unpack.1.key_ref.refs_0_
  55.7 0.3 collective-permute-start.6
  56.0 1.9 %own_scores.1 = (bf16[4,512,256]{2,1,0:T(8,128)(2,1)S(1)}, f32[4,512,256]{2,1,0:T(8,128)S(1)}, f32[4,8,256]{2,1,0:T(8,128)S(1)}) custom-call(s32[96,128]{1,0:T(8,128)S(1)} %pad.9.refs_0_.plan_ref.refs_14_, bf16[512,576]{1,0:T(8,128)(2,1)S(1)} %unpack.1.key_ref.refs_0_, bf16[256,576]{1,0:T(8,128)(2,1)S(1)} %get-tuple-element.32.refs_0_.refs_6_, ...), custom_call_target="tpu_custom_call" | custom-call | tf_op jit(solution)/shard_map/own_scores/pallas_call | solution.py:309
  57.9 0.2 collective-permute-done.6
  58.1 1.9 %other_scores.1 = (bf16[4,512,256]{2,1,0:T(8,128)(2,1)S(1)}, f32[4,512,256]{2,1,0:T(8,128)S(1)}, f32[4,8,256]{2,1,0:T(8,128)S(1)}) custom-call(s32[96,128]{1,0:T(8,128)S(1)} %pad.9.refs_0_.plan_ref.refs_14_, bf16[512,576]{1,0:T(8,128)(2,1)S(1)} %bitcast.9, bf16[256,576]{1,0:T(8,128)(2,1)S(1)} %get-tuple-element.32.refs_0_.refs_6_, ...), custom_call_target="tpu_custom_call" | custom-call | tf_op jit(solution)/shard_map/other_scores/pallas_call | solution.py:309
  60.0 1.6 %collective-permute-start.7 = (f32[4,8,256]{2,1,0:T(8,128)S(1)}, f32[4,8,256]{2,1,0:T(8,128)S(1)}, u32[]{:S(2)}, u32[]{:S(2)}) collective-permute-start(f32[4,8,256]{2,1,0:T(8,128)S(1)} %get-tuple-element.35.refs_6_.refs_2_.refs_0_), channel_id=1, source_target_pairs={{0,2},{1,3},{2,4},{3,5},{4,6},{5,7},{6,0},{7,1},{8,10},{9,11},{10,... | collective-permute-start | bytes 98312 | tf_op jit(solution)/shard_map/ppermute | solution.py:34
  61.6 2.7 %collective-permute-start.8 = (f32[4,8,256]{2,1,0:T(8,128)S(1)}, f32[4,8,256]{2,1,0:T(8,128)S(1)}, u32[]{:S(2)}, u32[]{:S(2)}) collective-permute-start(f32[4,8,256]{2,1,0:T(8,128)S(1)} %get-tuple-element.35.refs_6_.refs_2_.refs_0_), channel_id=1, source_target_pairs={{0,4},{1,5},{2,6},{3,7},{4,0},{5,1},{6,2},{7,3},{8,12},{9,13},{10,... | collective-permute-start | bytes 98312 | tf_op jit(solution)/shard_map/ppermute | solution.py:34
  64.3 1.4 %collective-permute-start.9 = (f32[4,8,256]{2,1,0:T(8,128)S(1)}, f32[4,8,256]{2,1,0:T(8,128)S(1)}, u32[]{:S(2)}, u32[]{:S(2)}) collective-permute-start(f32[4,8,256]{2,1,0:T(8,128)S(1)} %get-tuple-element.35.refs_6_.refs_2_.refs_0_), channel_id=1, source_target_pairs={{0,6},{1,7},{2,0},{3,1},{4,2},{5,3},{6,4},{7,5},{8,14},{9,15},{10,... | collective-permute-start | bytes 98312 | tf_op jit(solution)/shard_map/ppermute | solution.py:34
  65.8 2.6 %local.1 = (bf16[4,576,256]{2,1,0:T(8,128)(2,1)S(1)}, bf16[4,576,256]{2,1,0:T(8,128)(2,1)S(1)}) custom-call(bf16[512,576]{1,0:T(8,128)(2,1)S(1)} %unpack.1.key_ref.refs_0_, bf16[512,576]{1,0:T(8,128)(2,1)S(1)} %bitcast.10, bf16[4,512,256]{2,1,0:T(8,128)(2,1)S(1)} %get-tuple-element.38.refs_2_.refs_0_, ...), custom_call_target="tpu_custom_call" | custom-call | tf_op jit(solution)/shard_map/local/pallas_call | solution.py:309
  68.5 2.8 %other_grads.1 = (bf16[32,112,128]{2,1,0:T(8,128)(2,1)S(1)}, bf16[4,576,256]{2,1,0:T(8,128)(2,1)}, bf16[768,512]{1,0:T(8,128)(2,1)S(1)}, bf16[1024,576]{1,0:T(8,128)(2,1)S(1)}, bf16[1024,512]{1,0:T(8,128)(2,1)S(1)}) custom-call(bf16[4,512,256]{2,1,0:T(8,128)(2,1)S(1)} %get-tuple-element.36.refs_3_.refs_0_, ...), custom_call_target="tpu_custom_call" | custom-call | tf_op jit(solution)/shard_map/other_grads/pallas_call | solution.py:309
  71.3 0.3 collective-permute-start.16
  71.6 2.6 %own_grads.1 = (bf16[32,112,128]{2,1,0:T(8,128)(2,1)S(1)}, bf16[4,576,256]{2,1,0:T(8,128)(2,1)}) custom-call(bf16[4,512,256]{2,1,0:T(8,128)(2,1)S(1)} %get-tuple-element.38.refs_2_.refs_0_, f32[4,512,256]{2,1,0:T(8,128)S(1)} %get-tuple-element.39.refs_4_.refs_1_, f32[4,8,256]{2,1,0:T(8,128)S(1)} %get-tuple-element.35.refs_6_.refs_2_.refs_0_, ...), custom_call_target="tpu_custom_call" | custom-call | tf_op jit(solution)/shard_map/own_grads/pallas_call | solution.py:309
  74.3 1.2 %add_convert_fusion = bf16[32,112,128]{2,1,0:T(8,128)(2,1)} fusion(bf16[32,112,128]{2,1,0:T(8,128)(2,1)S(1)} %collective-permute-done.16, bf16[32,112,128]{2,1,0:T(8,128)(2,1)S(1)} %get-tuple-element.57), kind=kLoop, calls=%fused_computation.2 | loop fusion | flops 1835008 | bytes 2752512 | tf_op jit(solution)/shard_map/convert_element_type | solution.py:473
  75.5 6.8 %all-to-all-start.2 = ((bf16[32,112,128]{2,1,0:T(8,128)(2,1)}), bf16[32,112,128]{2,1,0:T(8,128)(2,1)S(1)}, u32[]{:S(2)}, u32[]{:S(2)}) async-start(bf16[32,112,128]{2,1,0:T(8,128)(2,1)} %add_convert_fusion), calls=%async_computation.2 | async-start | bytes 1835008 | tf_op jit(solution)/shard_map/all_to_all | solution.py:474
  82.3 1.3 %scale.3 = (bf16[512,256]{1,0:T(8,128)(2,1)S(1)}, bf16[576,256]{1,0:T(8,128)(2,1)S(1)}) custom-call(f32[4,8,256]{2,1,0:T(8,128)S(1)} %get-tuple-element.35.refs_6_.refs_2_.refs_0_, f32[4,8,256]{2,1,0:T(8,128)S(1)} %collective-permute-done.7.refs_3_.refs_1_, f32[4,8,256]{2,1,0:T(8,128)S(1)} %collective-permute-done.8.refs_4_.refs_2_, ...), custom_call_target="tpu_custom_call" | custom-call | tf_op jit(solution)/shard_map/scale/pallas_call | solution.py:309
  83.6 2.5 %collective-permute-start.14 = (bf16[576,256]{1,0:T(8,128)(2,1)S(1)}, bf16[576,256]{1,0:T(8,128)(2,1)S(1)}, u32[]{:S(2)}, u32[]{:S(2)}) collective-permute-start(bf16[576,256]{1,0:T(8,128)(2,1)S(1)} %get-tuple-element.54), channel_id=1, source_target_pairs={{0,6},{1,7},{2,0},{3,1},{4,2},{5,3},{6,4},{7,5},{8,14},{9,15},{10,... | collective-permute-start | bytes 884744 | tf_op jit(solution)/shard_map/ppermute | solution.py:34
  86.0 1.6 %scale.2 = (bf16[512,256]{1,0:T(8,128)(2,1)S(1)}, bf16[576,256]{1,0:T(8,128)(2,1)S(1)}, bf16[512,256]{1,0:T(8,128)(2,1)S(1)}, bf16[576,256]{1,0:T(8,128)(2,1)S(1...) custom-call(f32[4,8,256]{2,1,0:T(8,128)S(1)} %get-tuple-element.35.refs_6_.refs_2_.refs_0_, ...), custom_call_target="tpu_custom_call" | custom-call | tf_op jit(solution)/shard_map/scale/pallas_call | solution.py:309
  87.7 1.4 %collective-permute-start.13 = (bf16[576,256]{1,0:T(8,128)(2,1)S(1)}, bf16[576,256]{1,0:T(8,128)(2,1)S(1)}, u32[]{:S(2)}, u32[]{:S(2)}) collective-permute-start(bf16[576,256]{1,0:T(8,128)(2,1)S(1)} %get-tuple-element.52), channel_id=1, source_target_pairs={{0,2},{1,3},{2,4},{3,5},{4,6},{5,7},{6,0},{7,1},{8,10},{9,11},{10,... | collective-permute-start | bytes 884744 | tf_op jit(solution)/shard_map/ppermute | solution.py:34
  89.1 2.0 %collective-permute-start.12 = (bf16[512,256]{1,0:T(8,128)(2,1)S(1)}, bf16[512,256]{1,0:T(8,128)(2,1)S(1)}, u32[]{:S(2)}, u32[]{:S(2)}) collective-permute-start(bf16[512,256]{1,0:T(8,128)(2,1)S(1)} %get-tuple-element.50), channel_id=1, source_target_pairs={{0,6},{1,7},{2,0},{3,1},{4,2},{5,3},{6,4},{7,5},{8,14},{9,15},{10,... | collective-permute-start | bytes 786440 | tf_op jit(solution)/shard_map/ppermute | solution.py:34
  91.1 2.5 %collective-permute-done.14 = bf16[576,256]{1,0:T(8,128)(2,1)S(1)} collective-permute-done((bf16[576,256]{1,0:T(8,128)(2,1)S(1)}, bf16[576,256]{1,0:T(8,128)(2,1)S(1)}, u32[]{:S(2)}, u32[]{:S(2)}) %collective-permute-start.14) | collective-permute-done | bytes 294944 | tf_op jit(solution)/shard_map/ppermute | solution.py:34
  93.6 3.7 %collective-permute-start.15 = (bf16[576,256]{1,0:T(8,128)(2,1)S(1)}, bf16[576,256]{1,0:T(8,128)(2,1)S(1)}, u32[]{:S(2)}, u32[]{:S(2)}) collective-permute-start(bf16[576,256]{1,0:T(8,128)(2,1)S(1)} %add_convert_fusion.1), channel_id=1, source_target_pairs={{0,6},{1,7},{2,0},{3,1},{4,2},{5,3},{6,4},{7,5},{8,14},{9,15},{10,... | collective-permute-start | bytes 884744 | tf_op jit(solution)/shard_map/ppermute | solution.py:34
  97.4 0.6 asked.1.hot_ref
  98.0 1.1 %collective-permute-done.12.refs_2_ = bf16[512,256]{1,0:T(8,128)(2,1)S(1)} collective-permute-done((bf16[512,256]{1,0:T(8,128)(2,1)S(1)}, bf16[512,256]{1,0:T(8,128)(2,1)S(1)}, u32[]{:S(2)}, u32[]{:S(2)}) %collective-permute-start.12) | collective-permute-done | bytes 262176 | tf_op jit(solution)/shard_map/ppermute | solution.py:34
  99.2 3.6 %collective-permute-done.13.refs_4_ = bf16[576,256]{1,0:T(8,128)(2,1)S(1)} collective-permute-done((bf16[576,256]{1,0:T(8,128)(2,1)S(1)}, bf16[576,256]{1,0:T(8,128)(2,1)S(1)}, u32[]{:S(2)}, u32[]{:S(2)}) %collective-permute-start.13) | collective-permute-done | bytes 294944 | tf_op jit(solution)/shard_map/ppermute | solution.py:34
  102.8 4.3 %collective-permute-done.11.refs_1_ = bf16[512,256]{1,0:T(8,128)(2,1)S(1)} collective-permute-done((bf16[512,256]{1,0:T(8,128)(2,1)S(1)}, bf16[512,256]{1,0:T(8,128)(2,1)S(1)}, u32[]{:S(2)}, u32[]{:S(2)}) %collective-permute-start.11) | collective-permute-done | bytes 262176 | tf_op jit(solution)/shard_map/ppermute | solution.py:34
  107.1 1.0 combine.1
  108.2 1.2 %owner_sum.1 = bf16[256,576]{1,0:T(8,128)(2,1)} custom-call(bf16[256,768]{1,0:T(8,128)(2,1)S(1)} %asked.1.hot_ref, bf16[32,112,128]{2,1,0:T(8,128)(2,1)S(1)} %all-to-all-done.2.parcel_ref), custom_call_target="tpu_custom_call" | custom-call | tf_op jit(solution)/shard_map/owner_sum/pallas_call | solution.py:309
  (37 shorter events, 1.9 us)
Async XLA Ops:
  2.5 20.2 %all-to-all-start = ((s32[32,1,32]{2,1,0:T(1,128)}), s32[32,1,32]{2,1,0:T(1,128)S(1)}, u32[]{:S(2)}, u32[]{:S(2)}) async-start(s32[32,1,32]{2,1,0:T(1,128)} %reshape.154), calls=%async_computation | async-start | bytes 32768 | tf_op jit(solution)/shard_map/all_to_all | solution.py:359
  25.2 29.7 %all-to-all-start.1 = ((bf16[32,112,128]{2,1,0:T(8,128)(2,1)}), bf16[32,112,128]{2,1,0:T(8,128)(2,1)S(1)}, u32[]{:S(2)}, u32[]{:S(2)}) async-start(bf16[32,112,128]{2,1,0:T(8,128)(2,1)} %get-tuple-element.31), calls=%async_computation.1 | async-start | bytes 1835008 | tf_op jit(solution)/shard_map/all_to_all | solution.py:396
  30.2 9.6 %collective-permute-start = (bf16[256,576]{1,0:T(8,128)(2,1)S(1)}, bf16[256,576]{1,0:T(8,128)(2,1)S(1)}, u32[]{:S(2)}, u32[]{:S(2)}) collective-permute-start(bf16[256,576]{1,0:T(8,128)(2,1)S(1)} %get-tuple-element.32.refs_0_.refs_6_), channel_id=1, source_target_pairs={{0,2},{1,3},{2,4},{3,5},{4,6},{5,7},{6,0},{7,1},{8,10},{9,11},{10,... | collective-permute-start | bytes 884744 | tf_op jit(solution)/shard_map/ppermute | solution.py:34
  31.8 9.8 %collective-permute-start.4 = (bf16[256,512]{1,0:T(8,128)(2,1)S(1)}, bf16[256,512]{1,0:T(8,128)(2,1)S(1)}, u32[]{:S(2)}, u32[]{:S(2)}) collective-permute-start(bf16[256,512]{1,0:T(8,128)(2,1)S(1)} %get-tuple-element.33.refs_4_.refs_10_), channel_id=1, source_target_pairs={{0,6},{1,7},{2,0},{3,1},{4,2},{5,3},{6,4},{7,5},{8,14},{9,15},{10,... | collective-permute-start | bytes 786440 | tf_op jit(solution)/shard_map/ppermute | solution.py:34
  33.5 20.5 %collective-permute-start.2 = (bf16[256,576]{1,0:T(8,128)(2,1)S(1)}, bf16[256,576]{1,0:T(8,128)(2,1)S(1)}, u32[]{:S(2)}, u32[]{:S(2)}) collective-permute-start(bf16[256,576]{1,0:T(8,128)(2,1)S(1)} %get-tuple-element.32.refs_0_.refs_6_), channel_id=1, source_target_pairs={{0,6},{1,7},{2,0},{3,1},{4,2},{5,3},{6,4},{7,5},{8,14},{9,15},{10,... | collective-permute-start | bytes 884744 | tf_op jit(solution)/shard_map/ppermute | solution.py:34
  39.8 14.2 %collective-permute-start.1 = (bf16[256,576]{1,0:T(8,128)(2,1)S(1)}, bf16[256,576]{1,0:T(8,128)(2,1)S(1)}, u32[]{:S(2)}, u32[]{:S(2)}) collective-permute-start(bf16[256,576]{1,0:T(8,128)(2,1)S(1)} %collective-permute-done.refs_0_.refs_1_.refs_7_), channel_id=1, source_target_pairs={{0,2},{1,3},{2,4},{3,5},{4,6},{5,7},{6,0},{7,1},{8,10},{9,11},{10,... | collective-permute-start | bytes 884744 | tf_op jit(solution)/shard_map/ppermute | solution.py:34
  40.1 13.9 %collective-permute-start.3 = (bf16[256,512]{1,0:T(8,128)(2,1)S(1)}, bf16[256,512]{1,0:T(8,128)(2,1)S(1)}, u32[]{:S(2)}, u32[]{:S(2)}) collective-permute-start(bf16[256,512]{1,0:T(8,128)(2,1)S(1)} %get-tuple-element.33.refs_4_.refs_10_), channel_id=1, source_target_pairs={{0,2},{1,3},{2,4},{3,5},{4,6},{5,7},{6,0},{7,1},{8,10},{9,11},{10,... | collective-permute-start | bytes 786440 | tf_op jit(solution)/shard_map/ppermute | solution.py:34
  41.5 12.4 %collective-permute-start.5 = (bf16[256,512]{1,0:T(8,128)(2,1)S(1)}, bf16[256,512]{1,0:T(8,128)(2,1)S(1)}, u32[]{:S(2)}, u32[]{:S(2)}) collective-permute-start(bf16[256,512]{1,0:T(8,128)(2,1)S(1)} %collective-permute-done.4.refs_5_.refs_7_.refs_13_), channel_id=1, source_target_pairs={{0,6},{1,7},{2,0},{3,1},{4,2},{5,3},{6,4},{7,5},{8,14},{9,15},{10,... | collective-permute-start | bytes 786440 | tf_op jit(solution)/shard_map/ppermute | solution.py:34
  55.7 2.4 %collective-permute-start.6 = (bf16[64,8,576]{2,1,0:T(8,128)(2,1)S(1)}, bf16[64,8,576]{2,1,0:T(8,128)(2,1)S(1)}, u32[]{:S(2)}, u32[]{:S(2)}) collective-permute-start(bf16[64,8,576]{2,1,0:T(8,128)(2,1)S(1)} %bitcast.8), channel_id=1, source_target_pairs={{0,1},{1,0},{2,3},{3,2},{4,5},{5,4},{6,7},{7,6},{8,9},{9,8},{10,11... | collective-permute-start | bytes 1769480 | tf_op jit(solution)/shard_map/ppermute | solution.py:410
  60.0 8.4 %collective-permute-start.7 = (f32[4,8,256]{2,1,0:T(8,128)S(1)}, f32[4,8,256]{2,1,0:T(8,128)S(1)}, u32[]{:S(2)}, u32[]{:S(2)}) collective-permute-start(f32[4,8,256]{2,1,0:T(8,128)S(1)} %get-tuple-element.35.refs_6_.refs_2_.refs_0_), channel_id=1, source_target_pairs={{0,2},{1,3},{2,4},{3,5},{4,6},{5,7},{6,0},{7,1},{8,10},{9,11},{10,... | collective-permute-start | bytes 98312 | tf_op jit(solution)/shard_map/ppermute | solution.py:34
  61.6 6.8 %collective-permute-start.8 = (f32[4,8,256]{2,1,0:T(8,128)S(1)}, f32[4,8,256]{2,1,0:T(8,128)S(1)}, u32[]{:S(2)}, u32[]{:S(2)}) collective-permute-start(f32[4,8,256]{2,1,0:T(8,128)S(1)} %get-tuple-element.35.refs_6_.refs_2_.refs_0_), channel_id=1, source_target_pairs={{0,4},{1,5},{2,6},{3,7},{4,0},{5,1},{6,2},{7,3},{8,12},{9,13},{10,... | collective-permute-start | bytes 98312 | tf_op jit(solution)/shard_map/ppermute | solution.py:34
  64.3 4.1 %collective-permute-start.9 = (f32[4,8,256]{2,1,0:T(8,128)S(1)}, f32[4,8,256]{2,1,0:T(8,128)S(1)}, u32[]{:S(2)}, u32[]{:S(2)}) collective-permute-start(f32[4,8,256]{2,1,0:T(8,128)S(1)} %get-tuple-element.35.refs_6_.refs_2_.refs_0_), channel_id=1, source_target_pairs={{0,6},{1,7},{2,0},{3,1},{4,2},{5,3},{6,4},{7,5},{8,14},{9,15},{10,... | collective-permute-start | bytes 98312 | tf_op jit(solution)/shard_map/ppermute | solution.py:34
  71.3 3.0 %collective-permute-start.16 = (bf16[32,112,128]{2,1,0:T(8,128)(2,1)S(1)}, bf16[32,112,128]{2,1,0:T(8,128)(2,1)S(1)}, u32[]{:S(2)}, u32[]{:S(2)}) collective-permute-start(bf16[32,112,128]{2,1,0:T(8,128)(2,1)S(1)} %get-tuple-element.58), channel_id=1, source_target_pairs={{0,1},{1,0},{2,3},{3,2},{4,5},{5,4},{6,7},{7,6},{8,9},{9,8},{10,11... | collective-permute-start | bytes 2752520 | tf_op jit(solution)/shard_map/ppermute | solution.py:464
  75.5 32.7 %all-to-all-start.2 = ((bf16[32,112,128]{2,1,0:T(8,128)(2,1)}), bf16[32,112,128]{2,1,0:T(8,128)(2,1)S(1)}, u32[]{:S(2)}, u32[]{:S(2)}) async-start(bf16[32,112,128]{2,1,0:T(8,128)(2,1)} %add_convert_fusion), calls=%async_computation.2 | async-start | bytes 1835008 | tf_op jit(solution)/shard_map/all_to_all | solution.py:474
  83.6 10.0 %collective-permute-start.14 = (bf16[576,256]{1,0:T(8,128)(2,1)S(1)}, bf16[576,256]{1,0:T(8,128)(2,1)S(1)}, u32[]{:S(2)}, u32[]{:S(2)}) collective-permute-start(bf16[576,256]{1,0:T(8,128)(2,1)S(1)} %get-tuple-element.54), channel_id=1, source_target_pairs={{0,6},{1,7},{2,0},{3,1},{4,2},{5,3},{6,4},{7,5},{8,14},{9,15},{10,... | collective-permute-start | bytes 884744 | tf_op jit(solution)/shard_map/ppermute | solution.py:34
  86.0 11.2 %collective-permute-start.10 = (bf16[512,256]{1,0:T(8,128)(2,1)S(1)}, bf16[512,256]{1,0:T(8,128)(2,1)S(1)}, u32[]{:S(2)}, u32[]{:S(2)}) collective-permute-start(bf16[512,256]{1,0:T(8,128)(2,1)S(1)} %get-tuple-element.49), channel_id=1, source_target_pairs={{0,2},{1,3},{2,4},{3,5},{4,6},{5,7},{6,0},{7,1},{8,10},{9,11},{10,... | collective-permute-start | bytes 786440 | tf_op jit(solution)/shard_map/ppermute | solution.py:34
  87.7 15.1 %collective-permute-start.13 = (bf16[576,256]{1,0:T(8,128)(2,1)S(1)}, bf16[576,256]{1,0:T(8,128)(2,1)S(1)}, u32[]{:S(2)}, u32[]{:S(2)}) collective-permute-start(bf16[576,256]{1,0:T(8,128)(2,1)S(1)} %get-tuple-element.52), channel_id=1, source_target_pairs={{0,2},{1,3},{2,4},{3,5},{4,6},{5,7},{6,0},{7,1},{8,10},{9,11},{10,... | collective-permute-start | bytes 884744 | tf_op jit(solution)/shard_map/ppermute | solution.py:34
  89.1 10.1 %collective-permute-start.12 = (bf16[512,256]{1,0:T(8,128)(2,1)S(1)}, bf16[512,256]{1,0:T(8,128)(2,1)S(1)}, u32[]{:S(2)}, u32[]{:S(2)}) collective-permute-start(bf16[512,256]{1,0:T(8,128)(2,1)S(1)} %get-tuple-element.50), channel_id=1, source_target_pairs={{0,6},{1,7},{2,0},{3,1},{4,2},{5,3},{6,4},{7,5},{8,14},{9,15},{10,... | collective-permute-start | bytes 786440 | tf_op jit(solution)/shard_map/ppermute | solution.py:34
  93.6 13.4 %collective-permute-start.15 = (bf16[576,256]{1,0:T(8,128)(2,1)S(1)}, bf16[576,256]{1,0:T(8,128)(2,1)S(1)}, u32[]{:S(2)}, u32[]{:S(2)}) collective-permute-start(bf16[576,256]{1,0:T(8,128)(2,1)S(1)} %add_convert_fusion.1), channel_id=1, source_target_pairs={{0,6},{1,7},{2,0},{3,1},{4,2},{5,3},{6,4},{7,5},{8,14},{9,15},{10,... | collective-permute-start | bytes 884744 | tf_op jit(solution)/shard_map/ppermute | solution.py:34
  97.4 9.7 %collective-permute-start.11 = (bf16[512,256]{1,0:T(8,128)(2,1)S(1)}, bf16[512,256]{1,0:T(8,128)(2,1)S(1)}, u32[]{:S(2)}, u32[]{:S(2)}) collective-permute-start(bf16[512,256]{1,0:T(8,128)(2,1)S(1)} %add_convert_fusion.2), channel_id=1, source_target_pairs={{0,2},{1,3},{2,4},{3,5},{4,6},{5,7},{6,0},{7,1},{8,10},{9,11},{10,... | collective-permute-start | bytes 786440 | tf_op jit(solution)/shard_map/ppermute | solution.py:34

commit v8 on v7

--- a/solution.py
+++ b/solution.py
@@ -474,7 +474,7 @@
     returned = lax.all_to_all(returning, "ctx", 0, 0, tiled=True)
 
     att, qg = {}, {}
-    for blocks in ((2,), (3, 1, 0)):
+    for blocks in ((2,), (3, 1), (0,)):
         outs = call(
             functools.partial(scale_kernel, blocks),
             [shaped((value_width, rows)), shaped((width, rows))] * len(blocks),

time: 110 us -> 110 us (level)
  waiting for transfers between devices: 32.2 us -> 31.1 us
    ppermute x15, waiting for transfers between devices: 26.3 us -> 25.1 us  [send_x(): return lax.ppermute(value, 'tp', x_shift(k % XN))]
    pallas_call x12 -> x13, Pallas kernels: 21.1 us -> 22.2 us  [call(): pl.pallas_call(kernel, out_shape=[pltpu.HBM(x.shape, x.dtype) if i in far...]
  transfers between devices with their start and end apart: 20 -> 20, of which waited for: 10 -> 9; matrix products, arithmetic and copies ran while one was open for 3% -> 3% of each run, Pallas kernels for 11% -> 12%
where the time goes in v8:
time: 110 us; the launch traced here: 109 us
  starting transfers between devices  48.5 us (44%)
  waiting for transfers between devices  31.1 us (28%)
  Pallas kernels  22.2 us (20%)
  other arithmetic  4.31 us (4%)
  local copies, waits for them, and re-layouts  2.4 us (2%)
    ppermute x15, waiting for transfers between devices, send_x(): return lax.ppermute(value, 'tp', x_shift(k % XN))  25.1 us
    ppermute x15, starting transfers between devices, send_x(): return lax.ppermute(value, 'tp', x_shift(k % XN))  24.4 us
    pallas_call x13, Pallas kernels, call(): pl.pallas_call(kernel, out_shape=[pltpu.HBM(x.shape, x.dtype) if i in far...  22.2 us
    all_to_all x1, starting transfers between devices, on_device(): lax.all_to_all(wanted.astype(jnp.int32)[:, None, :], 'ctx', split_axis=0,...  11.7 us
    all_to_all x1, starting transfers between devices, on_device(): returned = lax.all_to_all(returning, 'ctx', 0, 0, tiled=True)  6.81 us
    all_to_all x1, starting transfers between devices, on_device(): fetched = lax.all_to_all(packed, 'ctx', 0, 0, tiled=True)  5.02 us
    all_to_all x1, waiting for transfers between devices, on_device(): lax.all_to_all(wanted.astype(jnp.int32)[:, None, :], 'ctx', split_axis=0,...  4.8 us
  transfers between devices with their start and end apart: 20, of which 9 were waited for; matrix products, arithmetic and copies ran while one was open for 3% of the time, Pallas kernels for 12%

profile of v8, /device:TPU:8, one launch (start us, length us, event | category | flops | bytes accessed | tf_op | source)
XLA Modules:
  0.0 109.4 jit_solution(8010320240895760780)
XLA Ops:
  0.6 0.8 eq.26
  1.4 0.4 fusion
  1.8 0.7 reshape.154
  2.5 11.7 %all-to-all-start = ((s32[32,1,32]{2,1,0:T(1,128)}), s32[32,1,32]{2,1,0:T(1,128)S(1)}, u32[]{:S(2)}, u32[]{:S(2)}) async-start(s32[32,1,32]{2,1,0:T(1,128)} %reshape.154), calls=%async_computation | async-start | bytes 32768 | tf_op jit(solution)/shard_map/all_to_all | solution.py:359
  14.3 0.2 reduce_window_sum.18
  14.5 0.2 select_reduce_fusion
  14.6 0.2 fusion.2
  15.8 0.9 compare_reduce_fusion
  16.9 0.7 fusion.4
  17.8 4.8 %all-to-all-done.asked_ref = s32[32,1,32]{2,1,0:T(1,128)S(1)} async-done(((s32[32,1,32]{2,1,0:T(1,128)}), s32[32,1,32]{2,1,0:T(1,128)S(1)}, u32[]{:S(2)}, u32[]{:S(2)}) %all-to-all-start) | async-done | bytes 4128 | tf_op jit(solution)/shard_map/all_to_all | solution.py:359
  22.6 2.5 %pack.1 = (bf16[32,112,128]{2,1,0:T(8,128)(2,1)}, bf16[256,576]{1,0:T(8,128)(2,1)S(1)}, bf16[256,512]{1,0:T(8,128)(2,1)S(1)}) custom-call(s32[32,1,32]{2,1,0:T(1,128)S(1)} %all-to-all-done.asked_ref, bf16[32,64,576]{2,1,0:T(8,128)(2,1)} %cache_ref.1, bf16[256,576]{1,0:T(8,128)(2,1)} %bitcast.11, bf16[256,512]{1,0:T(8,128)(2,1)} %bitcast.13, ...), custom_call_target="tpu_custom_call" | custom-call | tf_op jit(solution)/shard_map/pack/pallas_call | solution.py:309
  25.1 5.0 %all-to-all-start.1 = ((bf16[32,112,128]{2,1,0:T(8,128)(2,1)}), bf16[32,112,128]{2,1,0:T(8,128)(2,1)S(1)}, u32[]{:S(2)}, u32[]{:S(2)}) async-start(bf16[32,112,128]{2,1,0:T(8,128)(2,1)} %get-tuple-element.31), calls=%async_computation.1 | async-start | bytes 1835008 | tf_op jit(solution)/shard_map/all_to_all | solution.py:396
  30.2 1.6 %collective-permute-start = (bf16[256,576]{1,0:T(8,128)(2,1)S(1)}, bf16[256,576]{1,0:T(8,128)(2,1)S(1)}, u32[]{:S(2)}, u32[]{:S(2)}) collective-permute-start(bf16[256,576]{1,0:T(8,128)(2,1)S(1)} %get-tuple-element.32.refs_0_.refs_6_), channel_id=1, source_target_pairs={{0,2},{1,3},{2,4},{3,5},{4,6},{5,7},{6,0},{7,1},{8,10},{9,11},{10,... | collective-permute-start | bytes 884744 | tf_op jit(solution)/shard_map/ppermute | solution.py:34
  31.7 1.7 %collective-permute-start.4 = (bf16[256,512]{1,0:T(8,128)(2,1)S(1)}, bf16[256,512]{1,0:T(8,128)(2,1)S(1)}, u32[]{:S(2)}, u32[]{:S(2)}) collective-permute-start(bf16[256,512]{1,0:T(8,128)(2,1)S(1)} %get-tuple-element.33.refs_4_.refs_10_), channel_id=1, source_target_pairs={{0,6},{1,7},{2,0},{3,1},{4,2},{5,3},{6,4},{7,5},{8,14},{9,15},{10,... | collective-permute-start | bytes 786440 | tf_op jit(solution)/shard_map/ppermute | solution.py:34
  33.5 1.5 %collective-permute-start.2 = (bf16[256,576]{1,0:T(8,128)(2,1)S(1)}, bf16[256,576]{1,0:T(8,128)(2,1)S(1)}, u32[]{:S(2)}, u32[]{:S(2)}) collective-permute-start(bf16[256,576]{1,0:T(8,128)(2,1)S(1)} %get-tuple-element.32.refs_0_.refs_6_), channel_id=1, source_target_pairs={{0,6},{1,7},{2,0},{3,1},{4,2},{5,3},{6,4},{7,5},{8,14},{9,15},{10,... | collective-permute-start | bytes 884744 | tf_op jit(solution)/shard_map/ppermute | solution.py:34
  35.0 4.7 %collective-permute-done.refs_0_.refs_1_.refs_7_ = bf16[256,576]{1,0:T(8,128)(2,1)S(1)} collective-permute-done((bf16[256,576]{1,0:T(8,128)(2,1)S(1)}, bf16[256,576]{1,0:T(8,128)(2,1)S(1)}, u32[]{:S(2)}, u32[]{:S(2)}) %collective-permute-start) | collective-permute-done | bytes 294944 | tf_op jit(solution)/shard_map/ppermute | solution.py:34
  39.8 0.3 collective-permute-start.1
  40.0 1.5 %collective-permute-start.3 = (bf16[256,512]{1,0:T(8,128)(2,1)S(1)}, bf16[256,512]{1,0:T(8,128)(2,1)S(1)}, u32[]{:S(2)}, u32[]{:S(2)}) collective-permute-start(bf16[256,512]{1,0:T(8,128)(2,1)S(1)} %get-tuple-element.33.refs_4_.refs_10_), channel_id=1, source_target_pairs={{0,2},{1,3},{2,4},{3,5},{4,6},{5,7},{6,0},{7,1},{8,10},{9,11},{10,... | collective-permute-start | bytes 786440 | tf_op jit(solution)/shard_map/ppermute | solution.py:34
  41.5 2.4 %collective-permute-start.5 = (bf16[256,512]{1,0:T(8,128)(2,1)S(1)}, bf16[256,512]{1,0:T(8,128)(2,1)S(1)}, u32[]{:S(2)}, u32[]{:S(2)}) collective-permute-start(bf16[256,512]{1,0:T(8,128)(2,1)S(1)} %collective-permute-done.4.refs_5_.refs_7_.refs_13_), channel_id=1, source_target_pairs={{0,6},{1,7},{2,0},{3,1},{4,2},{5,3},{6,4},{7,5},{8,14},{9,15},{10,... | collective-permute-start | bytes 786440 | tf_op jit(solution)/shard_map/ppermute | solution.py:34
  43.9 10.0 %collective-permute-done.3.refs_3_.refs_5_.refs_11_ = bf16[256,512]{1,0:T(8,128)(2,1)S(1)} collective-permute-done((bf16[256,512]{1,0:T(8,128)(2,1)S(1)}, bf16[256,512]{1,0:T(8,128)(2,1)S(1)}, u32[]{:S(2)}, u32[]{:S(2)}) %collective-permute-start.3) | collective-permute-done | bytes 262176 | tf_op jit(solution)/shard_map/ppermute | solution.py:34
  54.0 0.9 all-to-all-done.1.parcel_ref
  54.8 0.9 unpack.1.key_ref.refs_0_
  55.7 0.3 collective-permute-start.6
  56.0 1.9 %own_scores.1 = (bf16[4,512,256]{2,1,0:T(8,128)(2,1)S(1)}, f32[4,512,256]{2,1,0:T(8,128)S(1)}, f32[4,8,256]{2,1,0:T(8,128)S(1)}) custom-call(s32[96,128]{1,0:T(8,128)S(1)} %pad.9.refs_0_.plan_ref.refs_14_, bf16[512,576]{1,0:T(8,128)(2,1)S(1)} %unpack.1.key_ref.refs_0_, bf16[256,576]{1,0:T(8,128)(2,1)S(1)} %get-tuple-element.32.refs_0_.refs_6_, ...), custom_call_target="tpu_custom_call" | custom-call | tf_op jit(solution)/shard_map/own_scores/pallas_call | solution.py:309
  57.9 0.2 collective-permute-done.6
  58.1 1.9 %other_scores.1 = (bf16[4,512,256]{2,1,0:T(8,128)(2,1)S(1)}, f32[4,512,256]{2,1,0:T(8,128)S(1)}, f32[4,8,256]{2,1,0:T(8,128)S(1)}) custom-call(s32[96,128]{1,0:T(8,128)S(1)} %pad.9.refs_0_.plan_ref.refs_14_, bf16[512,576]{1,0:T(8,128)(2,1)S(1)} %bitcast.9, bf16[256,576]{1,0:T(8,128)(2,1)S(1)} %get-tuple-element.32.refs_0_.refs_6_, ...), custom_call_target="tpu_custom_call" | custom-call | tf_op jit(solution)/shard_map/other_scores/pallas_call | solution.py:309
  60.0 1.6 %collective-permute-start.7 = (f32[4,8,256]{2,1,0:T(8,128)S(1)}, f32[4,8,256]{2,1,0:T(8,128)S(1)}, u32[]{:S(2)}, u32[]{:S(2)}) collective-permute-start(f32[4,8,256]{2,1,0:T(8,128)S(1)} %get-tuple-element.35.refs_6_.refs_2_.refs_0_), channel_id=1, source_target_pairs={{0,2},{1,3},{2,4},{3,5},{4,6},{5,7},{6,0},{7,1},{8,10},{9,11},{10,... | collective-permute-start | bytes 98312 | tf_op jit(solution)/shard_map/ppermute | solution.py:34
  61.6 2.7 %collective-permute-start.8 = (f32[4,8,256]{2,1,0:T(8,128)S(1)}, f32[4,8,256]{2,1,0:T(8,128)S(1)}, u32[]{:S(2)}, u32[]{:S(2)}) collective-permute-start(f32[4,8,256]{2,1,0:T(8,128)S(1)} %get-tuple-element.35.refs_6_.refs_2_.refs_0_), channel_id=1, source_target_pairs={{0,4},{1,5},{2,6},{3,7},{4,0},{5,1},{6,2},{7,3},{8,12},{9,13},{10,... | collective-permute-start | bytes 98312 | tf_op jit(solution)/shard_map/ppermute | solution.py:34
  64.3 1.4 %collective-permute-start.9 = (f32[4,8,256]{2,1,0:T(8,128)S(1)}, f32[4,8,256]{2,1,0:T(8,128)S(1)}, u32[]{:S(2)}, u32[]{:S(2)}) collective-permute-start(f32[4,8,256]{2,1,0:T(8,128)S(1)} %get-tuple-element.35.refs_6_.refs_2_.refs_0_), channel_id=1, source_target_pairs={{0,6},{1,7},{2,0},{3,1},{4,2},{5,3},{6,4},{7,5},{8,14},{9,15},{10,... | collective-permute-start | bytes 98312 | tf_op jit(solution)/shard_map/ppermute | solution.py:34
  65.8 2.6 %local.1 = (bf16[4,576,256]{2,1,0:T(8,128)(2,1)S(1)}, bf16[4,576,256]{2,1,0:T(8,128)(2,1)S(1)}) custom-call(bf16[512,576]{1,0:T(8,128)(2,1)S(1)} %unpack.1.key_ref.refs_0_, bf16[512,576]{1,0:T(8,128)(2,1)S(1)} %bitcast.10, bf16[4,512,256]{2,1,0:T(8,128)(2,1)S(1)} %get-tuple-element.38.refs_2_.refs_0_, ...), custom_call_target="tpu_custom_call" | custom-call | tf_op jit(solution)/shard_map/local/pallas_call | solution.py:309
  68.5 2.8 %other_grads.1 = (bf16[32,112,128]{2,1,0:T(8,128)(2,1)S(1)}, bf16[4,576,256]{2,1,0:T(8,128)(2,1)}, bf16[768,512]{1,0:T(8,128)(2,1)S(1)}, bf16[1024,576]{1,0:T(8,128)(2,1)S(1)}, bf16[1024,512]{1,0:T(8,128)(2,1)S(1)}) custom-call(bf16[4,512,256]{2,1,0:T(8,128)(2,1)S(1)} %get-tuple-element.36.refs_3_.refs_0_, ...), custom_call_target="tpu_custom_call" | custom-call | tf_op jit(solution)/shard_map/other_grads/pallas_call | solution.py:309
  71.3 0.3 collective-permute-start.16
  71.6 2.6 %own_grads.1 = (bf16[32,112,128]{2,1,0:T(8,128)(2,1)S(1)}, bf16[4,576,256]{2,1,0:T(8,128)(2,1)}) custom-call(bf16[4,512,256]{2,1,0:T(8,128)(2,1)S(1)} %get-tuple-element.38.refs_2_.refs_0_, f32[4,512,256]{2,1,0:T(8,128)S(1)} %get-tuple-element.39.refs_4_.refs_1_, f32[4,8,256]{2,1,0:T(8,128)S(1)} %get-tuple-element.35.refs_6_.refs_2_.refs_0_, ...), custom_call_target="tpu_custom_call" | custom-call | tf_op jit(solution)/shard_map/own_grads/pallas_call | solution.py:309
  74.3 1.2 %add_convert_fusion = bf16[32,112,128]{2,1,0:T(8,128)(2,1)} fusion(bf16[32,112,128]{2,1,0:T(8,128)(2,1)S(1)} %collective-permute-done.16, bf16[32,112,128]{2,1,0:T(8,128)(2,1)S(1)} %get-tuple-element.57), kind=kLoop, calls=%fused_computation.2 | loop fusion | flops 1835008 | bytes 2752512 | tf_op jit(solution)/shard_map/convert_element_type | solution.py:473
  75.5 6.8 %all-to-all-start.2 = ((bf16[32,112,128]{2,1,0:T(8,128)(2,1)}), bf16[32,112,128]{2,1,0:T(8,128)(2,1)S(1)}, u32[]{:S(2)}, u32[]{:S(2)}) async-start(bf16[32,112,128]{2,1,0:T(8,128)(2,1)} %add_convert_fusion), calls=%async_computation.2 | async-start | bytes 1835008 | tf_op jit(solution)/shard_map/all_to_all | solution.py:474
  82.3 1.3 %scale.5 = (bf16[512,256]{1,0:T(8,128)(2,1)S(1)}, bf16[576,256]{1,0:T(8,128)(2,1)S(1)}) custom-call(f32[4,8,256]{2,1,0:T(8,128)S(1)} %get-tuple-element.35.refs_6_.refs_2_.refs_0_, f32[4,8,256]{2,1,0:T(8,128)S(1)} %collective-permute-done.7.refs_3_.refs_1_, f32[4,8,256]{2,1,0:T(8,128)S(1)} %collective-permute-done.8.refs_4_.refs_2_, ...), custom_call_target="tpu_custom_call" | custom-call | tf_op jit(solution)/shard_map/scale/pallas_call | solution.py:309
  83.6 2.5 %collective-permute-start.14 = (bf16[576,256]{1,0:T(8,128)(2,1)S(1)}, bf16[576,256]{1,0:T(8,128)(2,1)S(1)}, u32[]{:S(2)}, u32[]{:S(2)}) collective-permute-start(bf16[576,256]{1,0:T(8,128)(2,1)S(1)} %get-tuple-element.54), channel_id=1, source_target_pairs={{0,6},{1,7},{2,0},{3,1},{4,2},{5,3},{6,4},{7,5},{8,14},{9,15},{10,... | collective-permute-start | bytes 884744 | tf_op jit(solution)/shard_map/ppermute | solution.py:34
  86.0 1.5 %scale.4 = (bf16[512,256]{1,0:T(8,128)(2,1)S(1)}, bf16[576,256]{1,0:T(8,128)(2,1)S(1)}, bf16[512,256]{1,0:T(8,128)(2,1)S(1)}, bf16[576,256]{1,0:T(8,128)(2,1)S(1)}) custom-call(f32[4,8,256]{2,1,0:T(8,128)S(1)} %get-tuple-element.35.refs_6_.refs_2_.refs_0_, f32[4,8,256]{2,1,0:T(8,128)S(1)} %collective-permute-done.7.refs_3_.refs_1_, ...), custom_call_target="tpu_custom_call" | custom-call | tf_op jit(solution)/shard_map/scale/pallas_call | solution.py:309
  87.5 1.4 %collective-permute-start.13 = (bf16[576,256]{1,0:T(8,128)(2,1)S(1)}, bf16[576,256]{1,0:T(8,128)(2,1)S(1)}, u32[]{:S(2)}, u32[]{:S(2)}) collective-permute-start(bf16[576,256]{1,0:T(8,128)(2,1)S(1)} %get-tuple-element.52), channel_id=1, source_target_pairs={{0,2},{1,3},{2,4},{3,5},{4,6},{5,7},{6,0},{7,1},{8,10},{9,11},{10,... | collective-permute-start | bytes 884744 | tf_op jit(solution)/shard_map/ppermute | solution.py:34
  88.9 2.0 %collective-permute-start.12 = (bf16[512,256]{1,0:T(8,128)(2,1)S(1)}, bf16[512,256]{1,0:T(8,128)(2,1)S(1)}, u32[]{:S(2)}, u32[]{:S(2)}) collective-permute-start(bf16[512,256]{1,0:T(8,128)(2,1)S(1)} %get-tuple-element.50), channel_id=1, source_target_pairs={{0,6},{1,7},{2,0},{3,1},{4,2},{5,3},{6,4},{7,5},{8,14},{9,15},{10,... | collective-permute-start | bytes 786440 | tf_op jit(solution)/shard_map/ppermute | solution.py:34
  90.9 2.6 %collective-permute-done.14 = bf16[576,256]{1,0:T(8,128)(2,1)S(1)} collective-permute-done((bf16[576,256]{1,0:T(8,128)(2,1)S(1)}, bf16[576,256]{1,0:T(8,128)(2,1)S(1)}, u32[]{:S(2)}, u32[]{:S(2)}) %collective-permute-start.14) | collective-permute-done | bytes 294944 | tf_op jit(solution)/shard_map/ppermute | solution.py:34
  93.6 3.7 %collective-permute-start.15 = (bf16[576,256]{1,0:T(8,128)(2,1)S(1)}, bf16[576,256]{1,0:T(8,128)(2,1)S(1)}, u32[]{:S(2)}, u32[]{:S(2)}) collective-permute-start(bf16[576,256]{1,0:T(8,128)(2,1)S(1)} %add_convert_fusion.1), channel_id=1, source_target_pairs={{0,6},{1,7},{2,0},{3,1},{4,2},{5,3},{6,4},{7,5},{8,14},{9,15},{10,... | collective-permute-start | bytes 884744 | tf_op jit(solution)/shard_map/ppermute | solution.py:34
  97.4 0.6 asked.1.hot_ref
  98.0 1.3 %scale.3 = (bf16[512,256]{1,0:T(8,128)(2,1)S(1)}, bf16[576,256]{1,0:T(8,128)(2,1)S(1)}) custom-call(f32[4,8,256]{2,1,0:T(8,128)S(1)} %get-tuple-element.35.refs_6_.refs_2_.refs_0_, f32[4,8,256]{2,1,0:T(8,128)S(1)} %collective-permute-done.7.refs_3_.refs_1_, f32[4,8,256]{2,1,0:T(8,128)S(1)} %collective-permute-done.8.refs_4_.refs_2_, ...), custom_call_target="tpu_custom_call" | custom-call | tf_op jit(solution)/shard_map/scale/pallas_call | solution.py:309
  99.3 3.5 %collective-permute-done.13.refs_4_ = bf16[576,256]{1,0:T(8,128)(2,1)S(1)} collective-permute-done((bf16[576,256]{1,0:T(8,128)(2,1)S(1)}, bf16[576,256]{1,0:T(8,128)(2,1)S(1)}, u32[]{:S(2)}, u32[]{:S(2)}) %collective-permute-start.13) | collective-permute-done | bytes 294944 | tf_op jit(solution)/shard_map/ppermute | solution.py:34
  102.8 4.3 %collective-permute-done.11.refs_1_ = bf16[512,256]{1,0:T(8,128)(2,1)S(1)} collective-permute-done((bf16[512,256]{1,0:T(8,128)(2,1)S(1)}, bf16[512,256]{1,0:T(8,128)(2,1)S(1)}, u32[]{:S(2)}, u32[]{:S(2)}) %collective-permute-start.11) | collective-permute-done | bytes 262176 | tf_op jit(solution)/shard_map/ppermute | solution.py:34
  107.0 1.0 combine.1
  108.2 1.2 %owner_sum.1 = bf16[256,576]{1,0:T(8,128)(2,1)} custom-call(bf16[256,768]{1,0:T(8,128)(2,1)S(1)} %asked.1.hot_ref, bf16[32,112,128]{2,1,0:T(8,128)(2,1)S(1)} %all-to-all-done.2.parcel_ref), custom_call_target="tpu_custom_call" | custom-call | tf_op jit(solution)/shard_map/owner_sum/pallas_call | solution.py:309
  (38 shorter events, 1.9 us)
Async XLA Ops:
  2.5 20.2 %all-to-all-start = ((s32[32,1,32]{2,1,0:T(1,128)}), s32[32,1,32]{2,1,0:T(1,128)S(1)}, u32[]{:S(2)}, u32[]{:S(2)}) async-start(s32[32,1,32]{2,1,0:T(1,128)} %reshape.154), calls=%async_computation | async-start | bytes 32768 | tf_op jit(solution)/shard_map/all_to_all | solution.py:359
  25.1 29.7 %all-to-all-start.1 = ((bf16[32,112,128]{2,1,0:T(8,128)(2,1)}), bf16[32,112,128]{2,1,0:T(8,128)(2,1)S(1)}, u32[]{:S(2)}, u32[]{:S(2)}) async-start(bf16[32,112,128]{2,1,0:T(8,128)(2,1)} %get-tuple-element.31), calls=%async_computation.1 | async-start | bytes 1835008 | tf_op jit(solution)/shard_map/all_to_all | solution.py:396
  30.2 9.6 %collective-permute-start = (bf16[256,576]{1,0:T(8,128)(2,1)S(1)}, bf16[256,576]{1,0:T(8,128)(2,1)S(1)}, u32[]{:S(2)}, u32[]{:S(2)}) collective-permute-start(bf16[256,576]{1,0:T(8,128)(2,1)S(1)} %get-tuple-element.32.refs_0_.refs_6_), channel_id=1, source_target_pairs={{0,2},{1,3},{2,4},{3,5},{4,6},{5,7},{6,0},{7,1},{8,10},{9,11},{10,... | collective-permute-start | bytes 884744 | tf_op jit(solution)/shard_map/ppermute | solution.py:34
  31.7 9.8 %collective-permute-start.4 = (bf16[256,512]{1,0:T(8,128)(2,1)S(1)}, bf16[256,512]{1,0:T(8,128)(2,1)S(1)}, u32[]{:S(2)}, u32[]{:S(2)}) collective-permute-start(bf16[256,512]{1,0:T(8,128)(2,1)S(1)} %get-tuple-element.33.refs_4_.refs_10_), channel_id=1, source_target_pairs={{0,6},{1,7},{2,0},{3,1},{4,2},{5,3},{6,4},{7,5},{8,14},{9,15},{10,... | collective-permute-start | bytes 786440 | tf_op jit(solution)/shard_map/ppermute | solution.py:34
  33.5 20.5 %collective-permute-start.2 = (bf16[256,576]{1,0:T(8,128)(2,1)S(1)}, bf16[256,576]{1,0:T(8,128)(2,1)S(1)}, u32[]{:S(2)}, u32[]{:S(2)}) collective-permute-start(bf16[256,576]{1,0:T(8,128)(2,1)S(1)} %get-tuple-element.32.refs_0_.refs_6_), channel_id=1, source_target_pairs={{0,6},{1,7},{2,0},{3,1},{4,2},{5,3},{6,4},{7,5},{8,14},{9,15},{10,... | collective-permute-start | bytes 884744 | tf_op jit(solution)/shard_map/ppermute | solution.py:34
  39.8 14.2 %collective-permute-start.1 = (bf16[256,576]{1,0:T(8,128)(2,1)S(1)}, bf16[256,576]{1,0:T(8,128)(2,1)S(1)}, u32[]{:S(2)}, u32[]{:S(2)}) collective-permute-start(bf16[256,576]{1,0:T(8,128)(2,1)S(1)} %collective-permute-done.refs_0_.refs_1_.refs_7_), channel_id=1, source_target_pairs={{0,2},{1,3},{2,4},{3,5},{4,6},{5,7},{6,0},{7,1},{8,10},{9,11},{10,... | collective-permute-start | bytes 884744 | tf_op jit(solution)/shard_map/ppermute | solution.py:34
  40.0 13.9 %collective-permute-start.3 = (bf16[256,512]{1,0:T(8,128)(2,1)S(1)}, bf16[256,512]{1,0:T(8,128)(2,1)S(1)}, u32[]{:S(2)}, u32[]{:S(2)}) collective-permute-start(bf16[256,512]{1,0:T(8,128)(2,1)S(1)} %get-tuple-element.33.refs_4_.refs_10_), channel_id=1, source_target_pairs={{0,2},{1,3},{2,4},{3,5},{4,6},{5,7},{6,0},{7,1},{8,10},{9,11},{10,... | collective-permute-start | bytes 786440 | tf_op jit(solution)/shard_map/ppermute | solution.py:34
  41.5 12.4 %collective-permute-start.5 = (bf16[256,512]{1,0:T(8,128)(2,1)S(1)}, bf16[256,512]{1,0:T(8,128)(2,1)S(1)}, u32[]{:S(2)}, u32[]{:S(2)}) collective-permute-start(bf16[256,512]{1,0:T(8,128)(2,1)S(1)} %collective-permute-done.4.refs_5_.refs_7_.refs_13_), channel_id=1, source_target_pairs={{0,6},{1,7},{2,0},{3,1},{4,2},{5,3},{6,4},{7,5},{8,14},{9,15},{10,... | collective-permute-start | bytes 786440 | tf_op jit(solution)/shard_map/ppermute | solution.py:34
  55.7 2.4 %collective-permute-start.6 = (bf16[64,8,576]{2,1,0:T(8,128)(2,1)S(1)}, bf16[64,8,576]{2,1,0:T(8,128)(2,1)S(1)}, u32[]{:S(2)}, u32[]{:S(2)}) collective-permute-start(bf16[64,8,576]{2,1,0:T(8,128)(2,1)S(1)} %bitcast.8), channel_id=1, source_target_pairs={{0,1},{1,0},{2,3},{3,2},{4,5},{5,4},{6,7},{7,6},{8,9},{9,8},{10,11... | collective-permute-start | bytes 1769480 | tf_op jit(solution)/shard_map/ppermute | solution.py:410
  60.0 8.4 %collective-permute-start.7 = (f32[4,8,256]{2,1,0:T(8,128)S(1)}, f32[4,8,256]{2,1,0:T(8,128)S(1)}, u32[]{:S(2)}, u32[]{:S(2)}) collective-permute-start(f32[4,8,256]{2,1,0:T(8,128)S(1)} %get-tuple-element.35.refs_6_.refs_2_.refs_0_), channel_id=1, source_target_pairs={{0,2},{1,3},{2,4},{3,5},{4,6},{5,7},{6,0},{7,1},{8,10},{9,11},{10,... | collective-permute-start | bytes 98312 | tf_op jit(solution)/shard_map/ppermute | solution.py:34
  61.6 6.8 %collective-permute-start.8 = (f32[4,8,256]{2,1,0:T(8,128)S(1)}, f32[4,8,256]{2,1,0:T(8,128)S(1)}, u32[]{:S(2)}, u32[]{:S(2)}) collective-permute-start(f32[4,8,256]{2,1,0:T(8,128)S(1)} %get-tuple-element.35.refs_6_.refs_2_.refs_0_), channel_id=1, source_target_pairs={{0,4},{1,5},{2,6},{3,7},{4,0},{5,1},{6,2},{7,3},{8,12},{9,13},{10,... | collective-permute-start | bytes 98312 | tf_op jit(solution)/shard_map/ppermute | solution.py:34
  64.3 4.1 %collective-permute-start.9 = (f32[4,8,256]{2,1,0:T(8,128)S(1)}, f32[4,8,256]{2,1,0:T(8,128)S(1)}, u32[]{:S(2)}, u32[]{:S(2)}) collective-permute-start(f32[4,8,256]{2,1,0:T(8,128)S(1)} %get-tuple-element.35.refs_6_.refs_2_.refs_0_), channel_id=1, source_target_pairs={{0,6},{1,7},{2,0},{3,1},{4,2},{5,3},{6,4},{7,5},{8,14},{9,15},{10,... | collective-permute-start | bytes 98312 | tf_op jit(solution)/shard_map/ppermute | solution.py:34
  71.3 3.0 %collective-permute-start.16 = (bf16[32,112,128]{2,1,0:T(8,128)(2,1)S(1)}, bf16[32,112,128]{2,1,0:T(8,128)(2,1)S(1)}, u32[]{:S(2)}, u32[]{:S(2)}) collective-permute-start(bf16[32,112,128]{2,1,0:T(8,128)(2,1)S(1)} %get-tuple-element.58), channel_id=1, source_target_pairs={{0,1},{1,0},{2,3},{3,2},{4,5},{5,4},{6,7},{7,6},{8,9},{9,8},{10,11... | collective-permute-start | bytes 2752520 | tf_op jit(solution)/shard_map/ppermute | solution.py:464
  75.5 32.7 %all-to-all-start.2 = ((bf16[32,112,128]{2,1,0:T(8,128)(2,1)}), bf16[32,112,128]{2,1,0:T(8,128)(2,1)S(1)}, u32[]{:S(2)}, u32[]{:S(2)}) async-start(bf16[32,112,128]{2,1,0:T(8,128)(2,1)} %add_convert_fusion), calls=%async_computation.2 | async-start | bytes 1835008 | tf_op jit(solution)/shard_map/all_to_all | solution.py:474
  83.6 10.0 %collective-permute-start.14 = (bf16[576,256]{1,0:T(8,128)(2,1)S(1)}, bf16[576,256]{1,0:T(8,128)(2,1)S(1)}, u32[]{:S(2)}, u32[]{:S(2)}) collective-permute-start(bf16[576,256]{1,0:T(8,128)(2,1)S(1)} %get-tuple-element.54), channel_id=1, source_target_pairs={{0,6},{1,7},{2,0},{3,1},{4,2},{5,3},{6,4},{7,5},{8,14},{9,15},{10,... | collective-permute-start | bytes 884744 | tf_op jit(solution)/shard_map/ppermute | solution.py:34
  86.0 11.2 %collective-permute-start.10 = (bf16[512,256]{1,0:T(8,128)(2,1)S(1)}, bf16[512,256]{1,0:T(8,128)(2,1)S(1)}, u32[]{:S(2)}, u32[]{:S(2)}) collective-permute-start(bf16[512,256]{1,0:T(8,128)(2,1)S(1)} %get-tuple-element.49), channel_id=1, source_target_pairs={{0,2},{1,3},{2,4},{3,5},{4,6},{5,7},{6,0},{7,1},{8,10},{9,11},{10,... | collective-permute-start | bytes 786440 | tf_op jit(solution)/shard_map/ppermute | solution.py:34
  87.5 15.3 %collective-permute-start.13 = (bf16[576,256]{1,0:T(8,128)(2,1)S(1)}, bf16[576,256]{1,0:T(8,128)(2,1)S(1)}, u32[]{:S(2)}, u32[]{:S(2)}) collective-permute-start(bf16[576,256]{1,0:T(8,128)(2,1)S(1)} %get-tuple-element.52), channel_id=1, source_target_pairs={{0,2},{1,3},{2,4},{3,5},{4,6},{5,7},{6,0},{7,1},{8,10},{9,11},{10,... | collective-permute-start | bytes 884744 | tf_op jit(solution)/shard_map/ppermute | solution.py:34
  88.9 10.4 %collective-permute-start.12 = (bf16[512,256]{1,0:T(8,128)(2,1)S(1)}, bf16[512,256]{1,0:T(8,128)(2,1)S(1)}, u32[]{:S(2)}, u32[]{:S(2)}) collective-permute-start(bf16[512,256]{1,0:T(8,128)(2,1)S(1)} %get-tuple-element.50), channel_id=1, source_target_pairs={{0,6},{1,7},{2,0},{3,1},{4,2},{5,3},{6,4},{7,5},{8,14},{9,15},{10,... | collective-permute-start | bytes 786440 | tf_op jit(solution)/shard_map/ppermute | solution.py:34
  93.6 13.4 %collective-permute-start.15 = (bf16[576,256]{1,0:T(8,128)(2,1)S(1)}, bf16[576,256]{1,0:T(8,128)(2,1)S(1)}, u32[]{:S(2)}, u32[]{:S(2)}) collective-permute-start(bf16[576,256]{1,0:T(8,128)(2,1)S(1)} %add_convert_fusion.1), channel_id=1, source_target_pairs={{0,6},{1,7},{2,0},{3,1},{4,2},{5,3},{6,4},{7,5},{8,14},{9,15},{10,... | collective-permute-start | bytes 884744 | tf_op jit(solution)/shard_map/ppermute | solution.py:34
  97.3 9.7 %collective-permute-start.11 = (bf16[512,256]{1,0:T(8,128)(2,1)S(1)}, bf16[512,256]{1,0:T(8,128)(2,1)S(1)}, u32[]{:S(2)}, u32[]{:S(2)}) collective-permute-start(bf16[512,256]{1,0:T(8,128)(2,1)S(1)} %add_convert_fusion.2), channel_id=1, source_target_pairs={{0,2},{1,3},{2,4},{3,5},{4,6},{5,7},{6,0},{7,1},{8,10},{9,11},{10,... | collective-permute-start | bytes 786440 | tf_op jit(solution)/shard_map/ppermute | solution.py:34
